TPU v7x, 128 devices: a whole 4x4x4 slice. The times are simulated.
128 devices in a mesh: lat: 16 (over x_hi, z, core), lon: 8 (over y, x_lo).
Axes of the slice: x: 4 (x_hi: 2, x_lo: 2; x = x_hi * 2 + x_lo), y: 4, z: 4, core: 2. Of those that a mesh axis runs over, the one named last changes fastest.
Arguments:
- pedersen: float32 [16, 2048, 4096], P(None, 'lat', 'lon'), may hold values from 0.2 to 2
- hall_conductivity: float32 [16, 2048, 4096], P(None, 'lat', 'lon'), may hold values from 0.1 to 1.5
- east_wind: float32 [16, 2048, 4096], P(None, 'lat', 'lon'), may hold values from -6 to 6
- north_wind: float32 [16, 2048, 4096], P(None, 'lat', 'lon'), may hold values from -6 to 6
- ion_density: float32 [3, 2048, 4096], P(None, 'lat', 'lon'), may hold values from 0.5 to 2
Outputs:
- potential: float32 [2048, 4096], P('lat', 'lon')
- ion_update: float32 [3, 2048, 4096], P(None, 'lat', 'lon')
All inputs are finite; a program needn't handle non-finite values. Where the computation divides by a largest or mean magnitude, that divisor is 1e-20 or more.
Results may differ from a plain program's by a relative error of at most 0.00002.
Values sent between devices are 32-bit elements; how exact they have to be, the bound alone decides.
No kernel may reach another device: no remote copies, remote signals or barrier semaphores. Data moves between devices by JAX's collectives and lax.ppermute only.
A program may use at most 192 MiB of HBM per device.

v0:
```python
import jax
import jax.numpy as jnp
from jax import lax
from jax.sharding import PartitionSpec as P

LEV = 16
SWEEPS = 16


DAMPING = 0.0001
LOW_BOUND = 0.05
HIGH_BOUND = 2.0
COURANT = 0.8
MOBILITY = (1.0, 0.6, 0.3)
NEIGHBOURS = (
    (-1, 0, 1.0),
    (1, 0, 1.0),
    (0, -1, 1.0),
    (0, 1, 1.0),
    (-1, -1, 0.5),
    (-1, 1, 0.5),
    (1, -1, 0.5),
    (1, 1, 0.5),
)


def padded(array, sides, width):
    for axis, dim in sides:
        peers, length = (lax.axis_size(axis), array.shape[dim])
        up = [(i, (i + 1) % peers) for i in range(peers)]
        down = [(j, i) for i, j in up]
        last = lax.slice_in_dim(array, length - width, length, axis=dim)
        initial = lax.slice_in_dim(array, 0, width, axis=dim)
        before = lax.ppermute(last, axis, up)
        after = lax.ppermute(initial, axis, down)
        array = jnp.concatenate([before, array, after], axis=dim)
    return array


def thickness():
    levels = jnp.arange(LEV, dtype=jnp.float32)
    return (0.5 + levels / LEV) / LEV


def chebyshev_factors():
    theta = 0.5 * (HIGH_BOUND + LOW_BOUND)
    delta = 0.5 * (HIGH_BOUND - LOW_BOUND)
    sigma_one = theta / delta
    rho_prev = 1.0 / sigma_one
    first_list = []
    second_list = []
    for sweep in range(SWEEPS):
        rho_next = 1.0 / (2.0 * sigma_one - rho_prev)
        first_list.append(rho_next * rho_prev)
        second_list.append(2.0 * rho_next / delta)
        rho_prev = rho_next
    return (theta, first_list, second_list)


def window(array, shift_lat, shift_lon):
    height = array.shape[0] - 2
    breadth = array.shape[1] - 2
    return array[1 + shift_lat : 1 + shift_lat + height, 1 + shift_lon : 1 + shift_lon + breadth]


def stencil(sigma_ext):
    center = window(sigma_ext, 0, 0)
    weights = []
    diagonal = jnp.zeros_like(center) + DAMPING
    for shift_lat, shift_lon, factor in NEIGHBOURS:
        weight = factor * 0.5 * (center + window(sigma_ext, shift_lat, shift_lon))
        weights.append(weight)
    for weight in weights:
        diagonal = diagonal + weight
    return (weights, diagonal)


def apply_operator(field_ext, weights, diagonal):
    result = diagonal * window(field_ext, 0, 0)
    for index_pair, (shift_lat, shift_lon, factor) in enumerate(NEIGHBOURS):
        result = result - weights[index_pair] * window(field_ext, shift_lat, shift_lon)
    return result


def divergence(east_ext, north_ext):
    return 0.5 * (window(east_ext, 0, 1) - window(east_ext, 0, -1)) + 0.5 * (
        window(north_ext, 1, 0) - window(north_ext, -1, 0)
    )


def advect(density_ext, cross_east, cross_north):
    density = window(density_ext, 0, 0)
    result = density - jnp.maximum(cross_east, 0.0) * (density - window(density_ext, 0, -1))
    result = result - jnp.minimum(cross_east, 0.0) * (window(density_ext, 0, 1) - density)
    result = result - jnp.maximum(cross_north, 0.0) * (density - window(density_ext, -1, 0))
    result = result - jnp.minimum(cross_north, 0.0) * (window(density_ext, 1, 0) - density)
    return result


def shards(pedersen, hall_conductivity, east_wind, north_wind, ion_density):
    lat_rows = pedersen.shape[1]
    lon_cells = pedersen.shape[2]
    lat_total = lat_rows * lax.axis_size("lat")
    band_index = lax.axis_index("lat")

    def inside(width):
        global_rows = (
            band_index * lat_rows - width + jnp.arange(lat_rows + 2 * width, dtype=jnp.int32)
        )
        return jnp.where((global_rows >= 0) & (global_rows < lat_total), 1.0, 0.0).astype(
            jnp.float32
        )[:, None]

    layer = thickness()[:, None, None]
    sigma = jnp.sum(layer * pedersen, 0)
    current_east = jnp.sum(layer * (pedersen * east_wind + hall_conductivity * north_wind), 0)
    current_north = jnp.sum(layer * (pedersen * north_wind - hall_conductivity * east_wind), 0)
    stacked = jnp.stack([sigma, current_east, current_north])
    flat_rows = stacked[:, ::-1, :].reshape(3, 1, lat_rows * lon_cells)
    spread = lax.all_to_all(flat_rows, "lat", split_axis=2, concat_axis=1, tiled=True)
    spread = spread[:, ::-1, :]
    returned = lax.all_to_all(spread, "lat", split_axis=1, concat_axis=2, tiled=True)
    mirrored = returned.reshape(3, lat_rows, lon_cells)
    combined = stacked + mirrored
    depth = 1
    reach = depth + 1
    drivers = padded(combined, (("lat", 1), ("lon", 2)), reach)
    drivers = drivers * inside(reach)[None]
    weights, diagonal = stencil(drivers[0])
    source = divergence(drivers[1], drivers[2])
    mask_inner = inside(depth)
    theta, first_list, second_list = chebyshev_factors()
    first_table = jnp.array(first_list, jnp.float32)
    second_table = jnp.array(second_list, jnp.float32)

    def crop(array):
        return array[depth : depth + lat_rows, depth : depth + lon_cells]

    solution = jnp.zeros((lat_rows, lon_cells), jnp.float32)
    update = crop(source / diagonal / theta)

    def group(group_index, carry):
        state = jnp.stack([carry[0], carry[1]])
        state_ext = padded(state, (("lat", 1), ("lon", 2)), depth)
        solution_ext = state_ext[0] * mask_inner
        update_ext = state_ext[1] * mask_inner
        position = group_index * depth + 0
        solution_ext = solution_ext + update_ext
        image = apply_operator(jnp.pad(solution_ext, 1), weights, diagonal)
        scaled = mask_inner * ((source - image) / diagonal)
        update_ext = first_table[position] * update_ext + second_table[position] * scaled
        return (crop(solution_ext), crop(update_ext))

    solution, update = lax.fori_loop(0, SWEEPS // depth, group, (solution, update))
    fields = jnp.concatenate([solution[None], ion_density], 0)
    fields_ext = padded(fields, (("lat", 1), ("lon", 2)), 1)
    fields_ext = fields_ext * inside(1)[None]
    potential_ext = fields_ext[0]
    drift_east = -0.5 * (window(potential_ext, 1, 0) - window(potential_ext, -1, 0))
    drift_north = 0.5 * (window(potential_ext, 0, 1) - window(potential_ext, 0, -1))
    fastest = lax.pmax(jnp.max(jnp.abs(drift_east) + jnp.abs(drift_north)), ("lat", "lon"))
    time_step = COURANT / (fastest + 1e-06)
    results = []
    for species in range(3):
        cross_east = MOBILITY[species] * time_step * drift_east
        cross_north = MOBILITY[species] * time_step * drift_north
        results.append(advect(fields_ext[species + 1], cross_east, cross_north))
    return (solution, jnp.stack(results))


def solution(mesh):
    in_specs = (
        P(None, "lat", "lon"),
        P(None, "lat", "lon"),
        P(None, "lat", "lon"),
        P(None, "lat", "lon"),
        P(None, "lat", "lon"),
    )
    out_specs = (P("lat", "lon"), P(None, "lat", "lon"))
    return jax.shard_map(shards, mesh=mesh, in_specs=in_specs, out_specs=out_specs, check_vma=False)
```

profile of v0, /device:TPU:1, one launch (start us, length us, event | category | flops | bytes accessed | tf_op | source)
XLA Modules:
  0.0 910.4 jit_solution(12292882548486129008)
XLA Ops:
  0.6 7.1 multiply_reduce_fusion.1
  8.2 16.4 %copy.16 = f32[3,128,512]{0,2,1:T(8,128)} copy(f32[3,128,512]{2,1,0:T(8,128)S(1)} %rev.6) | data formatting | bytes 1572864 | tf_op jit(solution)/shard_map/reshape | solution.py:119
  25.2 291.0 %reduce = f32[65536,3]{1,0:T(8,128)} reduce(f32[65536,1,3]{2,1,0:T(1,128)} %bitcast.57, f32[]{:T(128)} %broadcast.166), dimensions={1}, to_apply=%bitcast.43.reduce_sub_computation | reduce | bytes 1572868
  316.2 26.4 %reshape.60 = f32[16,1,12288]{2,1,0:T(1,128)S(1)} reshape(f32[65536,3]{1,0:T(8,128)} %reduce) | data formatting | bytes 1572864
  342.6 23.7 %all_to_all.21 = f32[16,1,12288]{2,1,0:T(1,128)S(1)} all-to-all(f32[16,1,12288]{2,1,0:T(1,128)S(1)} %reshape.60), channel_id=1, replica_groups=mesh['lat'=16,'lon'=8] {'lat'}, dimensions={0} | all-to-all | bytes 1572864 | tf_op jit(solution)/shard_map/all_to_all | solution.py:120
  368.8 62.8 %reshape.61 = f32[65536,1,3]{2,1,0:T(1,128)} reshape(f32[16,12288]{1,0:T(8,128)S(1)} %reduce.1) | data formatting | bytes 1572864
  431.6 18.8 %copy.17 = f32[3,16,4096]{2,1,0:T(8,128)S(1)} copy(f32[3,16,4096]{0,2,1:T(8,128)} %bitcast.58) | data formatting | bytes 1572864 | tf_op jit(solution)/shard_map/all_to_all | solution.py:120
  451.6 20.4 %all_to_all.22 = f32[3,16,4096]{2,0,1:T(4,128)S(1)} all-to-all(f32[3,16,4096]{2,0,1:T(4,128)S(1)} %copy.14), channel_id=1, replica_groups=mesh['lat'=16,'lon'=8] {'lat'}, dimensions={1} | all-to-all | bytes 1572864 | tf_op jit(solution)/shard_map/all_to_all | solution.py:122
  476.6 3.4 collective-permute-start.7
  487.3 326.1 %while.19 = (s32[]{:T(128)}, f32[128,512]{1,0:T(8,128)S(1)}, f32[128,512]{1,0:T(8,128)S(1)}, f32[130,514]{1,0:T(8,128)S(1)}, f32[130,514]{1,0:T(8,128)S(1)}, /*i...) while((s32[]{:T(128)}, f32[128,512]{1,0:T(8,128)S(1)}, ...), condition=%wide.region_4.5_spmd.clone.clone, body=%wide.region_3.4_spmd.sunk.clone.clone.sunk | while | flops 2400792 | bytes 9622957 | solution.py:154
  487.3 5.8 collective-permute-start
  493.9 4.2 collective-permute-done.1
  503.3 3.8 collective-permute-done.3
  512.0 7.5 collective-permute-start
  532.6 6.9 collective-permute-start
  552.6 6.8 collective-permute-start
  572.5 6.8 collective-permute-start
  592.4 6.9 collective-permute-start
  612.7 7.1 collective-permute-start
  632.9 6.9 collective-permute-start
  652.9 6.8 collective-permute-start
  672.8 6.8 collective-permute-start
  692.8 6.9 collective-permute-start
  713.0 7.1 collective-permute-start
  733.3 6.8 collective-permute-start
  753.2 6.8 collective-permute-start
  773.2 6.8 collective-permute-start
  793.1 7.0 collective-permute-start
  817.7 3.8 collective-permute-start.9
  823.6 3.6 collective-permute-start.11
  827.2 3.9 collective-permute-done.10
  834.5 73.1 %pmax.7 = f32[]{:T(128)} all-reduce(f32[]{:T(128)} %get-tuple-element.486), channel_id=1, replica_groups=mesh['lat'=16,'lon'=8] {'lat','lon'}, use_global_device_ids=true, to_apply=%region_6.7 | all-reduce | flops 1 | bytes 8 | tf_op jit(solution)/shard_map/pmax | solution.py:161
  (365 shorter events, 235.4 us)
Async XLA Ops:
  476.2 6.8 collective-permute-start.6
  476.6 7.7 collective-permute-start.7
  487.3 6.6 collective-permute-start
  512.0 8.3 collective-permute-start
  521.4 6.3 collective-permute-start.3
  532.6 7.7 collective-permute-start
  541.5 6.3 collective-permute-start.3
  552.6 7.6 collective-permute-start
  561.4 6.3 collective-permute-start.3
  572.5 7.6 collective-permute-start
  581.3 6.3 collective-permute-start.3
  592.4 7.8 collective-permute-start
  612.7 7.9 collective-permute-start
  621.8 6.3 collective-permute-start.3
  632.9 7.7 collective-permute-start
  641.8 6.3 collective-permute-start.3
  652.9 7.6 collective-permute-start
  661.7 6.3 collective-permute-start.3
  672.8 7.6 collective-permute-start
  681.6 6.3 collective-permute-start.3
  692.8 7.8 collective-permute-start
  713.0 7.9 collective-permute-start
  722.1 6.3 collective-permute-start.3
  733.3 7.6 collective-permute-start
  742.0 6.3 collective-permute-start.3
  753.2 7.6 collective-permute-start
  762.0 6.3 collective-permute-start.3
  773.2 7.6 collective-permute-start
  793.1 7.8 collective-permute-start
  814.3 7.8 collective-permute-start.8
  823.5 7.6 collective-permute-start.10
  823.6 8.2 collective-permute-start.11
  (60 other events, 269.2 us)
where the time goes:
time: 919 us; the launch traced here: 910 us
  other arithmetic  397 us (43%)
  local copies, waits for them, and re-layouts  151 us (16%)
  starting transfers between devices  150 us (16%)
  blocking collectives  117 us (13%)
  waiting for transfers between devices  93.4 us (10%)
    unnamed x1, other arithmetic  291 us
    ppermute x36, starting transfers between devices, padded(): after = lax.ppermute(initial, axis, down)  124 us
    unnamed x11, local copies, waits for them, and re-layouts  90.2 us
    pmax x1, blocking collectives, shards(): lax.pmax(jnp.max(jnp.abs(drift_east) + jnp.abs(drift_north)), ('lat', 'lo...  73.1 us
    ppermute x36, waiting for transfers between devices, padded(): before = lax.ppermute(last, axis, up)  51.2 us
    ppermute x36, waiting for transfers between devices, padded(): after = lax.ppermute(initial, axis, down)  42.2 us
    add x16, other arithmetic, group(): first_table[position] * update_ext + second_table[position] * scaled  26.7 us
    sub x16, other arithmetic, apply_operator(): result - weights[index_pair] * window(field_ext, shift_lat, shift_lon)  26.3 us
  transfers between devices with their start and end apart: 72, of which 72 were waited for; matrix products, arithmetic and copies ran while one was open for 2% of the time, Pallas kernels for 0%

commit v1 on v0

v1 whole, which is shorter than its diff:
```python
import functools

import jax
import jax.numpy as jnp
from jax import lax
from jax.experimental import pallas as pl
from jax.experimental.pallas import tpu as pltpu
from jax.sharding import PartitionSpec as P

LEV = 16
SWEEPS = 16
DAMPING = 0.0001
LOW_BOUND = 0.05
HIGH_BOUND = 2.0
COURANT = 0.8
MOBILITY = (1.0, 0.6, 0.3)

LANES = 128
ROWS = 128
COLS = 512
TILES = COLS // LANES
EDGE = 24
SIDE = 32
MID = ROWS - 2 * EDGE
EXT = ROWS + 2 * EDGE
BAND = 2 * EDGE + 8
STRIP = ROWS + 8
CHUNK = 16
VMEM_BYTES = 48 * 1024 * 1024


def chebyshev_factors():
    theta = 0.5 * (HIGH_BOUND + LOW_BOUND)
    delta = 0.5 * (HIGH_BOUND - LOW_BOUND)
    sigma_one = theta / delta
    rho_prev = 1.0 / sigma_one
    first_list = []
    second_list = []
    for sweep in range(SWEEPS):
        rho_next = 1.0 / (2.0 * sigma_one - rho_prev)
        first_list.append(rho_next * rho_prev)
        second_list.append(2.0 * rho_next / delta)
        rho_prev = rho_next
    return (theta, first_list, second_list)


def lane_index(rows):
    return lax.broadcasted_iota(jnp.int32, (rows, LANES), 1)


def row_index(rows, cols=LANES):
    return lax.broadcasted_iota(jnp.int32, (rows, cols), 0)


def reversed_rows(tile):
    row = row_index(8, tile.shape[1])
    tile = pltpu.roll(tile, 4, 0)
    tile = jnp.where((row & 2) == 0, pltpu.roll(tile, 6, 0), pltpu.roll(tile, 2, 0))
    return jnp.where((row & 1) == 0, pltpu.roll(tile, 7, 0), pltpu.roll(tile, 1, 0))


def shifted(tiles, to_right):
    count = len(tiles)
    lane = lane_index(tiles[0].shape[0])
    if to_right:
        turned = [pltpu.roll(tile, 1, 1) for tile in tiles]
        return [jnp.where(lane == 0, turned[t - 1], turned[t]) for t in range(count)]
    turned = [pltpu.roll(tile, LANES - 1, 1) for tile in tiles]
    return [jnp.where(lane == LANES - 1, turned[(t + 1) % count], turned[t]) for t in range(count)]


def local_source(east, north, source, start, rows):
    tiles = [east[start : start + rows, t * LANES : (t + 1) * LANES] for t in range(TILES)]
    lane = lane_index(rows)
    row = row_index(rows)
    left = [pltpu.roll(tile, 1, 1) for tile in tiles]
    right = [pltpu.roll(tile, LANES - 1, 1) for tile in tiles]
    zero = jnp.zeros((rows, LANES), jnp.float32)
    for t in range(TILES):
        span = slice(t * LANES, (t + 1) * LANES)
        before = jnp.where(lane == 0, left[t - 1] if t else zero, left[t])
        after = jnp.where(lane == LANES - 1, right[t + 1] if t < TILES - 1 else zero, right[t])
        here = north[start : start + rows, span]
        up = pltpu.roll(here, 1, 0)
        down = pltpu.roll(here, rows - 1, 0)
        above = north[start - 8 : start, span][7:8] if start else zero[:1]
        below = north[start + rows : start + rows + 8, span][:1] if start + rows < ROWS else zero[:1]
        up = jnp.where(row == 0, above, up)
        down = jnp.where(row == rows - 1, below, down)
        source[start : start + rows, span] = 0.5 * (after - before) + 0.5 * (down - up)


def write_pieces(sigma, east, north, source, strips, bands, middle):
    for start in range(0, ROWS, 8):
        local_source(east, north, source, start, 8)
    lane = lane_index(ROWS)
    last = COLS - LANES
    strips[0, :ROWS] = jnp.where(
        lane < SIDE,
        sigma[:, :LANES],
        jnp.where(
            lane < 2 * SIDE,
            pltpu.roll(source[:, :LANES], SIDE, 1),
            jnp.where(lane == LANES - 1, pltpu.roll(east[:, :LANES], LANES - 1, 1), 0.0),
        ),
    )
    strips[1, :ROWS] = jnp.where(
        lane >= LANES - SIDE,
        sigma[:, last:],
        jnp.where(
            lane >= LANES - 2 * SIDE,
            pltpu.roll(source[:, last:], LANES - SIDE, 1),
            jnp.where(lane == 0, pltpu.roll(east[:, last:], 1, 1), 0.0),
        ),
    )
    row = row_index(8)
    for side, at in ((0, 0), (1, last)):
        span = slice(at, at + LANES)
        strips[side, ROWS:] = jnp.where(
            row == 0, north[0:8, span][:1], jnp.where(row == 1, north[ROWS - 8 :, span][7:8], 0.0)
        )
    wide = row_index(8, COLS)
    for side, at in ((0, 0), (1, ROWS - EDGE)):
        bands[side, :EDGE] = sigma[at : at + EDGE]
        bands[side, EDGE : 2 * EDGE] = source[at : at + EDGE]
        line = north[0:8][:1] if side == 0 else north[ROWS - 8 :][7:8]
        bands[side, 2 * EDGE :] = jnp.where(wide == 0, line, 0.0)
    middle[0] = sigma[EDGE : ROWS - EDGE]
    middle[1] = source[EDGE : ROWS - EDGE]


def column_kernel(
    pedersen, hall, east_wind, north_wind,
    own_strips, own_bands, own_middle, far_strips, far_bands, far_middle,
    sigma, east, north, sigma_far, east_far, north_far, source,
):
    step = pl.program_id(0)
    steps = ROWS // CHUNK
    for half in range(CHUNK // 8):
        span = slice(half * 8, half * 8 + 8)
        totals = [jnp.zeros((8, COLS), jnp.float32) for _ in range(3)]
        for level in range(LEV):
            layer = (0.5 + level / LEV) / LEV
            along = layer * pedersen[level, span, :]
            across = layer * hall[level, span, :]
            wind_e = east_wind[level, span, :]
            wind_n = north_wind[level, span, :]
            totals[0] = totals[0] + along
            totals[1] = totals[1] + (along * wind_e + across * wind_n)
            totals[2] = totals[2] + (along * wind_n - across * wind_e)
        near = pl.ds(pl.multiple_of(step * CHUNK + half * 8, 8), 8)
        away = pl.ds(pl.multiple_of((steps - 1 - step) * CHUNK + CHUNK - 8 - half * 8, 8), 8)
        for total, here, there in zip(totals, (sigma, east, north), (sigma_far, east_far, north_far)):
            here[near, :] = total
            there[away, :] = reversed_rows(total)

    @pl.when(step == steps - 1)
    def _():
        write_pieces(sigma_far, east_far, north_far, source, far_strips, far_bands, far_middle)
        write_pieces(sigma, east, north, source, own_strips, own_bands, own_middle)


def column_sums(pedersen, hall, east_wind, north_wind):
    block = pl.BlockSpec((LEV, CHUNK, COLS), lambda i: (0, i, 0))
    shapes = [(2, STRIP, LANES), (2, BAND, COLS), (2, MID, COLS)] * 2
    field = pltpu.VMEM((ROWS, COLS), jnp.float32)
    return pl.pallas_call(
        column_kernel,
        grid=(ROWS // CHUNK,),
        in_specs=[block] * 4,
        out_specs=[pl.BlockSpec(shape, lambda i: (0, 0, 0)) for shape in shapes],
        out_shape=[jax.ShapeDtypeStruct(shape, jnp.float32) for shape in shapes],
        scratch_shapes=[field] * 7,
        compiler_params=pltpu.CompilerParams(vmem_limit_bytes=VMEM_BYTES),
        name="column_sums",
    )(pedersen, hall, east_wind, north_wind)


def strip_kernel(own, far, ions_first, ions_last, to_left, to_right):
    lane = lane_index(ROWS)
    left = own[0, :ROWS] + far[0, :ROWS]
    right = own[1, :ROWS] + far[1, :ROWS]
    for s in range(3):
        left = jnp.where(lane == 2 * SIDE + s, pltpu.roll(ions_first[s], 2 * SIDE + s, 1), left)
        right = jnp.where(lane == SIDE + s, pltpu.roll(ions_last[s], SIDE + s + 1, 1), right)
    to_left[:ROWS] = left
    to_right[:ROWS] = right
    to_left[ROWS:] = own[0, ROWS:] + far[0, ROWS:]
    to_right[ROWS:] = own[1, ROWS:] + far[1, ROWS:]


def strips_to_send(own, far, ions):
    whole = pl.BlockSpec((2, STRIP, LANES), lambda i: (0, 0, 0))
    shape = jax.ShapeDtypeStruct((STRIP, LANES), jnp.float32)
    return pl.pallas_call(
        strip_kernel,
        grid=(1,),
        in_specs=[
            whole,
            whole,
            pl.BlockSpec((3, ROWS, LANES), lambda i: (0, 0, 0)),
            pl.BlockSpec((3, ROWS, LANES), lambda i: (0, 0, TILES - 1)),
        ],
        out_specs=[pl.BlockSpec((STRIP, LANES), lambda i: (0, 0))] * 2,
        out_shape=[shape, shape],
        name="lon_strips",
    )(own, far, ions, ions)


def halo_sigma(from_right, from_left):
    lane = lane_index(from_right.shape[0])
    return jnp.where(lane < SIDE, from_right, jnp.where(lane >= LANES - SIDE, from_left, 0.0))


def halo_source(from_right, from_left, own_left, own_right):
    lane = lane_index(from_right.shape[0])
    tile = jnp.where(
        lane < SIDE,
        pltpu.roll(from_right, LANES - SIDE, 1),
        jnp.where(lane >= LANES - SIDE, pltpu.roll(from_left, SIDE, 1), 0.0),
    )
    tile = tile - jnp.where(lane == 0, 0.5 * own_right, 0.0)
    return tile + jnp.where(lane == LANES - 1, 0.5 * own_left, 0.0)


def first_fix(from_left):
    return jnp.where(lane_index(from_left.shape[0]) == 0, -0.5 * from_left, 0.0)


def last_fix(from_right):
    return jnp.where(lane_index(from_right.shape[0]) == LANES - 1, 0.5 * from_right, 0.0)


def band_kernel(own, far, own_left, own_right, from_right, from_left, ions_top, ions_bottom, top, bottom):
    for side, out, start in ((0, top, 0), (1, bottom, ROWS - EDGE)):
        rows = slice(start, start + EDGE)
        out[:, :COLS] = own[side] + far[side]
        out[:EDGE, COLS:] = halo_sigma(from_right[rows], from_left[rows])
        out[EDGE : 2 * EDGE, COLS:] = halo_source(
            from_right[rows], from_left[rows], own_left[rows], own_right[rows]
        )
        part = slice(EDGE, 2 * EDGE)
        out[part, :LANES] += first_fix(from_left[rows])
        out[part, COLS - LANES : COLS] += last_fix(from_right[rows])
        extra = halo_sigma(from_right[ROWS:], from_left[ROWS:])
        out[2 * EDGE :, COLS:] = jnp.where(row_index(8) == 0, extra[side : side + 1], 0.0)
        ions = ions_top if side == 0 else ions_bottom
        wide = row_index(8, COLS)
        lines = out[2 * EDGE :, :COLS]
        for s in range(3):
            line = ions[s, 0:1] if side == 0 else ions[s, 7:8]
            lines = jnp.where(wide == s + 1, line, lines)
        out[2 * EDGE :, :COLS] = lines


def bands_to_send(own, far, own_left, own_right, from_right, from_left, ions):
    whole = pl.BlockSpec((2, BAND, COLS), lambda i: (0, 0, 0))
    strip = pl.BlockSpec((STRIP, LANES), lambda i: (0, 0))
    shape = jax.ShapeDtypeStruct((BAND, COLS + LANES), jnp.float32)
    return pl.pallas_call(
        band_kernel,
        grid=(1,),
        in_specs=[
            whole,
            whole,
            strip,
            strip,
            strip,
            strip,
            pl.BlockSpec((3, 8, COLS), lambda i: (0, 0, 0)),
            pl.BlockSpec((3, 8, COLS), lambda i: (0, ROWS // 8 - 1, 0)),
        ],
        out_specs=[pl.BlockSpec((BAND, COLS + LANES), lambda i: (0, 0))] * 2,
        out_shape=[shape, shape],
        name="lat_bands",
    )(own, far, own_left, own_right, from_right, from_left, ions, ions)


def solve_kernel(
    factors, band, top, bottom, above, below, own_middle, far_middle,
    own_left, own_right, from_right, from_left,
    potential, drift_east, drift_north, fastest,
    sigma, sigma_next, sigma_prev, half_inverse, scaled_source, update, field, carried,
):
    theta = 0.5 * (HIGH_BOUND + LOW_BOUND)
    count = TILES + 1
    spans = [slice(t * LANES, (t + 1) * LANES) for t in range(count)]
    middle = slice(EDGE, ROWS - EDGE)

    for t in range(count):
        for piece, at in ((above, 0), (top, EDGE), (bottom, EDGE + ROWS - EDGE), (below, EDGE + ROWS)):
            sigma[t, at : at + EDGE] = piece[:EDGE, spans[t]]
            scaled_source[t, at : at + EDGE] = piece[EDGE : 2 * EDGE, spans[t]]
        inner = slice(2 * EDGE, 2 * EDGE + MID)
        if t < TILES:
            sigma[t, inner] = own_middle[0, :, spans[t]] + far_middle[0, :, spans[t]]
            source = own_middle[1, :, spans[t]] + far_middle[1, :, spans[t]]
            if t == 0:
                source = source + first_fix(from_left[middle])
            if t == TILES - 1:
                source = source + last_fix(from_right[middle])
        else:
            sigma[t, inner] = halo_sigma(from_right[middle], from_left[middle])
            source = halo_source(
                from_right[middle], from_left[middle], own_left[middle], own_right[middle]
            )
        scaled_source[t, inner] = source
        line = slice(2 * EDGE, 2 * EDGE + 1)
        row = row_index(8)
        tile = scaled_source[t, EDGE - 8 : EDGE]
        scaled_source[t, EDGE - 8 : EDGE] = tile + jnp.where(row == 7, 0.5 * top[line, spans[t]], 0.0)
        tile = scaled_source[t, EDGE : EDGE + 8]
        scaled_source[t, EDGE : EDGE + 8] = tile - jnp.where(row == 0, 0.5 * above[line, spans[t]], 0.0)
        low = EDGE + ROWS
        tile = scaled_source[t, low - 8 : low]
        scaled_source[t, low - 8 : low] = tile + jnp.where(row == 7, 0.5 * below[line, spans[t]], 0.0)
        tile = scaled_source[t, low : low + 8]
        scaled_source[t, low : low + 8] = tile - jnp.where(row == 0, 0.5 * bottom[line, spans[t]], 0.0)

    first_band = band[0] == 0
    last_band = band[0] == band[1] - 1
    blank = jnp.zeros((8, LANES), jnp.float32)
    for t in range(count):
        for slot in range(2):
            for at in (0, EXT - 8):
                field[slot, t, at : at + 8] = blank
                carried[slot, t, at : at + 8] = blank

    for start in range(8, EXT - 8, 8):
        here = [sigma[t, start : start + 8] for t in range(count)]
        sides = [sigma[t, start - 1 : start + 7] + sigma[t, start + 1 : start + 9] for t in range(count)]
        tall = [here[t] + 0.5 * sides[t] for t in range(count)]
        left = shifted(tall, True)
        right = shifted(tall, False)
        following = shifted(here, False)
        preceding = shifted(here, True)
        outside = None
        if start < EDGE:
            outside = first_band
        if start >= EDGE + ROWS:
            outside = last_band
        for t in range(count):
            diagonal = 0.5 * (6.0 * here[t] + (sides[t] + (left[t] + right[t]))) + DAMPING
            inverse = 1.0 / diagonal
            if outside is not None:
                inverse = jnp.where(outside, 0.0, inverse)
            source = scaled_source[t, start : start + 8] * inverse
            initial = source * (1.0 / theta)
            sigma_next[t, start : start + 8] = following[t]
            sigma_prev[t, start : start + 8] = preceding[t]
            half_inverse[t, start : start + 8] = 0.5 * inverse
            scaled_source[t, start : start + 8] = source
            update[t, start : start + 8] = initial
            field[1, t, start : start + 8] = initial
            carried[1, t, start : start + 8] = here[t] * initial

    def sweep(k, low, high):
        now = lax.rem(k, 2)
        later = 1 - now
        keep = factors[0, k - 1]
        gain = factors[1, k - 1]
        for start in range(low, high, 8):
            rows = slice(start, start + 8)
            upper = slice(start - 1, start + 7)
            lower = slice(start + 1, start + 9)
            centre, eastward, westward = ([], [], [])
            for t in range(count):
                value = field[now, t, rows]
                flux = carried[now, t, rows]
                value_sides = field[now, t, upper] + field[now, t, lower]
                flux_sides = carried[now, t, upper] + carried[now, t, lower]
                tall = value + 0.5 * value_sides
                flux_tall = flux + 0.5 * flux_sides
                centre.append(sigma[t, rows] * value_sides + flux_sides)
                eastward.append(sigma_next[t, rows] * tall + flux_tall)
                westward.append(sigma_prev[t, rows] * tall + flux_tall)
            from_west = shifted(eastward, True)
            from_east = shifted(westward, False)
            for t in range(count):
                total = centre[t] + (from_west[t] + from_east[t])
                value = field[now, t, rows]
                residual = (scaled_source[t, rows] - value) + half_inverse[t, rows] * total
                step = keep * update[t, rows] + gain * residual
                update[t, rows] = step
                value = value + step
                field[later, t, rows] = value
                carried[later, t, rows] = sigma[t, rows] * value

    def early(k, _):
        sweep(k, 8, EXT - 8)
        return 0

    def late(k, _):
        sweep(k, 16, EXT - 16)
        return 0

    lax.fori_loop(1, 8, early, 0)
    lax.fori_loop(8, SWEEPS, late, 0)

    last = SWEEPS % 2
    top_speed = jnp.zeros((8, LANES), jnp.float32)
    for start in range(EDGE, EDGE + ROWS, 8):
        rows = slice(start, start + 8)
        out = slice(start - EDGE, start - EDGE + 8)
        tiles = [field[last, t, rows] for t in range(count)]
        west = shifted(tiles, True)
        east = shifted(tiles, False)
        for t in range(TILES):
            potential[out, spans[t]] = tiles[t]
            lift = -0.5 * (field[last, t, start + 1 : start + 9] - field[last, t, start - 1 : start + 7])
            shove = 0.5 * (east[t] - west[t])
            drift_east[out, spans[t]] = lift
            drift_north[out, spans[t]] = shove
            top_speed = jnp.maximum(top_speed, jnp.abs(lift) + jnp.abs(shove))
    peak = jnp.max(top_speed, axis=1, keepdims=True)
    peak = jnp.max(peak, axis=0, keepdims=True)
    fastest[...] = jnp.broadcast_to(peak[None], fastest.shape)


def solve(peers, factors, band, *fields):
    shapes = [(ROWS, COLS)] * 3 + [(peers, 1, LANES)]
    plane = (TILES + 1, EXT, LANES)
    memory = pltpu.VMEM(plane, jnp.float32)
    pair = pltpu.VMEM((2,) + plane, jnp.float32)
    return pl.pallas_call(
        solve_kernel,
        in_specs=[pl.BlockSpec(memory_space=pltpu.SMEM)] * 2
        + [pl.BlockSpec(memory_space=pltpu.VMEM)] * len(fields),
        out_specs=[pl.BlockSpec(memory_space=pltpu.VMEM)] * 4,
        out_shape=[jax.ShapeDtypeStruct(shape, jnp.float32) for shape in shapes],
        scratch_shapes=[memory] * 6 + [pair] * 2,
        compiler_params=pltpu.CompilerParams(vmem_limit_bytes=VMEM_BYTES),
        name="potential_solve",
    )(factors, band, *fields)


def advect_kernel(fastest, drift_east, drift_north, ions, above, below, from_right, from_left, out):
    peak = jnp.max(fastest[...], axis=0)
    peak = jnp.max(peak, axis=1, keepdims=True)
    time_step = COURANT / (peak + 1e-06)
    lane = lane_index(ROWS)
    wide = row_index(ROWS, LANES)
    for s in range(3):
        pace = MOBILITY[s] * time_step
        tiles = [ions[s, :, t * LANES : (t + 1) * LANES] for t in range(TILES)]
        left = [pltpu.roll(tile, 1, 1) for tile in tiles]
        right = [pltpu.roll(tile, LANES - 1, 1) for tile in tiles]
        edge_right = pltpu.roll(from_right[:ROWS], SIDE * 2 - 1 - s, 1)
        edge_left = pltpu.roll(from_left[:ROWS], LANES - SIDE - s, 1)
        for t in range(TILES):
            span = slice(t * LANES, (t + 1) * LANES)
            density = tiles[t]
            west = jnp.where(lane == 0, left[t - 1] if t else edge_left, left[t])
            east = jnp.where(lane == LANES - 1, right[t + 1] if t < TILES - 1 else edge_right, right[t])
            line = slice(2 * EDGE + 1 + s, 2 * EDGE + 2 + s)
            south = jnp.where(wide == 0, above[line, span], pltpu.roll(density, 1, 0))
            north = jnp.where(wide == ROWS - 1, below[line, span], pltpu.roll(density, ROWS - 1, 0))
            cross_east = pace * drift_east[:, span]
            cross_north = pace * drift_north[:, span]
            result = density - jnp.maximum(cross_east, 0.0) * (density - west)
            result = result - jnp.minimum(cross_east, 0.0) * (east - density)
            result = result - jnp.maximum(cross_north, 0.0) * (density - south)
            result = result - jnp.minimum(cross_north, 0.0) * (north - density)
            out[s, :, span] = result


def advect(*fields):
    return pl.pallas_call(
        advect_kernel,
        in_specs=[pl.BlockSpec(memory_space=pltpu.VMEM)] * len(fields),
        out_specs=pl.BlockSpec(memory_space=pltpu.VMEM),
        out_shape=jax.ShapeDtypeStruct((3, ROWS, COLS), jnp.float32),
        compiler_params=pltpu.CompilerParams(vmem_limit_bytes=VMEM_BYTES),
        name="ion_advection",
    )(*fields)


def shards(pedersen, hall_conductivity, east_wind, north_wind, ion_density):
    lats = lax.axis_size("lat")
    lons = lax.axis_size("lon")
    mirror = [(i, lats - 1 - i) for i in range(lats)]
    eastward = [(i, (i + 1) % lons) for i in range(lons)]
    westward = [(j, i) for i, j in eastward]
    rising = [(i, i + 1) for i in range(lats - 1)]
    falling = [(j, i) for i, j in rising]

    own_strips, own_bands, own_middle, strips, bands, middle = column_sums(
        pedersen, hall_conductivity, east_wind, north_wind
    )
    far_strips = lax.ppermute(strips, "lat", mirror)
    far_bands = lax.ppermute(bands, "lat", mirror)
    far_middle = lax.ppermute(middle, "lat", mirror)
    to_left, to_right = strips_to_send(own_strips, far_strips, ion_density)
    from_right = lax.ppermute(to_left, "lon", westward)
    from_left = lax.ppermute(to_right, "lon", eastward)
    top, bottom = bands_to_send(
        own_bands, far_bands, to_left, to_right, from_right, from_left, ion_density
    )
    above = lax.ppermute(bottom, "lat", rising)
    below = lax.ppermute(top, "lat", falling)

    theta, first_list, second_list = chebyshev_factors()
    factors = jnp.array([first_list, second_list], jnp.float32)
    band = jnp.stack([lax.axis_index("lat").astype(jnp.int32), jnp.int32(lats)])
    potential, drift_east, drift_north, peaks = solve(
        lats * lons, factors, band, top, bottom, above, below, own_middle, far_middle,
        to_left, to_right, from_right, from_left,
    )
    peaks = lax.all_to_all(peaks, ("lat", "lon"), 0, 0, tiled=True)
    ion_update = advect(
        peaks, drift_east, drift_north, ion_density, above, below, from_right, from_left
    )
    return (potential, ion_update)


def solution(mesh):
    spec = P(None, "lat", "lon")
    return jax.shard_map(
        shards,
        mesh=mesh,
        in_specs=(spec,) * 5,
        out_specs=(P("lat", "lon"), spec),
        check_vma=False,
    )
```

time: 919 us -> 109 us (0.12)
  other arithmetic: 397 us -> 0.08 us
  local copies, waits for them, and re-layouts: 151 us -> 10.2 us
  starting transfers between devices: 150 us -> 21.3 us
  blocking collectives: 117 us -> 19.3 us
  waiting for transfers between devices: 93.4 us -> 13.4 us
  Pallas kernels: 0 us -> 43.3 us
    unnamed x1 -> x0, other arithmetic: 291 us -> none
    ppermute x72 -> x7, starting transfers between devices: 150 us -> 21.3 us  [the longest x1 7.61 us: shards(): far_bands = lax.ppermute(bands, 'lat', mirror)]
    unnamed x11 -> x30, local copies, waits for them, and re-layouts: 90.2 us -> 10.2 us
    ppermute x72 -> x7, waiting for transfers between devices: 93.4 us -> 13.4 us  [the longest x1 4.49 us: shards(): far_strips = lax.ppermute(strips, 'lat', mirror)]
    pmax x1 -> x0, blocking collectives: 73.1 us -> none  [shards(): lax.pmax(jnp.max(jnp.abs(drift_east) + jnp.abs(drift_north)), ('lat', 'lo...]
    pallas_call x0 -> x5, Pallas kernels: none -> 43.3 us  [the longest x1 29.2 us: solve(): pl.pallas_call(solve_kernel, in_specs=[pl.BlockSpec(memory_space=pltpu.SM...]
    add x18 -> x0, other arithmetic: 28.5 us -> none  [the longest x16 26.7 us: group(): first_table[position] * update_ext + second_table[position] * scaled]
    sub x16 -> x0, other arithmetic: 26.3 us -> none  [apply_operator(): result - weights[index_pair] * window(field_ext, shift_lat, shift_lon)]
  transfers between devices with their start and end apart: 72 -> 7, of which waited for: 72 -> 5; matrix products, arithmetic and copies ran while one was open for 2% -> 0% of each run, Pallas kernels for 0% -> 4%
where the time goes in v1:
time: 109 us; the launch traced here: 108 us
  Pallas kernels  43.3 us (40%)
  starting transfers between devices  21.3 us (20%)
  blocking collectives  19.3 us (18%)
  waiting for transfers between devices  13.4 us (12%)
  local copies, waits for them, and re-layouts  10.2 us (9%)
    pallas_call x1, Pallas kernels, solve(): pl.pallas_call(solve_kernel, in_specs=[pl.BlockSpec(memory_space=pltpu.SM...  29.2 us
    all_to_all x1, blocking collectives, shards(): peaks = lax.all_to_all(peaks, ('lat', 'lon'), 0, 0, tiled=True)  19.3 us
    unnamed x30, local copies, waits for them, and re-layouts  10.2 us
    pallas_call x1, Pallas kernels, column_sums(): pl.pallas_call(column_kernel, grid=(ROWS // CHUNK,), in_specs=[block] * 4...  8.41 us
    ppermute x1, starting transfers between devices, shards(): far_bands = lax.ppermute(bands, 'lat', mirror)  7.61 us
    ppermute x1, starting transfers between devices, shards(): far_middle = lax.ppermute(middle, 'lat', mirror)  5.33 us
    ppermute x1, waiting for transfers between devices, shards(): far_strips = lax.ppermute(strips, 'lat', mirror)  4.49 us
    ppermute x1, waiting for transfers between devices, shards(): from_left = lax.ppermute(to_right, 'lon', eastward)  3.94 us
  transfers between devices with their start and end apart: 7, of which 5 were waited for; matrix products, arithmetic and copies ran while one was open for 0% of the time, Pallas kernels for 4%

profile of v1, /device:TPU:1, one launch (start us, length us, event | category | flops | bytes accessed | tf_op | source)
XLA Modules:
  0.0 108.4 jit_solution(12396125437752818406)
XLA Ops:
  0.6 2.2 %copy-done.1 = f32[16,128,512]{2,1,0:T(8,128)S(1)} copy-done((f32[16,128,512]{2,1,0:T(8,128)S(1)}, f32[16,128,512]{2,1,0:T(8,128)}, u32[]{:S(2)}) %copy-start.1) | copy-done | bytes 4194328
  2.8 8.4 %column_sums.1 = (f32[2,136,128]{2,1,0:T(8,128)S(1)}, f32[2,56,512]{2,1,0:T(8,128)S(1)}, f32[2,80,512]{2,1,0:T(8,128)S(1)}, f32[2,136,128]{2,1,0:T(8,128)S(1)}, ...) custom-call(f32[16,128,512]{2,1,0:T(8,128)S(1)} %copy-done.1, f32[16,128,512]{2,1,0:T(8,128)} %hall.1, ...), custom_call_target="tpu_custom_call" | custom-call | tf_op jit(solution)/shard_map/column_sums/pallas_call | solution.py:167
  11.2 0.0 copy-start.8
  11.3 0.7 copy-done.8
  11.9 0.7 copy-done.11
  12.6 7.6 %collective-permute-start = (f32[2,56,512]{2,1,0:T(8,128)S(1)}, f32[2,56,512]{2,1,0:T(8,128)S(1)}, u32[]{:S(2)}, u32[]{:S(2)}) collective-permute-start(f32[2,56,512]{2,1,0:T(8,128)S(1)} %get-tuple-element.17), channel_id=1, source_target_pairs={{0,120},{8,112},{16,104},{24,96},{32,88},{40,80},{48,72},{56,64},{... | collective-permute-start | bytes 688136 | tf_op jit(solution)/shard_map/ppermute | solution.py:491
  20.2 0.0 collective-permute-start.1
  20.2 5.3 %collective-permute-start.6 = (f32[2,80,512]{2,1,0:T(8,128)S(1)}, f32[2,80,512]{2,1,0:T(8,128)S(1)}, u32[]{:S(2)}, u32[]{:S(2)}) collective-permute-start(f32[2,80,512]{2,1,0:T(8,128)S(1)} %get-tuple-element.25), channel_id=1, source_target_pairs={{0,120},{8,112},{16,104},{24,96},{32,88},{40,80},{48,72},{56,64},{... | collective-permute-start | bytes 983048 | tf_op jit(solution)/shard_map/ppermute | solution.py:492
  25.6 4.5 %collective-permute-done.1.far = f32[2,136,128]{2,1,0:T(8,128)S(1)} collective-permute-done((f32[2,136,128]{2,1,0:T(8,128)S(1)}, f32[2,136,128]{2,1,0:T(8,128)S(1)}, u32[]{:S(2)}, u32[]{:S(2)}) %collective-permute-start.1) | collective-permute-done | bytes 139296 | tf_op jit(solution)/shard_map/ppermute | solution.py:490
  30.1 0.7 copy-done.14
  30.7 2.0 %lon_strips.1 = (f32[136,128]{1,0:T(8,128)}, f32[136,128]{1,0:T(8,128)}) custom-call(f32[2,136,128]{2,1,0:T(8,128)} %copy-done.11, f32[2,136,128]{2,1,0:T(8,128)} %copy-done.14, f32[3,128,512]{2,1,0:T(8,128)} %ions.1, f32[3,128,512]{2,1,0:T(8,128)} %ions.1), custom_call_target="tpu_custom_call" | custom-call | tf_op jit(solution)/shard_map/lon_strips/pallas_call | solution.py:195
  32.7 2.8 %collective-permute-start.2 = (f32[136,128]{1,0:T(8,128)}, f32[136,128]{1,0:T(8,128)S(1)}, u32[]{:S(2)}, u32[]{:S(2)}) collective-permute-start(f32[136,128]{1,0:T(8,128)} %get-tuple-element.20.own_left), channel_id=1, source_target_pairs={{1,0},{2,1},{3,2},{4,3},{5,4},{6,5},{7,6},{0,7},{9,8},{10,9},{11,1... | collective-permute-start | bytes 208904 | tf_op jit(solution)/shard_map/ppermute | solution.py:494
  35.4 0.0 collective-permute-start.3
  35.4 2.7 %collective-permute-done.2.from_right = f32[136,128]{1,0:T(8,128)S(1)} collective-permute-done((f32[136,128]{1,0:T(8,128)}, f32[136,128]{1,0:T(8,128)S(1)}, u32[]{:S(2)}, u32[]{:S(2)}) %collective-permute-start.2) | collective-permute-done | bytes 69664 | tf_op jit(solution)/shard_map/ppermute | solution.py:494
  38.2 3.9 %collective-permute-done.3.from_left = f32[136,128]{1,0:T(8,128)S(1)} collective-permute-done((f32[136,128]{1,0:T(8,128)}, f32[136,128]{1,0:T(8,128)S(1)}, u32[]{:S(2)}, u32[]{:S(2)}) %collective-permute-start.3) | collective-permute-done | bytes 69664 | tf_op jit(solution)/shard_map/ppermute | solution.py:495
  42.1 0.6 copy-done.4
  42.7 0.1 copy-done.13
  42.8 2.0 %lat_bands.1 = (f32[56,640]{1,0:T(8,128)}, f32[56,640]{1,0:T(8,128)}) custom-call(f32[2,56,512]{2,1,0:T(8,128)} %copy-done.8, f32[2,56,512]{2,1,0:T(8,128)} %copy-done.13, f32[136,128]{1,0:T(8,128)} %get-tuple-element.20.own_left, f32[136,128]{1,0:T(8,128)} %get-tuple-element.21.own_right, f32[136,128]{1,0:T(8,128)} %copy-done.2, f32[136,128]{1,0:T(8,128)} %copy-done.4, ...), custom_call_target="tpu_custom_call" | custom-call | tf_op jit(solution)/shard_map/lat_bands/pallas_call | solution.py:260
  44.8 2.3 %collective-permute-start.5 = (f32[56,640]{1,0:T(8,128)}, f32[56,640]{1,0:T(8,128)S(1)}, u32[]{:S(2)}, u32[]{:S(2)}) collective-permute-start(f32[56,640]{1,0:T(8,128)} %get-tuple-element.22.top), channel_id=1, source_target_pairs={{8,0},{16,8},{24,16},{32,24},{40,32},{48,40},{56,48},{64,56},{72,6... | collective-permute-start | bytes 430088 | tf_op jit(solution)/shard_map/ppermute | solution.py:500
  47.1 3.2 %collective-permute-start.4 = (f32[56,640]{1,0:T(8,128)}, f32[56,640]{1,0:T(8,128)S(1)}, u32[]{:S(2)}, u32[]{:S(2)}) collective-permute-start(f32[56,640]{1,0:T(8,128)} %get-tuple-element.23.bottom), channel_id=1, source_target_pairs={{0,8},{8,16},{16,24},{24,32},{32,40},{40,48},{48,56},{56,64},{64,7... | collective-permute-start | bytes 430088 | tf_op jit(solution)/shard_map/ppermute | solution.py:499
  50.4 0.1 pad_add_fusion.band
  50.4 1.0 collective-permute-done.5.below
  51.4 1.3 %collective-permute-done.4.above = f32[56,640]{1,0:T(8,128)S(1)} collective-permute-done((f32[56,640]{1,0:T(8,128)}, f32[56,640]{1,0:T(8,128)S(1)}, u32[]{:S(2)}, u32[]{:S(2)}) %collective-permute-start.4) | collective-permute-done | bytes 143392 | tf_op jit(solution)/shard_map/ppermute | solution.py:499
  52.7 0.9 copy-done.3
  53.6 0.9 copy-done.5
  54.5 0.9 copy-done.6
  55.4 0.9 copy-done.7
  56.3 0.9 copy-done.9
  57.2 0.9 copy-done.10
  58.1 29.2 %potential_solve.1 = (f32[128,512]{1,0:T(8,128)}, f32[128,512]{1,0:T(8,128)S(1)}, f32[128,512]{1,0:T(8,128)S(1)}, f32[128,1,128]{2,1,0:T(1,128)S(1)}) custom-call(f32[2,16]{1,0:T(2,128)S(1)} %copy-done.12, s32[2]{0:T(128)S(1)} %pad_add_fusion.band, f32[56,640]{1,0:T(8,128)S(1)} %copy-done.9, f32[56,640]{1,0:T(8,128)S(1)} %copy-done.10, ...), custom_call_target="tpu_custom_call" | custom-call | tf_op jit(solution)/shard_map/potential_solve/pallas_call | solution.py:425
  87.3 19.3 %all_to_all.5.fastest = f32[128,1,128]{2,1,0:T(1,128)S(1)} all-to-all(f32[128,1,128]{2,1,0:T(1,128)S(1)} %get-tuple-element.27), channel_id=1, replica_groups=mesh['lat'=16,'lon'=8] {'lat','lon'}, dimensions={0} | all-to-all | bytes 131072 | tf_op jit(solution)/shard_map/all_to_all | solution.py:509
  106.6 1.8 %ion_advection.1 = f32[3,128,512]{2,1,0:T(8,128)} custom-call(f32[128,1,128]{2,1,0:T(1,128)S(1)} %all_to_all.5.fastest, f32[128,512]{1,0:T(8,128)S(1)} %get-tuple-element.28.drift_east, f32[128,512]{1,0:T(8,128)S(1)} %get-tuple-element.29.drift_north, f32[3,128,512]{2,1,0:T(8,128)S(1)} %copy-done, f32[56,640]{1,0:T(8,128)S(1)} %collective-permute-done.4.above, ...), custom_call_target="tpu_custom_call" | custom-call | tf_op jit(solution)/shard_map/ion_advection/pallas_call | solution.py:468
  (19 shorter events, 0.0 us)
Async XLA Ops:
  0.6 2.2 %copy-start.1 = (f32[16,128,512]{2,1,0:T(8,128)S(1)}, f32[16,128,512]{2,1,0:T(8,128)}, u32[]{:S(2)}) copy-start(f32[16,128,512]{2,1,0:T(8,128)} %pedersen.1) | copy-start | bytes 12582916
  2.8 49.9 %copy-start.12 = (f32[2,16]{1,0:T(2,128)S(1)}, f32[2,16]{1,0:T(2,128)}, u32[]{:S(2)}) copy-start(f32[2,16]{1,0:T(2,128)} %constant.10.clone.factors) | copy-start | bytes 388
  11.2 0.7 copy-start.8
  11.9 0.7 copy-start.11
  12.6 94.0 %copy-start = (f32[3,128,512]{2,1,0:T(8,128)S(1)}, f32[3,128,512]{2,1,0:T(8,128)}, u32[]{:S(2)}) copy-start(f32[3,128,512]{2,1,0:T(8,128)} %ions.1) | copy-start | bytes 2359300
  12.6 29.5 %collective-permute-start = (f32[2,56,512]{2,1,0:T(8,128)S(1)}, f32[2,56,512]{2,1,0:T(8,128)S(1)}, u32[]{:S(2)}, u32[]{:S(2)}) collective-permute-start(f32[2,56,512]{2,1,0:T(8,128)S(1)} %get-tuple-element.17), channel_id=1, source_target_pairs={{0,120},{8,112},{16,104},{24,96},{32,88},{40,80},{48,72},{56,64},{... | collective-permute-start | bytes 688136 | tf_op jit(solution)/shard_map/ppermute | solution.py:491
  20.2 9.9 %collective-permute-start.1 = (f32[2,136,128]{2,1,0:T(8,128)S(1)}, f32[2,136,128]{2,1,0:T(8,128)S(1)}, u32[]{:S(2)}, u32[]{:S(2)}) collective-permute-start(f32[2,136,128]{2,1,0:T(8,128)S(1)} %get-tuple-element.19), channel_id=1, source_target_pairs={{0,120},{8,112},{16,104},{24,96},{32,88},{40,80},{48,72},{56,64},{... | collective-permute-start | bytes 417800 | tf_op jit(solution)/shard_map/ppermute | solution.py:490
  20.2 30.2 %collective-permute-start.6 = (f32[2,80,512]{2,1,0:T(8,128)S(1)}, f32[2,80,512]{2,1,0:T(8,128)S(1)}, u32[]{:S(2)}, u32[]{:S(2)}) collective-permute-start(f32[2,80,512]{2,1,0:T(8,128)S(1)} %get-tuple-element.25), channel_id=1, source_target_pairs={{0,120},{8,112},{16,104},{24,96},{32,88},{40,80},{48,72},{56,64},{... | collective-permute-start | bytes 983048 | tf_op jit(solution)/shard_map/ppermute | solution.py:492
  30.1 0.7 copy-start.14
  32.7 5.5 %collective-permute-start.2 = (f32[136,128]{1,0:T(8,128)}, f32[136,128]{1,0:T(8,128)S(1)}, u32[]{:S(2)}, u32[]{:S(2)}) collective-permute-start(f32[136,128]{1,0:T(8,128)} %get-tuple-element.20.own_left), channel_id=1, source_target_pairs={{1,0},{2,1},{3,2},{4,3},{5,4},{6,5},{7,6},{0,7},{9,8},{10,9},{11,1... | collective-permute-start | bytes 208904 | tf_op jit(solution)/shard_map/ppermute | solution.py:494
  35.4 6.7 %collective-permute-start.3 = (f32[136,128]{1,0:T(8,128)}, f32[136,128]{1,0:T(8,128)S(1)}, u32[]{:S(2)}, u32[]{:S(2)}) collective-permute-start(f32[136,128]{1,0:T(8,128)} %get-tuple-element.21.own_right), channel_id=1, source_target_pairs={{0,1},{1,2},{2,3},{3,4},{4,5},{5,6},{6,7},{7,0},{8,9},{9,10},{10,1... | collective-permute-start | bytes 208904 | tf_op jit(solution)/shard_map/ppermute | solution.py:495
  38.2 4.0 %copy-start.2 = (f32[136,128]{1,0:T(8,128)}, f32[136,128]{1,0:T(8,128)S(1)}, u32[]{:S(2)}) copy-start(f32[136,128]{1,0:T(8,128)S(1)} %collective-permute-done.2.from_right) | copy-start | bytes 208900
  42.1 0.6 copy-start.4
  42.1 0.7 copy-start.13
  44.8 6.6 %collective-permute-start.5 = (f32[56,640]{1,0:T(8,128)}, f32[56,640]{1,0:T(8,128)S(1)}, u32[]{:S(2)}, u32[]{:S(2)}) collective-permute-start(f32[56,640]{1,0:T(8,128)} %get-tuple-element.22.top), channel_id=1, source_target_pairs={{8,0},{16,8},{24,16},{32,24},{40,32},{48,40},{56,48},{64,56},{72,6... | collective-permute-start | bytes 430088 | tf_op jit(solution)/shard_map/ppermute | solution.py:500
  47.1 5.6 %collective-permute-start.4 = (f32[56,640]{1,0:T(8,128)}, f32[56,640]{1,0:T(8,128)S(1)}, u32[]{:S(2)}, u32[]{:S(2)}) collective-permute-start(f32[56,640]{1,0:T(8,128)} %get-tuple-element.23.bottom), channel_id=1, source_target_pairs={{0,8},{8,16},{16,24},{24,32},{32,40},{40,48},{48,56},{56,64},{64,7... | collective-permute-start | bytes 430088 | tf_op jit(solution)/shard_map/ppermute | solution.py:499
  52.7 0.9 copy-start.3
  53.6 0.9 copy-start.5
  54.5 0.9 copy-start.6
  55.4 0.9 copy-start.7
  56.3 0.9 copy-start.9
  57.2 0.9 copy-start.10

commit v2 on v1

v2 whole, which is shorter than its diff:
```python
import functools

import jax
import jax.numpy as jnp
from jax import lax
from jax.experimental import pallas as pl
from jax.experimental.pallas import tpu as pltpu
from jax.sharding import PartitionSpec as P

LEV = 16
SWEEPS = 16
DAMPING = 0.0001
LOW_BOUND = 0.05
HIGH_BOUND = 2.0
COURANT = 0.8
MOBILITY = (1.0, 0.6, 0.3)

LANES = 128
ROWS = 128
COLS = 512
TILES = COLS // LANES
WIDE = COLS + LANES
EDGE = 16
HALO = 24
MID = ROWS - 2 * EDGE
EXT = ROWS + 2 * HALO
SIGMA_PLUS = 2 * EDGE
CURRENT = SIGMA_PLUS + 1
IONS = SIGMA_PLUS + 2
NORTH = SIGMA_PLUS + 5
LINES = SIGMA_PLUS + 8
CHUNK = 16
VMEM_BYTES = 32 * 1024 * 1024


def chebyshev_factors():
    theta = 0.5 * (HIGH_BOUND + LOW_BOUND)
    delta = 0.5 * (HIGH_BOUND - LOW_BOUND)
    sigma_one = theta / delta
    rho_prev = 1.0 / sigma_one
    first_list = []
    second_list = []
    for sweep in range(SWEEPS):
        rho_next = 1.0 / (2.0 * sigma_one - rho_prev)
        first_list.append(rho_next * rho_prev)
        second_list.append(2.0 * rho_next / delta)
        rho_prev = rho_next
    return (theta, first_list, second_list)


def in_vmem(kernel, name, shapes, *fields):
    whole = pl.BlockSpec(memory_space=pltpu.VMEM)
    return pl.pallas_call(
        kernel,
        in_specs=[whole] * len(fields),
        out_specs=jax.tree.map(lambda _: whole, shapes),
        out_shape=shapes,
        compiler_params=pltpu.CompilerParams(vmem_limit_bytes=VMEM_BYTES),
        name=name,
    )(*fields)


def lane_index(rows):
    return lax.broadcasted_iota(jnp.int32, (rows, LANES), 1)


def row_index(rows, cols=LANES):
    return lax.broadcasted_iota(jnp.int32, (rows, cols), 0)


def reversed_rows(tile):
    row = row_index(8, tile.shape[1])
    tile = pltpu.roll(tile, 4, 0)
    tile = jnp.where((row & 2) == 0, pltpu.roll(tile, 6, 0), pltpu.roll(tile, 2, 0))
    return jnp.where((row & 1) == 0, pltpu.roll(tile, 7, 0), pltpu.roll(tile, 1, 0))


def shifted(tiles, to_right):
    count = len(tiles)
    lane = lane_index(tiles[0].shape[0])
    if to_right:
        turned = [pltpu.roll(tile, 1, 1) for tile in tiles]
        return [jnp.where(lane == 0, turned[t - 1], turned[t]) for t in range(count)]
    turned = [pltpu.roll(tile, LANES - 1, 1) for tile in tiles]
    return [jnp.where(lane == LANES - 1, turned[(t + 1) % count], turned[t]) for t in range(count)]


def local_source(east, north, source, start, rows):
    tiles = [east[start : start + rows, t * LANES : (t + 1) * LANES] for t in range(TILES)]
    lane = lane_index(rows)
    row = row_index(rows)
    left = [pltpu.roll(tile, 1, 1) for tile in tiles]
    right = [pltpu.roll(tile, LANES - 1, 1) for tile in tiles]
    zero = jnp.zeros((rows, LANES), jnp.float32)
    for t in range(TILES):
        span = slice(t * LANES, (t + 1) * LANES)
        before = jnp.where(lane == 0, left[t - 1] if t else zero, left[t])
        after = jnp.where(lane == LANES - 1, right[t + 1] if t < TILES - 1 else zero, right[t])
        here = north[start : start + rows, span]
        up = pltpu.roll(here, 1, 0)
        down = pltpu.roll(here, rows - 1, 0)
        above = north[start - 8 : start, span][7:8] if start else zero[:1]
        below = north[start + rows : start + rows + 8, span][:1] if start + rows < ROWS else zero[:1]
        up = jnp.where(row == 0, above, up)
        down = jnp.where(row == rows - 1, below, down)
        source[start : start + rows, span] = 0.5 * (after - before) + 0.5 * (down - up)


def put_lanes(tile, source, at, first, count):
    lane = lane_index(tile.shape[0])
    turn = (first - at) % LANES
    moved = pltpu.roll(source, turn, 1) if turn else source
    return jnp.where((lane >= first) & (lane < first + count), moved, tile)


def write_pieces(sigma, east, north, source, edges, middle):
    for start in range(0, ROWS, 8):
        local_source(east, north, source, start, 8)
    row = row_index(8)
    wide = row_index(8, COLS)
    for side in range(2):
        at = side * (COLS - LANES)
        span = slice(at, at + LANES)
        near = side * (LANES - EDGE)
        strip = jnp.zeros((ROWS, LANES), jnp.float32)
        strip = put_lanes(strip, sigma[:, span], near, 0, EDGE)
        strip = put_lanes(strip, source[:, span], near, EDGE, EDGE)
        strip = put_lanes(strip, sigma[:, span], LANES - EDGE - 1 if side else EDGE, SIGMA_PLUS, 1)
        strip = put_lanes(strip, east[:, span], side * (LANES - 1), CURRENT, 1)
        turned = strip.T
        edges[side, :SIGMA_PLUS, COLS:] = turned[:SIGMA_PLUS]
        tile = turned[SIGMA_PLUS:LINES]
        tile = jnp.where(row == NORTH - SIGMA_PLUS, north[0:8, span][:1], tile)
        tile = jnp.where(row == NORTH + 1 - SIGMA_PLUS, north[ROWS - 8 :, span][7:8], tile)
        edges[side, SIGMA_PLUS:, COLS:] = tile
        first = side * (ROWS - EDGE)
        edges[side, :EDGE, :COLS] = sigma[first : first + EDGE]
        edges[side, EDGE : 2 * EDGE, :COLS] = source[first : first + EDGE]
        if side == 0:
            further, line = (sigma[EDGE : EDGE + 8][:1], north[0:8][:1])
        else:
            further, line = (sigma[first - 8 : first][7:8], north[ROWS - 8 :][7:8])
        tile = jnp.where(wide == 0, further, 0.0)
        edges[side, SIGMA_PLUS:, :COLS] = jnp.where(wide == 1, line, tile)
    middle[0] = sigma[EDGE : ROWS - EDGE]
    middle[1] = source[EDGE : ROWS - EDGE]


def column_kernel(
    pedersen, hall, east_wind, north_wind,
    own_edges, own_middle, far_edges, far_middle,
    held, sigma, east, north, sigma_far, east_far, north_far, source, arrived,
):
    steps = ROWS // CHUNK

    def copies(step):
        rows = pl.ds(pl.multiple_of(step * CHUNK, CHUNK), CHUNK)
        return [
            pltpu.make_async_copy(field.at[:, rows, :], held.at[i, :, rows, :], arrived.at[i, step])
            for i, field in enumerate((pedersen, hall, east_wind, north_wind))
        ]

    for step in range(steps):
        for copy in copies(step):
            copy.start()

    def body(step, _):
        for copy in copies(step):
            copy.wait()
        for half in range(CHUNK // 8):
            near = pl.ds(pl.multiple_of(step * CHUNK + half * 8, 8), 8)
            away = pl.ds(pl.multiple_of(ROWS - 8 - step * CHUNK - half * 8, 8), 8)
            totals = [jnp.zeros((8, COLS), jnp.float32) for _ in range(3)]
            for level in range(LEV):
                layer = (0.5 + level / LEV) / LEV
                along = layer * held[0, level, near, :]
                across = layer * held[1, level, near, :]
                wind_e = held[2, level, near, :]
                wind_n = held[3, level, near, :]
                totals[0] = totals[0] + along
                totals[1] = totals[1] + (along * wind_e + across * wind_n)
                totals[2] = totals[2] + (along * wind_n - across * wind_e)
            pairs = zip(totals, (sigma, east, north), (sigma_far, east_far, north_far))
            for total, here, there in pairs:
                here[near, :] = total
                there[away, :] = reversed_rows(total)
        return 0

    lax.fori_loop(0, steps, body, 0)
    write_pieces(sigma_far, east_far, north_far, source, far_edges, far_middle)
    write_pieces(sigma, east, north, source, own_edges, own_middle)


def column_sums(*levels):
    shapes = [(2, LINES, WIDE), (2, MID, COLS)] * 2
    field = pltpu.VMEM((ROWS, COLS), jnp.float32)
    return pl.pallas_call(
        column_kernel,
        in_specs=[pl.BlockSpec(memory_space=pltpu.HBM)] * 4,
        out_specs=[pl.BlockSpec(memory_space=pltpu.VMEM)] * 4,
        out_shape=[jax.ShapeDtypeStruct(shape, jnp.float32) for shape in shapes],
        scratch_shapes=[pltpu.VMEM((4, LEV, ROWS, COLS), jnp.float32)]
        + [field] * 7
        + [pltpu.SemaphoreType.DMA((4, ROWS // CHUNK))],
        compiler_params=pltpu.CompilerParams(vmem_limit_bytes=VMEM_BYTES),
        name="column_sums",
    )(*levels)


def ion_kernel(ions, out):
    row = row_index(8)
    for side in range(2):
        at = side * (COLS - LANES)
        tile = jnp.zeros((8, LANES), jnp.float32)
        for s in range(3):
            turned = ions[s, :, at : at + LANES].T
            line = turned[LANES - 1 :] if side else turned[:1]
            tile = jnp.where(row == IONS - SIGMA_PLUS + s, line, tile)
        out[side] = tile


def ion_columns(ions):
    shape = jax.ShapeDtypeStruct((2, 8, LANES), jnp.float32)
    return in_vmem(ion_kernel, "ion_columns", shape, ions)


def strip_kernel(own, far, ion_lines, to_left, to_right):
    for side, out in ((0, to_left), (1, to_right)):
        total = own[side, :, COLS:] + far[side, :, COLS:]
        out[:SIGMA_PLUS] = total[:SIGMA_PLUS]
        out[SIGMA_PLUS:] = total[SIGMA_PLUS:] + ion_lines[side]


def strips_to_send(*fields):
    shape = jax.ShapeDtypeStruct((LINES, LANES), jnp.float32)
    return in_vmem(strip_kernel, "lon_strips", [shape, shape], *fields)


def turned_back(strip):
    rest = jnp.zeros((LANES - LINES, LANES), jnp.float32)
    return jnp.concatenate([strip[...], rest], 0).T


def band_kernel(own, far, own_left, own_right, from_right, from_left, ions, top, bottom, beside):
    right, left = (turned_back(from_right), turned_back(from_left))
    ours_right, ours_left = (turned_back(own_right), turned_back(own_left))
    blank = jnp.zeros((ROWS, LANES), jnp.float32)
    sigma = put_lanes(blank, right, 0, 0, EDGE)
    sigma = put_lanes(sigma, right, SIGMA_PLUS, EDGE, 1)
    sigma = put_lanes(sigma, left, 0, LANES - EDGE, EDGE)
    sigma = put_lanes(sigma, left, SIGMA_PLUS, LANES - EDGE - 1, 1)
    source = put_lanes(blank, right, EDGE, 0, EDGE)
    source = put_lanes(source, left, EDGE, LANES - EDGE, EDGE)
    source = source - 0.5 * put_lanes(blank, ours_right, CURRENT, 0, 1)
    source = source + 0.5 * put_lanes(blank, ours_left, CURRENT, LANES - 1, 1)
    mend = put_lanes(blank, -0.5 * left, CURRENT, 0, 1)
    mend = put_lanes(mend, 0.5 * right, CURRENT, LANES - 1, 1)
    beside[0] = sigma
    beside[1] = source
    beside[2] = mend

    part = slice(EDGE, 2 * EDGE)
    lane = lane_index(EDGE)
    row = row_index(8)
    wide = row_index(8, COLS)
    for side, out in ((0, top), (1, bottom)):
        first = side * (ROWS - EDGE)
        rows = slice(first, first + EDGE)
        out[:SIGMA_PLUS, :COLS] = own[side, :SIGMA_PLUS, :COLS] + far[side, :SIGMA_PLUS, :COLS]
        out[part, :LANES] += jnp.where(lane == 0, mend[rows], 0.0)
        out[part, COLS - LANES : COLS] += jnp.where(lane == LANES - 1, mend[rows], 0.0)
        lines = own[side, SIGMA_PLUS:, :COLS] + far[side, SIGMA_PLUS:, :COLS]
        for s in range(3):
            line = ions[s, ROWS - 8 :][7:8] if side else ions[s, :8][:1]
            lines = jnp.where(wide == IONS - SIGMA_PLUS + s, line, lines)
        out[SIGMA_PLUS:, :COLS] = lines
        out[:EDGE, COLS:] = sigma[rows]
        out[part, COLS:] = source[rows]
        further = sigma[first - 1 : first] if side else sigma[EDGE : EDGE + 1]
        north = jnp.where(
            lane[:1] < LANES // 2,
            from_right[SIGMA_PLUS:][NORTH - SIGMA_PLUS + side :][:1],
            from_left[SIGMA_PLUS:][NORTH - SIGMA_PLUS + side :][:1],
        )
        tile = jnp.where(row == 0, further, 0.0)
        out[SIGMA_PLUS:, COLS:] = jnp.where(row == CURRENT - SIGMA_PLUS, north, tile)


def bands_to_send(*fields):
    shape = jax.ShapeDtypeStruct((LINES, WIDE), jnp.float32)
    beside = jax.ShapeDtypeStruct((3, ROWS, LANES), jnp.float32)
    return in_vmem(band_kernel, "lat_bands", [shape, shape, beside], *fields)


def solve_kernel(
    factors, band, top, bottom, beside, above, below, own_middle, far_middle,
    potential, drift_east, drift_north, fastest,
    sigma, sigma_next, sigma_prev, half_inverse, scaled_source, update, field_a, field_b, carried_a, carried_b,
):
    theta = 0.5 * (HIGH_BOUND + LOW_BOUND)
    fields = (field_a, field_b)
    fluxes = (carried_a, carried_b)
    count = TILES + 1
    spans = [slice(t * LANES, (t + 1) * LANES) for t in range(count)]
    middle = slice(EDGE, ROWS - EDGE)
    row = row_index(8)
    low = HALO + ROWS

    for t in range(count):
        span = spans[t]
        for piece, at in ((above, HALO - EDGE), (top, HALO), (bottom, low - EDGE), (below, low)):
            sigma[t, at : at + EDGE] = piece[:EDGE, span]
            scaled_source[t, at : at + EDGE] = piece[EDGE : 2 * EDGE, span]
        outer = above[SIGMA_PLUS:, span][:1]
        sigma[t, :8] = jnp.where(row == 7, outer, 0.0)
        outer = below[SIGMA_PLUS:, span][:1]
        sigma[t, EXT - 8 :] = jnp.where(row == 0, outer, 0.0)
        inner = slice(HALO + EDGE, low - EDGE)
        if t < TILES:
            sigma[t, inner] = own_middle[0, :, span] + far_middle[0, :, span]
            source = own_middle[1, :, span] + far_middle[1, :, span]
            lane = lane_index(MID)
            if t == 0:
                source = source + jnp.where(lane == 0, beside[2, middle], 0.0)
            if t == TILES - 1:
                source = source + jnp.where(lane == LANES - 1, beside[2, middle], 0.0)
        else:
            sigma[t, inner] = beside[0, middle]
            source = beside[1, middle]
        scaled_source[t, inner] = source
        for at, spot, piece, half in (
            (HALO - 8, 7, top, 0.5),
            (HALO, 0, above, -0.5),
            (low - 8, 7, below, 0.5),
            (low, 0, bottom, -0.5),
        ):
            line = half * piece[SIGMA_PLUS:, span][CURRENT - SIGMA_PLUS :][:1]
            tile = scaled_source[t, at : at + 8]
            scaled_source[t, at : at + 8] = tile + jnp.where(row == spot, line, 0.0)

    first_band = band[0] == 0
    last_band = band[0] == band[1] - 1
    blank = jnp.zeros((8, LANES), jnp.float32)
    for t in range(count):
        for slot in range(2):
            for at in (0, EXT - 8):
                fields[slot][t, at : at + 8] = blank
                fluxes[slot][t, at : at + 8] = blank

    for start in range(8, EXT - 8, 8):
        here = [sigma[t, start : start + 8] for t in range(count)]
        sides = [sigma[t, start - 1 : start + 7] + sigma[t, start + 1 : start + 9] for t in range(count)]
        tall = [here[t] + 0.5 * sides[t] for t in range(count)]
        left = shifted(tall, True)
        right = shifted(tall, False)
        following = shifted(here, False)
        preceding = shifted(here, True)
        outside = None
        if start < HALO:
            outside = first_band
        if start >= HALO + ROWS:
            outside = last_band
        for t in range(count):
            diagonal = 0.5 * (6.0 * here[t] + (sides[t] + (left[t] + right[t]))) + DAMPING
            inverse = 1.0 / diagonal
            if outside is not None:
                inverse = jnp.where(outside, 0.0, inverse)
            source = scaled_source[t, start : start + 8] * inverse
            initial = source * (1.0 / theta)
            sigma_next[t, start : start + 8] = following[t]
            sigma_prev[t, start : start + 8] = preceding[t]
            half_inverse[t, start : start + 8] = 0.5 * inverse
            scaled_source[t, start : start + 8] = source
            update[t, start : start + 8] = initial
            field_b[t, start : start + 8] = initial
            carried_b[t, start : start + 8] = here[t] * initial

    def sweep(k, now, later, low, high):
        field_now, carried_now = (fields[now], fluxes[now])
        field_later, carried_later = (fields[later], fluxes[later])
        keep = factors[0, k - 1]
        gain = factors[1, k - 1]
        for start in range(low, high, 8):
            rows = slice(start, start + 8)
            upper = slice(start - 1, start + 7)
            lower = slice(start + 1, start + 9)
            centre, eastward, westward = ([], [], [])
            for t in range(count):
                value = field_now[t, rows]
                flux = carried_now[t, rows]
                value_sides = field_now[t, upper] + field_now[t, lower]
                flux_sides = carried_now[t, upper] + carried_now[t, lower]
                tall = value + 0.5 * value_sides
                flux_tall = flux + 0.5 * flux_sides
                centre.append(sigma[t, rows] * value_sides + flux_sides)
                eastward.append(sigma_next[t, rows] * tall + flux_tall)
                westward.append(sigma_prev[t, rows] * tall + flux_tall)
            from_west = shifted(eastward, True)
            from_east = shifted(westward, False)
            for t in range(count):
                total = centre[t] + (from_west[t] + from_east[t])
                value = field_now[t, rows]
                residual = (scaled_source[t, rows] - value) + half_inverse[t, rows] * total
                step = keep * update[t, rows] + gain * residual
                update[t, rows] = step
                value = value + step
                field_later[t, rows] = value
                carried_later[t, rows] = sigma[t, rows] * value

    def early(pair, _):
        sweep(2 * pair + 1, 1, 0, 8, EXT - 8)
        sweep(2 * pair + 2, 0, 1, 8, EXT - 8)
        return 0

    def late(pair, _):
        sweep(2 * pair + 9, 1, 0, 16, EXT - 16)
        sweep(2 * pair + 10, 0, 1, 16, EXT - 16)
        return 0

    lax.fori_loop(0, 4, early, 0)
    lax.fori_loop(0, 3, late, 0)
    sweep(15, 1, 0, 16, EXT - 16)

    last = fields[SWEEPS % 2]
    top_speed = jnp.zeros((8, LANES), jnp.float32)
    for start in range(HALO, HALO + ROWS, 8):
        rows = slice(start, start + 8)
        out = slice(start - HALO, start - HALO + 8)
        tiles = [last[t, rows] for t in range(count)]
        west = shifted(tiles, True)
        east = shifted(tiles, False)
        for t in range(TILES):
            potential[out, spans[t]] = tiles[t]
            lift = -0.5 * (last[t, start + 1 : start + 9] - last[t, start - 1 : start + 7])
            shove = 0.5 * (east[t] - west[t])
            drift_east[out, spans[t]] = lift
            drift_north[out, spans[t]] = shove
            top_speed = jnp.maximum(top_speed, jnp.abs(lift) + jnp.abs(shove))
    peak = jnp.max(top_speed, axis=1, keepdims=True)
    peak = jnp.max(peak, axis=0, keepdims=True)
    fastest[...] = jnp.broadcast_to(peak[None], fastest.shape)


def solve(peers, factors, band, *fields):
    shapes = [(ROWS, COLS)] * 3 + [(peers, 1, LANES)]
    plane = (TILES + 1, EXT, LANES)
    memory = pltpu.VMEM(plane, jnp.float32)
    return pl.pallas_call(
        solve_kernel,
        in_specs=[pl.BlockSpec(memory_space=pltpu.SMEM)] * 2
        + [pl.BlockSpec(memory_space=pltpu.VMEM)] * len(fields),
        out_specs=[pl.BlockSpec(memory_space=pltpu.VMEM)] * 4,
        out_shape=[jax.ShapeDtypeStruct(shape, jnp.float32) for shape in shapes],
        scratch_shapes=[memory] * 10,
        compiler_params=pltpu.CompilerParams(vmem_limit_bytes=VMEM_BYTES),
        name="potential_solve",
    )(factors, band, *fields)


def advect_kernel(fastest, drift_east, drift_north, ions, above, below, from_right, from_left, out):
    peak = jnp.max(fastest[...], axis=0)
    peak = jnp.max(peak, axis=1, keepdims=True)
    time_step = COURANT / (peak + 1e-06)
    lane = lane_index(ROWS)
    wide = row_index(ROWS, LANES)
    beyond_right, beyond_left = (turned_back(from_right), turned_back(from_left))
    for s in range(3):
        pace = MOBILITY[s] * time_step
        tiles = [ions[s, :, t * LANES : (t + 1) * LANES] for t in range(TILES)]
        left = [pltpu.roll(tile, 1, 1) for tile in tiles]
        right = [pltpu.roll(tile, LANES - 1, 1) for tile in tiles]
        edge_right = pltpu.roll(beyond_right, LANES - 1 - IONS - s, 1)
        edge_left = pltpu.roll(beyond_left, LANES - IONS - s, 1)
        for t in range(TILES):
            span = slice(t * LANES, (t + 1) * LANES)
            density = tiles[t]
            west = jnp.where(lane == 0, left[t - 1] if t else edge_left, left[t])
            east = jnp.where(lane == LANES - 1, right[t + 1] if t < TILES - 1 else edge_right, right[t])
            behind = above[SIGMA_PLUS:, span][IONS - SIGMA_PLUS + s :][:1]
            ahead = below[SIGMA_PLUS:, span][IONS - SIGMA_PLUS + s :][:1]
            south = jnp.where(wide == 0, behind, pltpu.roll(density, 1, 0))
            north = jnp.where(wide == ROWS - 1, ahead, pltpu.roll(density, ROWS - 1, 0))
            cross_east = pace * drift_east[:, span]
            cross_north = pace * drift_north[:, span]
            result = density - jnp.maximum(cross_east, 0.0) * (density - west)
            result = result - jnp.minimum(cross_east, 0.0) * (east - density)
            result = result - jnp.maximum(cross_north, 0.0) * (density - south)
            result = result - jnp.minimum(cross_north, 0.0) * (north - density)
            out[s, :, span] = result


def advect(*fields):
    shape = jax.ShapeDtypeStruct((3, ROWS, COLS), jnp.float32)
    return in_vmem(advect_kernel, "ion_advection", shape, *fields)


def shards(pedersen, hall_conductivity, east_wind, north_wind, ion_density):
    lats = lax.axis_size("lat")
    lons = lax.axis_size("lon")
    mirror = [(i, lats - 1 - i) for i in range(lats)]
    eastward = [(i, (i + 1) % lons) for i in range(lons)]
    westward = [(j, i) for i, j in eastward]
    rising = [(i, i + 1) for i in range(lats - 1)]
    falling = [(j, i) for i, j in rising]

    own_edges, own_middle, edges, middle = column_sums(
        pedersen, hall_conductivity, east_wind, north_wind
    )
    far_edges = lax.ppermute(edges, "lat", mirror)
    far_middle = lax.ppermute(middle, "lat", mirror)
    ion_lines = ion_columns(ion_density)
    to_left, to_right = strips_to_send(own_edges, far_edges, ion_lines)
    from_right = lax.ppermute(to_left, "lon", westward)
    from_left = lax.ppermute(to_right, "lon", eastward)
    top, bottom, beside = bands_to_send(
        own_edges, far_edges, to_left, to_right, from_right, from_left, ion_density
    )
    above = lax.ppermute(bottom, "lat", rising)
    below = lax.ppermute(top, "lat", falling)

    theta, first_list, second_list = chebyshev_factors()
    factors = jnp.array([first_list, second_list], jnp.float32)
    band = jnp.stack([lax.axis_index("lat").astype(jnp.int32), jnp.int32(lats)])
    potential, drift_east, drift_north, peaks = solve(
        lats * lons, factors, band, top, bottom, beside, above, below, own_middle, far_middle
    )
    peaks = lax.all_to_all(peaks, ("lat", "lon"), 0, 0, tiled=True)
    ion_update = advect(
        peaks, drift_east, drift_north, ion_density, above, below, from_right, from_left
    )
    return (potential, ion_update)


def solution(mesh):
    spec = P(None, "lat", "lon")
    return jax.shard_map(
        shards,
        mesh=mesh,
        in_specs=(spec,) * 5,
        out_specs=(P("lat", "lon"), spec),
        check_vma=False,
    )
```

time: 109 us -> 81.7 us (0.75)
  Pallas kernels: 43.3 us -> 14.4 us
  waiting for transfers between devices: 13.4 us -> 19.4 us
  starting transfers between devices: 21.3 us -> 17.1 us
  blocking collectives: 19.3 us -> 21.1 us
  local copies, waits for them, and re-layouts: 10.2 us -> 8.75 us
    pallas_call x1, Pallas kernels: 29.2 us -> 7.17 us  [solve(): pl.pallas_call(solve_kernel, in_specs=[pl.BlockSpec(memory_space=pltpu.SM...]
    ppermute x2 -> x1, waiting for transfers between devices: 4.5 us -> 13 us  [shards(): far_edges = lax.ppermute(edges, 'lat', mirror)]
    ppermute x2 -> x1, starting transfers between devices: 7.64 us -> 0.09 us  [shards(): far_edges = lax.ppermute(edges, 'lat', mirror)]
    pallas_call x4 -> x5, Pallas kernels: 14.1 us -> 7.19 us  [the longest x1 5 us: column_sums(): pl.pallas_call(column_kernel, in_specs=[pl.BlockSpec(memory_space=pltpu.H...]
    ppermute x1, starting transfers between devices: 5.33 us -> 7.69 us  [shards(): far_middle = lax.ppermute(middle, 'lat', mirror)]
    ppermute x1, waiting for transfers between devices: 2.71 us -> 0.91 us  [shards(): from_right = lax.ppermute(to_left, 'lon', westward)]
    all_to_all x1, blocking collectives: 19.3 us -> 21.1 us  [shards(): peaks = lax.all_to_all(peaks, ('lat', 'lon'), 0, 0, tiled=True)]
    unnamed x30 -> x12, local copies, waits for them, and re-layouts: 10.2 us -> 8.75 us
  transfers between devices with their start and end apart: 7 -> 6, of which waited for: 5 -> 5; matrix products, arithmetic and copies ran while one was open for 0% -> 0% of each run, Pallas kernels for 4% -> 1%
where the time goes in v2:
time: 81.7 us; the launch traced here: 81.4 us
  blocking collectives  21.1 us (26%)
  waiting for transfers between devices  19.4 us (24%)
  starting transfers between devices  17.1 us (21%)
  Pallas kernels  14.4 us (18%)
  local copies, waits for them, and re-layouts  8.75 us (11%)
    all_to_all x1, blocking collectives, shards(): peaks = lax.all_to_all(peaks, ('lat', 'lon'), 0, 0, tiled=True)  21.1 us
    ppermute x1, waiting for transfers between devices, shards(): far_edges = lax.ppermute(edges, 'lat', mirror)  13 us
    unnamed x12, local copies, waits for them, and re-layouts  8.75 us
    ppermute x1, starting transfers between devices, shards(): far_middle = lax.ppermute(middle, 'lat', mirror)  7.69 us
    pallas_call x1, Pallas kernels, solve(): pl.pallas_call(solve_kernel, in_specs=[pl.BlockSpec(memory_space=pltpu.SM...  7.17 us
    pallas_call x1, Pallas kernels, column_sums(): pl.pallas_call(column_kernel, in_specs=[pl.BlockSpec(memory_space=pltpu.H...  5 us
    ppermute x1, waiting for transfers between devices, shards(): from_left = lax.ppermute(to_right, 'lon', eastward)  3.83 us
    ppermute x1, starting transfers between devices, shards(): below = lax.ppermute(top, 'lat', falling)  3.55 us
  transfers between devices with their start and end apart: 6, of which 5 were waited for; matrix products, arithmetic and copies ran while one was open for 0% of the time, Pallas kernels for 1%

profile of v2, /device:TPU:1, one launch (start us, length us, event | category | flops | bytes accessed | tf_op | source)
XLA Modules:
  0.0 81.4 jit_solution(5741544132239642758)
XLA Ops:
  0.6 0.0 copy-start.1
  0.6 2.2 %copy-done.1 = f32[16,128,512]{2,1,0:T(8,128)S(1)} copy-done((f32[16,128,512]{2,1,0:T(8,128)S(1)}, f32[16,128,512]{2,1,0:T(8,128)}, u32[]{:S(2)}) %copy-start.1) | copy-done | bytes 4194328
  2.8 0.0 copy-start.2
  2.8 2.2 %copy-done.2 = f32[16,128,512]{2,1,0:T(8,128)S(1)} copy-done((f32[16,128,512]{2,1,0:T(8,128)S(1)}, f32[16,128,512]{2,1,0:T(8,128)}, u32[]{:S(2)}) %copy-start.2) | copy-done | bytes 4194328
  5.0 0.0 copy-start.3
  5.0 2.2 %copy-done.3 = f32[16,128,512]{2,1,0:T(8,128)S(1)} copy-done((f32[16,128,512]{2,1,0:T(8,128)S(1)}, f32[16,128,512]{2,1,0:T(8,128)}, u32[]{:S(2)}) %copy-start.3) | copy-done | bytes 4194328
  7.2 0.0 copy-start.4
  7.2 2.2 %copy-done.4 = f32[16,128,512]{2,1,0:T(8,128)S(1)} copy-done((f32[16,128,512]{2,1,0:T(8,128)S(1)}, f32[16,128,512]{2,1,0:T(8,128)}, u32[]{:S(2)}) %copy-start.4) | copy-done | bytes 4194328
  9.4 0.0 copy-start
  9.4 0.0 copy-start.5
  9.4 5.0 %column_sums.1 = (f32[2,40,640]{2,1,0:T(8,128)S(1)}, f32[2,96,512]{2,1,0:T(8,128)S(1)}, f32[2,40,640]{2,1,0:T(8,128)S(1)}, f32[2,96,512]{2,1,0:T(8,128)S(1)}) custom-call(f32[16,128,512]{2,1,0:T(8,128)S(1)} %copy-done.1, f32[16,128,512]{2,1,0:T(8,128)S(1)} %copy-done.2, f32[16,128,512]{2,1,0:T(8,128)S(1)} %copy-done.3, f32[16,128,512]{2,1,0:T(8,128)S(1)} %copy-done.4), custom_call_target="tpu_custom_call" | custom-call | tf_op jit(solution)/shard_map/column_sums/pallas_call | solution.py:197
  14.4 7.7 %collective-permute-start.5 = (f32[2,96,512]{2,1,0:T(8,128)S(1)}, f32[2,96,512]{2,1,0:T(8,128)S(1)}, u32[]{:S(2)}, u32[]{:S(2)}) collective-permute-start(f32[2,96,512]{2,1,0:T(8,128)S(1)} %get-tuple-element.23), channel_id=1, source_target_pairs={{0,120},{8,112},{16,104},{24,96},{32,88},{40,80},{48,72},{56,64},{... | collective-permute-start | bytes 1179656 | tf_op jit(solution)/shard_map/ppermute | solution.py:510
  22.1 0.1 collective-permute-start
  22.2 0.0 copy-done
  22.2 0.2 ion_columns.1.ion_lines
  22.3 13.0 %collective-permute-done.far = f32[2,40,640]{2,1,0:T(8,128)S(1)} collective-permute-done((f32[2,40,640]{2,1,0:T(8,128)S(1)}, f32[2,40,640]{2,1,0:T(8,128)S(1)}, u32[]{:S(2)}, u32[]{:S(2)}) %collective-permute-start) | collective-permute-done | bytes 204832 | tf_op jit(solution)/shard_map/ppermute | solution.py:509
  35.4 3.0 %collective-permute-start.1 = (f32[40,128]{1,0:T(8,128)S(1)}, f32[40,128]{1,0:T(8,128)S(1)}, u32[]{:S(2)}, u32[]{:S(2)}) collective-permute-start(f32[40,128]{1,0:T(8,128)S(1)} %get-tuple-element.17.own_left), channel_id=1, source_target_pairs={{1,0},{2,1},{3,2},{4,3},{5,4},{6,5},{7,6},{0,7},{9,8},{10,9},{11,1... | collective-permute-start | bytes 61448 | tf_op jit(solution)/shard_map/ppermute | solution.py:513
  38.4 0.0 collective-permute-start.2
  38.5 0.9 %collective-permute-done.1.from_right = f32[40,128]{1,0:T(8,128)S(1)} collective-permute-done((f32[40,128]{1,0:T(8,128)S(1)}, f32[40,128]{1,0:T(8,128)S(1)}, u32[]{:S(2)}, u32[]{:S(2)}) %collective-permute-start.1) | collective-permute-done | bytes 20512 | tf_op jit(solution)/shard_map/ppermute | solution.py:513
  39.4 3.8 %collective-permute-done.2.from_left = f32[40,128]{1,0:T(8,128)S(1)} collective-permute-done((f32[40,128]{1,0:T(8,128)S(1)}, f32[40,128]{1,0:T(8,128)S(1)}, u32[]{:S(2)}, u32[]{:S(2)}) %collective-permute-start.2) | collective-permute-done | bytes 20512 | tf_op jit(solution)/shard_map/ppermute | solution.py:514
  43.2 0.3 lat_bands.1
  43.5 3.5 %collective-permute-start.4 = (f32[40,640]{1,0:T(8,128)S(1)}, f32[40,640]{1,0:T(8,128)S(1)}, u32[]{:S(2)}, u32[]{:S(2)}) collective-permute-start(f32[40,640]{1,0:T(8,128)S(1)} %get-tuple-element.19.top), channel_id=1, source_target_pairs={{8,0},{16,8},{24,16},{32,24},{40,32},{48,40},{56,48},{64,56},{72,6... | collective-permute-start | bytes 307208 | tf_op jit(solution)/shard_map/ppermute | solution.py:519
  47.0 2.7 %collective-permute-start.3 = (f32[40,640]{1,0:T(8,128)S(1)}, f32[40,640]{1,0:T(8,128)S(1)}, u32[]{:S(2)}, u32[]{:S(2)}) collective-permute-start(f32[40,640]{1,0:T(8,128)S(1)} %get-tuple-element.20.bottom), channel_id=1, source_target_pairs={{0,8},{8,16},{16,24},{24,32},{32,40},{40,48},{48,56},{56,64},{64,7... | collective-permute-start | bytes 307208 | tf_op jit(solution)/shard_map/ppermute | solution.py:518
  49.7 0.1 pad_add_fusion.band
  49.8 0.3 collective-permute-done.4.below
  50.1 1.3 %collective-permute-done.3.above = f32[40,640]{1,0:T(8,128)S(1)} collective-permute-done((f32[40,640]{1,0:T(8,128)S(1)}, f32[40,640]{1,0:T(8,128)S(1)}, u32[]{:S(2)}, u32[]{:S(2)}) %collective-permute-start.3) | collective-permute-done | bytes 102432 | tf_op jit(solution)/shard_map/ppermute | solution.py:518
  51.4 0.0 collective-permute-done.5.far_middle
  51.4 0.0 copy-done.5
  51.4 7.2 %potential_solve.1 = (f32[128,512]{1,0:T(8,128)}, f32[128,512]{1,0:T(8,128)S(1)}, f32[128,512]{1,0:T(8,128)S(1)}, f32[128,1,128]{2,1,0:T(1,128)S(1)}) custom-call(f32[2,16]{1,0:T(2,128)S(1)} %copy-done.5, s32[2]{0:T(128)S(1)} %pad_add_fusion.band, f32[40,640]{1,0:T(8,128)S(1)} %get-tuple-element.19.top, f32[40,640]{1,0:T(8,128)S(1)} %get-tuple-element.20.bottom, ...), custom_call_target="tpu_custom_call" | custom-call | tf_op jit(solution)/shard_map/potential_solve/pallas_call | solution.py:448
  58.6 21.1 %all_to_all.5.fastest = f32[128,1,128]{2,1,0:T(1,128)S(1)} all-to-all(f32[128,1,128]{2,1,0:T(1,128)S(1)} %get-tuple-element.25), channel_id=1, replica_groups=mesh['lat'=16,'lon'=8] {'lat','lon'}, dimensions={0} | all-to-all | bytes 131072 | tf_op jit(solution)/shard_map/all_to_all | solution.py:527
  79.7 1.7 %ion_advection.1 = f32[3,128,512]{2,1,0:T(8,128)} custom-call(f32[128,1,128]{2,1,0:T(1,128)S(1)} %all_to_all.5.fastest, f32[128,512]{1,0:T(8,128)S(1)} %get-tuple-element.26.drift_east, f32[128,512]{1,0:T(8,128)S(1)} %get-tuple-element.27.drift_north, f32[3,128,512]{2,1,0:T(8,128)S(1)} %copy-done, f32[40,640]{1,0:T(8,128)S(1)} %collective-permute-done.3.above, ...), custom_call_target="tpu_custom_call" | custom-call | tf_op jit(solution)/shard_map/ion_advection/pallas_call | solution.py:53
  (1 shorter events, 0.0 us)
Async XLA Ops:
  0.6 2.2 %copy-start.1 = (f32[16,128,512]{2,1,0:T(8,128)S(1)}, f32[16,128,512]{2,1,0:T(8,128)}, u32[]{:S(2)}) copy-start(f32[16,128,512]{2,1,0:T(8,128)} %pedersen.1) | copy-start | bytes 12582916
  2.8 2.2 %copy-start.2 = (f32[16,128,512]{2,1,0:T(8,128)S(1)}, f32[16,128,512]{2,1,0:T(8,128)}, u32[]{:S(2)}) copy-start(f32[16,128,512]{2,1,0:T(8,128)} %hall.1) | copy-start | bytes 12582916
  5.0 2.2 %copy-start.3 = (f32[16,128,512]{2,1,0:T(8,128)S(1)}, f32[16,128,512]{2,1,0:T(8,128)}, u32[]{:S(2)}) copy-start(f32[16,128,512]{2,1,0:T(8,128)} %east_wind.1) | copy-start | bytes 12582916
  7.2 2.2 %copy-start.4 = (f32[16,128,512]{2,1,0:T(8,128)S(1)}, f32[16,128,512]{2,1,0:T(8,128)}, u32[]{:S(2)}) copy-start(f32[16,128,512]{2,1,0:T(8,128)} %north_wind.1) | copy-start | bytes 12582916
  9.4 12.8 %copy-start = (f32[3,128,512]{2,1,0:T(8,128)S(1)}, f32[3,128,512]{2,1,0:T(8,128)}, u32[]{:S(2)}) copy-start(f32[3,128,512]{2,1,0:T(8,128)} %ions.5) | copy-start | bytes 2359300
  9.4 42.0 %copy-start.5 = (f32[2,16]{1,0:T(2,128)S(1)}, f32[2,16]{1,0:T(2,128)}, u32[]{:S(2)}) copy-start(f32[2,16]{1,0:T(2,128)} %constant.10.clone.factors) | copy-start | bytes 388
  14.4 37.0 %collective-permute-start.5 = (f32[2,96,512]{2,1,0:T(8,128)S(1)}, f32[2,96,512]{2,1,0:T(8,128)S(1)}, u32[]{:S(2)}, u32[]{:S(2)}) collective-permute-start(f32[2,96,512]{2,1,0:T(8,128)S(1)} %get-tuple-element.23), channel_id=1, source_target_pairs={{0,120},{8,112},{16,104},{24,96},{32,88},{40,80},{48,72},{56,64},{... | collective-permute-start | bytes 1179656 | tf_op jit(solution)/shard_map/ppermute | solution.py:510
  22.1 13.3 %collective-permute-start = (f32[2,40,640]{2,1,0:T(8,128)S(1)}, f32[2,40,640]{2,1,0:T(8,128)S(1)}, u32[]{:S(2)}, u32[]{:S(2)}) collective-permute-start(f32[2,40,640]{2,1,0:T(8,128)S(1)} %get-tuple-element.16), channel_id=1, source_target_pairs={{0,120},{8,112},{16,104},{24,96},{32,88},{40,80},{48,72},{56,64},{... | collective-permute-start | bytes 614408 | tf_op jit(solution)/shard_map/ppermute | solution.py:509
  35.4 4.0 %collective-permute-start.1 = (f32[40,128]{1,0:T(8,128)S(1)}, f32[40,128]{1,0:T(8,128)S(1)}, u32[]{:S(2)}, u32[]{:S(2)}) collective-permute-start(f32[40,128]{1,0:T(8,128)S(1)} %get-tuple-element.17.own_left), channel_id=1, source_target_pairs={{1,0},{2,1},{3,2},{4,3},{5,4},{6,5},{7,6},{0,7},{9,8},{10,9},{11,1... | collective-permute-start | bytes 61448 | tf_op jit(solution)/shard_map/ppermute | solution.py:513
  38.4 4.7 %collective-permute-start.2 = (f32[40,128]{1,0:T(8,128)S(1)}, f32[40,128]{1,0:T(8,128)S(1)}, u32[]{:S(2)}, u32[]{:S(2)}) collective-permute-start(f32[40,128]{1,0:T(8,128)S(1)} %get-tuple-element.18.own_right), channel_id=1, source_target_pairs={{0,1},{1,2},{2,3},{3,4},{4,5},{5,6},{6,7},{7,0},{8,9},{9,10},{10,1... | collective-permute-start | bytes 61448 | tf_op jit(solution)/shard_map/ppermute | solution.py:514
  43.5 6.7 %collective-permute-start.4 = (f32[40,640]{1,0:T(8,128)S(1)}, f32[40,640]{1,0:T(8,128)S(1)}, u32[]{:S(2)}, u32[]{:S(2)}) collective-permute-start(f32[40,640]{1,0:T(8,128)S(1)} %get-tuple-element.19.top), channel_id=1, source_target_pairs={{8,0},{16,8},{24,16},{32,24},{40,32},{48,40},{56,48},{64,56},{72,6... | collective-permute-start | bytes 307208 | tf_op jit(solution)/shard_map/ppermute | solution.py:519
  47.0 4.4 %collective-permute-start.3 = (f32[40,640]{1,0:T(8,128)S(1)}, f32[40,640]{1,0:T(8,128)S(1)}, u32[]{:S(2)}, u32[]{:S(2)}) collective-permute-start(f32[40,640]{1,0:T(8,128)S(1)} %get-tuple-element.20.bottom), channel_id=1, source_target_pairs={{0,8},{8,16},{16,24},{24,32},{32,40},{40,48},{48,56},{56,64},{64,7... | collective-permute-start | bytes 307208 | tf_op jit(solution)/shard_map/ppermute | solution.py:518

commit v3 on v2

v3 whole, which is shorter than its diff:
```python
import functools

import jax
import jax.numpy as jnp
from jax import lax
from jax.experimental import pallas as pl
from jax.experimental.pallas import tpu as pltpu
from jax.sharding import PartitionSpec as P

LEV = 16
SWEEPS = 16
DAMPING = 0.0001
LOW_BOUND = 0.05
HIGH_BOUND = 2.0
COURANT = 0.8
MOBILITY = (1.0, 0.6, 0.3)

LANES = 128
ROWS = 128
COLS = 512
TILES = COLS // LANES
WIDE = COLS + LANES
SEND = WIDE + LANES
PART = COLS // 2
EDGE = 16
HALO = 24
MID = ROWS - 2 * EDGE
EXT = ROWS + 2 * HALO
SIGMA_PLUS = 2 * EDGE
CURRENT = SIGMA_PLUS + 1
IONS = SIGMA_PLUS + 2
NORTH = SIGMA_PLUS + 5
LINES = SIGMA_PLUS + 8
CHUNK = 16
VMEM_BYTES = 32 * 1024 * 1024
COLUMN_BYTES = 51 * 1024 * 1024


def chebyshev_factors():
    theta = 0.5 * (HIGH_BOUND + LOW_BOUND)
    delta = 0.5 * (HIGH_BOUND - LOW_BOUND)
    sigma_one = theta / delta
    rho_prev = 1.0 / sigma_one
    first_list = []
    second_list = []
    for sweep in range(SWEEPS):
        rho_next = 1.0 / (2.0 * sigma_one - rho_prev)
        first_list.append(rho_next * rho_prev)
        second_list.append(2.0 * rho_next / delta)
        rho_prev = rho_next
    return (theta, first_list, second_list)


def lane_index(rows):
    return lax.broadcasted_iota(jnp.int32, (rows, LANES), 1)


def row_index(rows, cols=LANES):
    return lax.broadcasted_iota(jnp.int32, (rows, cols), 0)


def reversed_rows(tile):
    row = row_index(8, tile.shape[1])
    tile = pltpu.roll(tile, 4, 0)
    tile = jnp.where((row & 2) == 0, pltpu.roll(tile, 6, 0), pltpu.roll(tile, 2, 0))
    return jnp.where((row & 1) == 0, pltpu.roll(tile, 7, 0), pltpu.roll(tile, 1, 0))


def shifted(tiles, to_right):
    count = len(tiles)
    lane = lane_index(tiles[0].shape[0])
    if to_right:
        turned = [pltpu.roll(tile, 1, 1) for tile in tiles]
        return [jnp.where(lane == 0, turned[t - 1], turned[t]) for t in range(count)]
    turned = [pltpu.roll(tile, LANES - 1, 1) for tile in tiles]
    return [jnp.where(lane == LANES - 1, turned[(t + 1) % count], turned[t]) for t in range(count)]


def local_source(east, north, source, start, wanted):
    rows = slice(start, start + 8)
    lane = lane_index(8)
    row = row_index(8)
    zero = jnp.zeros((8, LANES), jnp.float32)
    tiles = east.shape[1] // LANES
    for t in wanted:
        span = slice(t * LANES, (t + 1) * LANES)
        tile = east[rows, span]
        left = right = zero
        if t:
            left = pltpu.roll(east[rows, (t - 1) * LANES : t * LANES], 1, 1)
        if t < tiles - 1:
            right = pltpu.roll(east[rows, (t + 1) * LANES : (t + 2) * LANES], LANES - 1, 1)
        before = jnp.where(lane == 0, left, pltpu.roll(tile, 1, 1))
        after = jnp.where(lane == LANES - 1, right, pltpu.roll(tile, LANES - 1, 1))
        here = north[rows, span]
        above = north[start - 8 : start, span][7:8] if start else zero[:1]
        below = north[start + 8 : start + 16, span][:1] if start + 8 < ROWS else zero[:1]
        up = jnp.where(row == 0, above, pltpu.roll(here, 1, 0))
        down = jnp.where(row == 7, below, pltpu.roll(here, 7, 0))
        source[rows, span] = 0.5 * (after - before) + 0.5 * (down - up)


def put_lanes(tile, source, at, first, count):
    lane = lane_index(tile.shape[0])
    turn = (first - at) % LANES
    moved = pltpu.roll(source, turn, 1) if turn else source
    return jnp.where((lane >= first) & (lane < first + count), moved, tile)


def write_strips(sums, ions, source, strips):
    sigma, east, north = (sums.at[0], sums.at[1], sums.at[2])
    for start in range(0, ROWS, 8):
        local_source(east, north, source, start, (0, 1))
    row = row_index(8)
    for side, out in enumerate(strips):
        span = slice(side * LANES, (side + 1) * LANES)
        near = side * (LANES - EDGE)
        strip = jnp.zeros((ROWS, LANES), jnp.float32)
        strip = put_lanes(strip, sigma[:, span], near, 0, EDGE)
        strip = put_lanes(strip, source[:, span], near, EDGE, EDGE)
        strip = put_lanes(strip, sigma[:, span], LANES - EDGE - 1 if side else EDGE, SIGMA_PLUS, 1)
        strip = put_lanes(strip, east[:, span], side * (LANES - 1), CURRENT, 1)
        if ions is not None:
            for s in range(3):
                strip = put_lanes(strip, ions[s, :, span], side * (LANES - 1), IONS + s, 1)
        turned = strip.T
        out[:SIGMA_PLUS] = turned[:SIGMA_PLUS]
        tile = turned[SIGMA_PLUS:LINES]
        tile = jnp.where(row == NORTH - SIGMA_PLUS, north[0:8, span][:1], tile)
        out[SIGMA_PLUS:] = jnp.where(row == NORTH + 1 - SIGMA_PLUS, north[ROWS - 8 :, span][7:8], tile)


def sum_levels(fields, spans, held, arrived, own, far, before=()):
    steps = ROWS // CHUNK

    def copies(step):
        rows = pl.ds(pl.multiple_of(step * CHUNK, CHUNK), CHUNK)
        out = []
        for i, field in enumerate(fields):
            at = 0
            for j, (first, width) in enumerate(spans):
                source = field.at[:, rows, pl.ds(first, width)]
                target = held.at[i, :, rows, pl.ds(at, width)]
                out.append(pltpu.make_async_copy(source, target, arrived.at[i, step, j]))
                at += width
        return out

    for step in range(steps):
        for copy in copies(step):
            copy.start()
    for copy in before:
        copy.start()

    def body(step, _):
        for copy in copies(step):
            copy.wait()
        for half in range(CHUNK // 8):
            near = pl.ds(pl.multiple_of(step * CHUNK + half * 8, 8), 8)
            away = pl.ds(pl.multiple_of(ROWS - 8 - step * CHUNK - half * 8, 8), 8)
            totals = [jnp.zeros((8, PART), jnp.float32) for _ in range(3)]
            for level in range(LEV):
                layer = (0.5 + level / LEV) / LEV
                along = layer * held[0, level, near, :]
                across = layer * held[1, level, near, :]
                wind_e = held[2, level, near, :]
                wind_n = held[3, level, near, :]
                totals[0] = totals[0] + along
                totals[1] = totals[1] + (along * wind_e + across * wind_n)
                totals[2] = totals[2] + (along * wind_n - across * wind_e)
            for i, total in enumerate(totals):
                own[i, near, :] = total
                far[i, away, :] = reversed_rows(total)
        return 0

    lax.fori_loop(0, steps, body, 0)
    for copy in before:
        copy.wait()


def outer_kernel(
    pedersen, hall, east_wind, north_wind, ions,
    to_left, to_right, own, far, held, source, held_ions, arrived, ions_arrived,
):
    last = COLS - LANES
    spans = ((0, LANES), (last, LANES))
    copies = [
        pltpu.make_async_copy(
            ions.at[:, :, pl.ds(first, LANES)],
            held_ions.at[:, :, pl.ds(i * LANES, LANES)],
            ions_arrived.at[i],
        )
        for i, (first, _) in enumerate(spans)
    ]
    sum_levels((pedersen, hall, east_wind, north_wind), spans, held, arrived, own, far, copies)
    for v, (sums, lines) in enumerate(((own, held_ions), (far, None))):
        rows = pl.ds(v * LINES, LINES)
        write_strips(sums, lines, source, (to_left.at[rows], to_right.at[rows]))


def inner_kernel(pedersen, hall, east_wind, north_wind, own, far, held, arrived):
    spans = ((LANES, PART),)
    sum_levels((pedersen, hall, east_wind, north_wind), spans, held, arrived, own, far)


def level_sums(kernel, name, shapes, scratch, parts, *fields):
    sums = jax.ShapeDtypeStruct((3, ROWS, PART), jnp.float32)
    out = [jax.ShapeDtypeStruct(shape, jnp.float32) for shape in shapes] + [sums, sums]
    steps = ROWS // CHUNK
    return pl.pallas_call(
        kernel,
        in_specs=[pl.BlockSpec(memory_space=pltpu.HBM)] * len(fields),
        out_specs=[pl.BlockSpec(memory_space=pltpu.VMEM)] * len(out),
        out_shape=out,
        scratch_shapes=[pltpu.VMEM((4, LEV, ROWS, PART), jnp.float32)]
        + [pltpu.VMEM(shape, jnp.float32) for shape in scratch]
        + [pltpu.SemaphoreType.DMA((4, steps, parts))]
        + ([pltpu.SemaphoreType.DMA((2,))] if scratch else []),
        compiler_params=pltpu.CompilerParams(vmem_limit_bytes=COLUMN_BYTES),
        cost_estimate=pl.CostEstimate(flops=1 << 23, bytes_accessed=1 << 23, transcendentals=0),
        name=name,
    )(*fields)


def turned_back(strip):
    rest = jnp.zeros((LANES - LINES, LANES), jnp.float32)
    return jnp.concatenate([strip[...], rest], 0).T


def gather_columns(outer, inner, fields):
    for i, field in enumerate(fields):
        field[:, :LANES] = outer[i, :, :LANES]
        field[:, LANES : COLS - LANES] = inner[i]
        field[:, COLS - LANES :] = outer[i, :, LANES:]


def write_edges(fields, from_right, from_left, ions, source, edges, everything):
    sigma, east, north = fields
    last = COLS - LANES
    for start in range(0, ROWS, 8):
        outer = everything or start < EDGE or start >= ROWS - EDGE
        local_source(east, north, source, start, range(TILES) if outer else (0, TILES - 1))
    right, left = (turned_back(from_right), turned_back(from_left))
    blank = jnp.zeros((ROWS, LANES), jnp.float32)
    sigma_x = put_lanes(blank, right, 0, 0, EDGE)
    sigma_x = put_lanes(sigma_x, right, SIGMA_PLUS, EDGE, 1)
    sigma_x = put_lanes(sigma_x, left, 0, LANES - EDGE, EDGE)
    sigma_x = put_lanes(sigma_x, left, SIGMA_PLUS, LANES - EDGE - 1, 1)
    source_x = put_lanes(blank, right, EDGE, 0, EDGE)
    source_x = put_lanes(source_x, left, EDGE, LANES - EDGE, EDGE)
    source_x = source_x - 0.5 * put_lanes(blank, east[:, last:], LANES - 1, 0, 1)
    source_x = source_x + 0.5 * put_lanes(blank, east[:, :LANES], 0, LANES - 1, 1)
    source[:, :LANES] += put_lanes(blank, -0.5 * left, CURRENT, 0, 1)
    source[:, last:] += put_lanes(blank, 0.5 * right, CURRENT, LANES - 1, 1)

    lane = lane_index(1)
    row = row_index(8)
    wide = row_index(8, COLS)
    for side in range(2):
        first = side * (ROWS - EDGE)
        rows = slice(first, first + EDGE)
        edges[side, :EDGE, :COLS] = sigma[rows]
        edges[side, EDGE:SIGMA_PLUS, :COLS] = source[rows]
        edges[side, :EDGE, COLS:WIDE] = sigma_x[rows]
        edges[side, EDGE:SIGMA_PLUS, COLS:WIDE] = source_x[rows]
        if side == 0:
            further, line = (sigma[EDGE : EDGE + 8][:1], north[0:8][:1])
            further_x = sigma_x[EDGE : EDGE + 1]
        else:
            further, line = (sigma[first - 8 : first][7:8], north[ROWS - 8 :][7:8])
            further_x = sigma_x[first - 1 : first]
        tile = jnp.where(wide == 0, further, 0.0)
        tile = jnp.where(wide == CURRENT - SIGMA_PLUS, line, tile)
        if ions is not None:
            for s in range(3):
                line = ions[s, ROWS - 8 :][7:8] if side else ions[s, :8][:1]
                tile = jnp.where(wide == IONS - SIGMA_PLUS + s, line, tile)
        edges[side, SIGMA_PLUS:, :COLS] = tile
        line = NORTH - SIGMA_PLUS + side
        north_x = jnp.where(
            lane < LANES // 2, from_right[SIGMA_PLUS:][line:][:1], from_left[SIGMA_PLUS:][line:][:1]
        )
        tile = jnp.where(row == 0, further_x, 0.0)
        edges[side, SIGMA_PLUS:, COLS:WIDE] = jnp.where(row == CURRENT - SIGMA_PLUS, north_x, tile)
        strip = put_lanes(blank, sigma_x, side * (LANES - EDGE - 1), 0, EDGE + 1)
        strip = put_lanes(strip, source_x, side * (LANES - EDGE), EDGE + 1, EDGE)
        edges[side, :, WIDE:] = strip.T[:LINES]


def far_kernel(outer, inner, from_right, from_left, edges, sigma, east, north, source):
    fields = (sigma, east, north)
    gather_columns(outer, inner, fields)
    rows = pl.ds(LINES, LINES)
    write_edges(fields, from_right.at[rows], from_left.at[rows], None, source, edges, False)


def piece_kernel(
    outer_far, inner_far, outer, inner, from_right, from_left, ions,
    middle, own_edges, own_middle, sigma, east, north, source, spare,
):
    fields = (sigma, east, north)
    for v, sums, out in ((1, (outer_far, inner_far), middle), (0, (outer, inner), own_middle)):
        gather_columns(*sums, fields)
        rows = pl.ds(v * LINES, LINES)
        write_edges(
            fields, from_right.at[rows], from_left.at[rows], None if v else ions, source,
            spare if v else own_edges, True,
        )
        out[0] = sigma[EDGE : ROWS - EDGE]
        out[1] = source[EDGE : ROWS - EDGE]


def build(kernel, name, shapes, spare, *fields):
    whole = pl.BlockSpec(memory_space=pltpu.VMEM)
    return pl.pallas_call(
        kernel,
        in_specs=[whole] * len(fields),
        out_specs=[whole] * len(shapes),
        out_shape=[jax.ShapeDtypeStruct(shape, jnp.float32) for shape in shapes],
        scratch_shapes=[pltpu.VMEM((ROWS, COLS), jnp.float32)] * 4
        + [pltpu.VMEM(shape, jnp.float32) for shape in spare],
        compiler_params=pltpu.CompilerParams(vmem_limit_bytes=VMEM_BYTES),
        name=name,
    )(*fields)


def band_kernel(band, own, far, to_chip, to_next):
    odd = lax.rem(band[0], 2)
    to_chip[...] = own[1 - odd, :, :WIDE] + far[1 - odd, :, :WIDE]
    to_next[...] = own[odd, :, :WIDE] + far[odd, :, :WIDE]


def bands_to_send(band, *fields):
    shape = jax.ShapeDtypeStruct((LINES, WIDE), jnp.float32)
    whole = pl.BlockSpec(memory_space=pltpu.VMEM)
    return pl.pallas_call(
        band_kernel,
        in_specs=[pl.BlockSpec(memory_space=pltpu.SMEM)] + [whole] * len(fields),
        out_specs=[whole] * 2,
        out_shape=[shape, shape],
        compiler_params=pltpu.CompilerParams(vmem_limit_bytes=VMEM_BYTES),
        name="lat_bands",
    )(band, *fields)


def solve_kernel(
    factors, band, own_edges, far_edges, from_chip, from_next, own_middle, far_middle,
    potential, drift_east, drift_north, fastest,
    sigma, sigma_next, sigma_prev, half_inverse, scaled_source, update, field_a, field_b, carried_a, carried_b,
    ours, theirs,
):
    theta = 0.5 * (HIGH_BOUND + LOW_BOUND)
    fields = (field_a, field_b)
    fluxes = (carried_a, carried_b)
    odd = lax.rem(band[0], 2)
    ours[...] = own_edges[:, :, :WIDE] + far_edges[:, :, :WIDE]
    theirs[1 - odd] = from_chip[...]
    theirs[odd] = from_next[...]
    top, bottom = (ours.at[0], ours.at[1])
    above, below = (theirs.at[0], theirs.at[1])
    count = TILES + 1
    spans = [slice(t * LANES, (t + 1) * LANES) for t in range(count)]
    middle = slice(EDGE, ROWS - EDGE)
    row = row_index(8)
    low = HALO + ROWS

    blank = jnp.zeros((ROWS, LANES), jnp.float32)
    right = turned_back(own_edges[0, :, WIDE:] + far_edges[0, :, WIDE:])
    left = turned_back(own_edges[1, :, WIDE:] + far_edges[1, :, WIDE:])
    sigma_x = put_lanes(blank, right, 0, 0, EDGE + 1)
    sigma_x = put_lanes(sigma_x, left, 0, LANES - EDGE - 1, EDGE + 1)
    source_x = put_lanes(blank, right, EDGE + 1, 0, EDGE)
    source_x = put_lanes(source_x, left, EDGE + 1, LANES - EDGE, EDGE)

    for t in range(count):
        span = spans[t]
        for piece, at in ((above, HALO - EDGE), (top, HALO), (bottom, low - EDGE), (below, low)):
            sigma[t, at : at + EDGE] = piece[:EDGE, span]
            scaled_source[t, at : at + EDGE] = piece[EDGE : 2 * EDGE, span]
        outer = above[SIGMA_PLUS:, span][:1]
        sigma[t, :8] = jnp.where(row == 7, outer, 0.0)
        outer = below[SIGMA_PLUS:, span][:1]
        sigma[t, EXT - 8 :] = jnp.where(row == 0, outer, 0.0)
        inner = slice(HALO + EDGE, low - EDGE)
        if t < TILES:
            sigma[t, inner] = own_middle[0, :, span] + far_middle[0, :, span]
            source = own_middle[1, :, span] + far_middle[1, :, span]
        else:
            sigma[t, inner] = sigma_x[middle]
            source = source_x[middle]
        scaled_source[t, inner] = source
        for at, spot, piece, half in (
            (HALO - 8, 7, top, 0.5),
            (HALO, 0, above, -0.5),
            (low - 8, 7, below, 0.5),
            (low, 0, bottom, -0.5),
        ):
            line = half * piece[SIGMA_PLUS:, span][CURRENT - SIGMA_PLUS :][:1]
            tile = scaled_source[t, at : at + 8]
            scaled_source[t, at : at + 8] = tile + jnp.where(row == spot, line, 0.0)

    first_band = band[0] == 0
    last_band = band[0] == band[1] - 1
    blank = jnp.zeros((8, LANES), jnp.float32)
    for t in range(count):
        for slot in range(2):
            for at in (0, EXT - 8):
                fields[slot][t, at : at + 8] = blank
                fluxes[slot][t, at : at + 8] = blank

    for start in range(8, EXT - 8, 8):
        here = [sigma[t, start : start + 8] for t in range(count)]
        sides = [sigma[t, start - 1 : start + 7] + sigma[t, start + 1 : start + 9] for t in range(count)]
        tall = [here[t] + 0.5 * sides[t] for t in range(count)]
        left = shifted(tall, True)
        right = shifted(tall, False)
        following = shifted(here, False)
        preceding = shifted(here, True)
        outside = None
        if start < HALO:
            outside = first_band
        if start >= HALO + ROWS:
            outside = last_band
        for t in range(count):
            diagonal = 0.5 * (6.0 * here[t] + (sides[t] + (left[t] + right[t]))) + DAMPING
            inverse = 1.0 / diagonal
            if outside is not None:
                inverse = jnp.where(outside, 0.0, inverse)
            source = scaled_source[t, start : start + 8] * inverse
            initial = source * (1.0 / theta)
            sigma_next[t, start : start + 8] = following[t]
            sigma_prev[t, start : start + 8] = preceding[t]
            half_inverse[t, start : start + 8] = 0.5 * inverse
            scaled_source[t, start : start + 8] = source
            update[t, start : start + 8] = initial
            field_b[t, start : start + 8] = initial
            carried_b[t, start : start + 8] = here[t] * initial

    def sweep(k, now, later, low, high):
        field_now, carried_now = (fields[now], fluxes[now])
        field_later, carried_later = (fields[later], fluxes[later])
        keep = factors[0, k - 1]
        gain = factors[1, k - 1]
        for start in range(low, high, 8):
            rows = slice(start, start + 8)
            upper = slice(start - 1, start + 7)
            lower = slice(start + 1, start + 9)
            centre, eastward, westward = ([], [], [])
            for t in range(count):
                value = field_now[t, rows]
                flux = carried_now[t, rows]
                value_sides = field_now[t, upper] + field_now[t, lower]
                flux_sides = carried_now[t, upper] + carried_now[t, lower]
                tall = value + 0.5 * value_sides
                flux_tall = flux + 0.5 * flux_sides
                centre.append(sigma[t, rows] * value_sides + flux_sides)
                eastward.append(sigma_next[t, rows] * tall + flux_tall)
                westward.append(sigma_prev[t, rows] * tall + flux_tall)
            from_west = shifted(eastward, True)
            from_east = shifted(westward, False)
            for t in range(count):
                total = centre[t] + (from_west[t] + from_east[t])
                value = field_now[t, rows]
                residual = (scaled_source[t, rows] - value) + half_inverse[t, rows] * total
                step = keep * update[t, rows] + gain * residual
                update[t, rows] = step
                value = value + step
                field_later[t, rows] = value
                carried_later[t, rows] = sigma[t, rows] * value

    def early(pair, _):
        sweep(2 * pair + 1, 1, 0, 8, EXT - 8)
        sweep(2 * pair + 2, 0, 1, 8, EXT - 8)
        return 0

    def late(pair, _):
        sweep(2 * pair + 9, 1, 0, 16, EXT - 16)
        sweep(2 * pair + 10, 0, 1, 16, EXT - 16)
        return 0

    lax.fori_loop(0, 4, early, 0)
    lax.fori_loop(0, 3, late, 0)
    sweep(15, 1, 0, 16, EXT - 16)

    last = fields[SWEEPS % 2]
    top_speed = jnp.zeros((8, LANES), jnp.float32)
    for start in range(HALO, HALO + ROWS, 8):
        rows = slice(start, start + 8)
        out = slice(start - HALO, start - HALO + 8)
        tiles = [last[t, rows] for t in range(count)]
        west = shifted(tiles, True)
        east = shifted(tiles, False)
        for t in range(TILES):
            potential[out, spans[t]] = tiles[t]
            lift = -0.5 * (last[t, start + 1 : start + 9] - last[t, start - 1 : start + 7])
            shove = 0.5 * (east[t] - west[t])
            drift_east[out, spans[t]] = lift
            drift_north[out, spans[t]] = shove
            top_speed = jnp.maximum(top_speed, jnp.abs(lift) + jnp.abs(shove))
    peak = jnp.max(top_speed, axis=1, keepdims=True)
    peak = jnp.max(peak, axis=0, keepdims=True)
    fastest[...] = jnp.broadcast_to(peak[None], fastest.shape)


def solve(peers, factors, band, *fields):
    shapes = [(ROWS, COLS)] * 3 + [(peers, 1, LANES)]
    plane = (TILES + 1, EXT, LANES)
    memory = pltpu.VMEM(plane, jnp.float32)
    return pl.pallas_call(
        solve_kernel,
        in_specs=[pl.BlockSpec(memory_space=pltpu.SMEM)] * 2
        + [pl.BlockSpec(memory_space=pltpu.VMEM)] * len(fields),
        out_specs=[pl.BlockSpec(memory_space=pltpu.VMEM)] * 4,
        out_shape=[jax.ShapeDtypeStruct(shape, jnp.float32) for shape in shapes],
        scratch_shapes=[memory] * 10 + [pltpu.VMEM((2, LINES, WIDE), jnp.float32)] * 2,
        compiler_params=pltpu.CompilerParams(vmem_limit_bytes=VMEM_BYTES),
        name="potential_solve",
    )(factors, band, *fields)


def advect_kernel(
    band, fastest, drift_east, drift_north, ions, from_chip, from_next, from_right, from_left, out, theirs
):
    odd = lax.rem(band[0], 2)
    theirs[1 - odd] = from_chip[SIGMA_PLUS:]
    theirs[odd] = from_next[SIGMA_PLUS:]
    above, below = (theirs.at[0], theirs.at[1])
    peak = jnp.max(fastest[...], axis=0)
    peak = jnp.max(peak, axis=1, keepdims=True)
    time_step = COURANT / (peak + 1e-06)
    lane = lane_index(ROWS)
    wide = row_index(ROWS, LANES)
    beyond_right, beyond_left = (turned_back(from_right[:LINES]), turned_back(from_left[:LINES]))
    for s in range(3):
        pace = MOBILITY[s] * time_step
        tiles = [ions[s, :, t * LANES : (t + 1) * LANES] for t in range(TILES)]
        left = [pltpu.roll(tile, 1, 1) for tile in tiles]
        right = [pltpu.roll(tile, LANES - 1, 1) for tile in tiles]
        edge_right = pltpu.roll(beyond_right, LANES - 1 - IONS - s, 1)
        edge_left = pltpu.roll(beyond_left, LANES - IONS - s, 1)
        for t in range(TILES):
            span = slice(t * LANES, (t + 1) * LANES)
            density = tiles[t]
            west = jnp.where(lane == 0, left[t - 1] if t else edge_left, left[t])
            east = jnp.where(lane == LANES - 1, right[t + 1] if t < TILES - 1 else edge_right, right[t])
            behind = above[:, span][IONS - SIGMA_PLUS + s :][:1]
            ahead = below[:, span][IONS - SIGMA_PLUS + s :][:1]
            south = jnp.where(wide == 0, behind, pltpu.roll(density, 1, 0))
            north = jnp.where(wide == ROWS - 1, ahead, pltpu.roll(density, ROWS - 1, 0))
            cross_east = pace * drift_east[:, span]
            cross_north = pace * drift_north[:, span]
            result = density - jnp.maximum(cross_east, 0.0) * (density - west)
            result = result - jnp.minimum(cross_east, 0.0) * (east - density)
            result = result - jnp.maximum(cross_north, 0.0) * (density - south)
            result = result - jnp.minimum(cross_north, 0.0) * (north - density)
            out[s, :, span] = result


def advect(band, *fields):
    whole = pl.BlockSpec(memory_space=pltpu.VMEM)
    return pl.pallas_call(
        advect_kernel,
        in_specs=[pl.BlockSpec(memory_space=pltpu.SMEM)] + [whole] * len(fields),
        out_specs=whole,
        out_shape=jax.ShapeDtypeStruct((3, ROWS, COLS), jnp.float32),
        scratch_shapes=[pltpu.VMEM((2, 8, WIDE), jnp.float32)],
        compiler_params=pltpu.CompilerParams(vmem_limit_bytes=VMEM_BYTES),
        name="ion_advection",
    )(band, *fields)


def shards(pedersen, hall_conductivity, east_wind, north_wind, ion_density):
    lats = lax.axis_size("lat")
    lons = lax.axis_size("lon")
    mirror = [(i, lats - 1 - i) for i in range(lats)]
    eastward = [(i, (i + 1) % lons) for i in range(lons)]
    westward = [(j, i) for i, j in eastward]
    chip = [(i, i ^ 1) for i in range(lats)]
    beyond = [(i, i + 1 if i % 2 else i - 1) for i in range(1, lats - 1)]
    band = jnp.stack([lax.axis_index("lat").astype(jnp.int32), jnp.int32(lats)])

    levels = (pedersen, hall_conductivity, east_wind, north_wind)
    strip = (2 * LINES, LANES)
    to_left, to_right, outer, outer_far = level_sums(
        outer_kernel, "outer_sums", [strip] * 2, [(ROWS, PART), (3, ROWS, PART)], 2, *levels, ion_density
    )
    from_right = lax.ppermute(to_left, "lon", westward)
    from_left = lax.ppermute(to_right, "lon", eastward)
    inner, inner_far = level_sums(inner_kernel, "inner_sums", [], [], 1, *levels)
    (edges,) = build(
        far_kernel, "wide_edges", [(2, LINES, SEND)], [], outer_far, inner_far, from_right, from_left
    )
    far_edges = lax.ppermute(edges, "lat", mirror)
    middle, own_edges, own_middle = build(
        piece_kernel, "pieces", [(2, MID, COLS), (2, LINES, SEND), (2, MID, COLS)], [(2, LINES, SEND)],
        outer_far, inner_far, outer, inner, from_right, from_left, ion_density,
    )
    far_middle = lax.ppermute(middle, "lat", mirror)
    to_chip, to_next = bands_to_send(band, own_edges, far_edges)
    from_chip = lax.ppermute(to_chip, "lat", chip)
    from_next = lax.ppermute(to_next, "lat", beyond)

    theta, first_list, second_list = chebyshev_factors()
    factors = jnp.array([first_list, second_list], jnp.float32)
    potential, drift_east, drift_north, peaks = solve(
        lats * lons, factors, band, own_edges, far_edges, from_chip, from_next, own_middle, far_middle
    )
    peaks = lax.all_to_all(peaks, ("lat", "lon"), 0, 0, tiled=True)
    ion_update = advect(
        band, peaks, drift_east, drift_north, ion_density, from_chip, from_next, from_right, from_left
    )
    return (potential, ion_update)


def solution(mesh):
    spec = P(None, "lat", "lon")
    return jax.shard_map(
        shards,
        mesh=mesh,
        in_specs=(spec,) * 5,
        out_specs=(P("lat", "lon"), spec),
        check_vma=False,
    )
```

time: 81.7 us -> 75 us (0.918)
  local copies, waits for them, and re-layouts: 8.75 us -> 1.14 us
  Pallas kernels: 14.4 us -> 20.7 us
  waiting for transfers between devices: 19.4 us -> 17.4 us
  blocking collectives: 21.1 us -> 19.4 us
  starting transfers between devices: 17.1 us -> 15.4 us
    unnamed x12 -> x6, local copies, waits for them, and re-layouts: 8.75 us -> 1.14 us
    pallas_call x5 -> x6, Pallas kernels: 7.19 us -> 13.5 us  [the longest x2 9.17 us: level_sums(): pl.pallas_call(kernel, in_specs=[pl.BlockSpec(memory_space=pltpu.HBM)] *...]
    ppermute x2, starting transfers between devices: 6.24 us -> 2.84 us  [the longest x1 2.76 us: shards(): from_next = lax.ppermute(to_next, 'lat', beyond)]
    ppermute x1, waiting for transfers between devices: 3.83 us -> 0.99 us  [shards(): from_left = lax.ppermute(to_right, 'lon', eastward)]
    all_to_all x1, blocking collectives: 21.1 us -> 19.4 us  [shards(): peaks = lax.all_to_all(peaks, ('lat', 'lon'), 0, 0, tiled=True)]
    ppermute x2, waiting for transfers between devices: 1.58 us -> 3.21 us  [the longest x1 3.2 us: shards(): from_next = lax.ppermute(to_next, 'lat', beyond)]
    ppermute x1, starting transfers between devices: 3.04 us -> 4.56 us  [shards(): from_right = lax.ppermute(to_left, 'lon', westward)]
    ppermute x1, waiting for transfers between devices: 0.91 us -> 0.01 us  [shards(): from_right = lax.ppermute(to_left, 'lon', westward)]
  transfers between devices with their start and end apart: 6 -> 6, of which waited for: 5 -> 3; matrix products, arithmetic and copies ran while one was open for 0% -> 0% of each run, Pallas kernels for 1% -> 7%
where the time goes in v3:
time: 75 us; the launch traced here: 74.8 us
  Pallas kernels  20.7 us (28%)
  blocking collectives  19.4 us (26%)
  waiting for transfers between devices  17.4 us (23%)
  starting transfers between devices  15.4 us (21%)
  local copies, waits for them, and re-layouts  1.14 us (2%)
    all_to_all x1, blocking collectives, shards(): peaks = lax.all_to_all(peaks, ('lat', 'lon'), 0, 0, tiled=True)  19.4 us
    ppermute x1, waiting for transfers between devices, shards(): far_edges = lax.ppermute(edges, 'lat', mirror)  13.2 us
    pallas_call x2, Pallas kernels, level_sums(): pl.pallas_call(kernel, in_specs=[pl.BlockSpec(memory_space=pltpu.HBM)] *...  9.17 us
    ppermute x1, starting transfers between devices, shards(): far_middle = lax.ppermute(middle, 'lat', mirror)  7.94 us
    pallas_call x1, Pallas kernels, solve(): pl.pallas_call(solve_kernel, in_specs=[pl.BlockSpec(memory_space=pltpu.SM...  7.26 us
    ppermute x1, starting transfers between devices, shards(): from_right = lax.ppermute(to_left, 'lon', westward)  4.56 us
    ppermute x1, waiting for transfers between devices, shards(): from_next = lax.ppermute(to_next, 'lat', beyond)  3.2 us
    ppermute x1, starting transfers between devices, shards(): from_next = lax.ppermute(to_next, 'lat', beyond)  2.76 us
  transfers between devices with their start and end apart: 6, of which 3 were waited for; matrix products, arithmetic and copies ran while one was open for 0% of the time, Pallas kernels for 7%

profile of v3, /device:TPU:1, one launch (start us, length us, event | category | flops | bytes accessed | tf_op | source)
XLA Modules:
  0.0 74.8 jit_solution(11424465276303209572)
XLA Ops:
  0.6 0.0 copy-start
  0.6 1.1 %copy-done = f32[3,128,512]{2,1,0:T(8,128)S(1)} copy-done((f32[3,128,512]{2,1,0:T(8,128)S(1)}, f32[3,128,512]{2,1,0:T(8,128)}, u32[]{:S(2)}) %copy-start) | copy-done | bytes 786456
  1.8 5.2 %outer_sums.1 = (f32[80,128]{1,0:T(8,128)S(1)}, f32[80,128]{1,0:T(8,128)S(1)}, f32[3,128,256]{2,1,0:T(8,128)S(1)}, f32[3,128,256]{2,1,0:T(8,128)S(1)}) custom-call(f32[16,128,512]{2,1,0:T(8,128)} %pedersen.3, f32[16,128,512]{2,1,0:T(8,128)} %hall.3, f32[16,128,512]{2,1,0:T(8,128)} %east_wind.3, f32[16,128,512]{2,1,0:T(8,128)} %north_wind.3, ...), custom_call_target="tpu_custom_call" | custom-call | flops 8388608 | bytes 8388608 | tf_op jit(solution)/shard_map/outer_sums/pallas_call | solution.py:209
  7.0 4.6 %collective-permute-start = (f32[80,128]{1,0:T(8,128)S(1)}, f32[80,128]{1,0:T(8,128)S(1)}, u32[]{:S(2)}, u32[]{:S(2)}) collective-permute-start(f32[80,128]{1,0:T(8,128)S(1)} %get-tuple-element.21), channel_id=1, source_target_pairs={{1,0},{2,1},{3,2},{4,3},{5,4},{6,5},{7,6},{0,7},{9,8},{10,9},{11,1... | collective-permute-start | bytes 122888 | tf_op jit(solution)/shard_map/ppermute | solution.py:586
  11.6 0.0 copy-start.1
  11.6 0.0 copy-start.2
  11.6 0.0 collective-permute-start.1
  11.6 3.9 %inner_sums.1 = (f32[3,128,256]{2,1,0:T(8,128)S(1)}, f32[3,128,256]{2,1,0:T(8,128)S(1)}) custom-call(f32[16,128,512]{2,1,0:T(8,128)} %pedersen.3, f32[16,128,512]{2,1,0:T(8,128)} %hall.3, f32[16,128,512]{2,1,0:T(8,128)} %east_wind.3, f32[16,128,512]{2,1,0:T(8,128)} %north_wind.3), custom_call_target="tpu_custom_call" | custom-call | flops 8388608 | bytes 8388608 | tf_op jit(solution)/shard_map/inner_sums/pallas_call | solution.py:209
  15.5 0.0 collective-permute-done.from_right
  15.5 1.0 %collective-permute-done.1.from_left = f32[80,128]{1,0:T(8,128)S(1)} collective-permute-done((f32[80,128]{1,0:T(8,128)S(1)}, f32[80,128]{1,0:T(8,128)S(1)}, u32[]{:S(2)}, u32[]{:S(2)}) %collective-permute-start.1) | collective-permute-done | bytes 40992 | tf_op jit(solution)/shard_map/ppermute | solution.py:587
  16.5 0.0 copy-done.1
  16.5 0.9 %pieces.1 = (f32[2,96,512]{2,1,0:T(8,128)S(1)}, f32[2,40,768]{2,1,0:T(8,128)S(1)}, f32[2,96,512]{2,1,0:T(8,128)S(1)}) custom-call(f32[3,128,256]{2,1,0:T(8,128)S(1)} %get-tuple-element.17.outer_far.outer, f32[3,128,256]{2,1,0:T(8,128)S(1)} %get-tuple-element.18.inner_far.inner, f32[3,128,256]{2,1,0:T(8,128)S(1)} %get-tuple-element.19.outer, ...), custom_call_target="tpu_custom_call" | custom-call | tf_op jit(solution)/shard_map/pieces/pallas_call | solution.py:314
  17.4 7.9 %collective-permute-start.5 = (f32[2,96,512]{2,1,0:T(8,128)S(1)}, f32[2,96,512]{2,1,0:T(8,128)S(1)}, u32[]{:S(2)}, u32[]{:S(2)}) collective-permute-start(f32[2,96,512]{2,1,0:T(8,128)S(1)} %get-tuple-element.27), channel_id=1, source_target_pairs={{0,120},{8,112},{16,104},{24,96},{32,88},{40,80},{48,72},{56,64},{... | collective-permute-start | bytes 1179656 | tf_op jit(solution)/shard_map/ppermute | solution.py:597
  25.4 0.5 wide_edges.1
  25.9 0.0 collective-permute-start.2
  25.9 0.1 pad_add_fusion.band
  26.0 13.2 %collective-permute-done.2.far.far_edges = f32[2,40,768]{2,1,0:T(8,128)S(1)} collective-permute-done((f32[2,40,768]{2,1,0:T(8,128)S(1)}, f32[2,40,768]{2,1,0:T(8,128)S(1)}, u32[]{:S(2)}, u32[]{:S(2)}) %collective-permute-start.2) | collective-permute-done | bytes 245792 | tf_op jit(solution)/shard_map/ppermute | solution.py:592
  39.2 0.6 lat_bands.1
  39.8 0.1 collective-permute-start.3
  39.9 2.8 %collective-permute-start.4 = (f32[40,640]{1,0:T(8,128)S(1)}, f32[40,640]{1,0:T(8,128)S(1)}, u32[]{:S(2)}, u32[]{:S(2)}) collective-permute-start(f32[40,640]{1,0:T(8,128)S(1)} %get-tuple-element.25), channel_id=1, source_target_pairs={{8,16},{16,8},{24,32},{32,24},{40,48},{48,40},{56,64},{64,56},{72,... | collective-permute-start | bytes 307208 | tf_op jit(solution)/shard_map/ppermute | solution.py:600
  42.6 0.0 collective-permute-done.3.from_chip
  42.6 3.2 %collective-permute-done.4.from_next = f32[40,640]{1,0:T(8,128)S(1)} collective-permute-done((f32[40,640]{1,0:T(8,128)S(1)}, f32[40,640]{1,0:T(8,128)S(1)}, u32[]{:S(2)}, u32[]{:S(2)}) %collective-permute-start.4) | collective-permute-done | bytes 102432 | tf_op jit(solution)/shard_map/ppermute | solution.py:600
  45.8 0.0 collective-permute-done.5.far_middle
  45.8 0.0 copy-done.2
  45.8 7.3 %potential_solve.1 = (f32[128,512]{1,0:T(8,128)}, f32[128,512]{1,0:T(8,128)S(1)}, f32[128,512]{1,0:T(8,128)S(1)}, f32[128,1,128]{2,1,0:T(1,128)S(1)}) custom-call(f32[2,16]{1,0:T(2,128)S(1)} %copy-done.2, s32[2]{0:T(128)S(1)} %pad_add_fusion.band, f32[2,40,768]{2,1,0:T(8,128)S(1)} %get-tuple-element.23.own.own_edges, ...), custom_call_target="tpu_custom_call" | custom-call | tf_op jit(solution)/shard_map/potential_solve/pallas_call | solution.py:508
  53.1 19.4 %all_to_all.5.fastest = f32[128,1,128]{2,1,0:T(1,128)S(1)} all-to-all(f32[128,1,128]{2,1,0:T(1,128)S(1)} %get-tuple-element.29), channel_id=1, replica_groups=mesh['lat'=16,'lon'=8] {'lat','lon'}, dimensions={0} | all-to-all | bytes 131072 | tf_op jit(solution)/shard_map/all_to_all | solution.py:607
  72.5 2.3 %ion_advection.1 = f32[3,128,512]{2,1,0:T(8,128)} custom-call(s32[2]{0:T(128)S(1)} %pad_add_fusion.band, f32[128,1,128]{2,1,0:T(1,128)S(1)} %all_to_all.5.fastest, f32[128,512]{1,0:T(8,128)S(1)} %get-tuple-element.30.drift_east, f32[128,512]{1,0:T(8,128)S(1)} %get-tuple-element.31.drift_north, f32[3,128,512]{2,1,0:T(8,128)S(1)} %copy-done.1, ...), custom_call_target="tpu_custom_call" | custom-call | tf_op jit(solution)/shard_map/ion_advection/pallas_call | solution.py:560
Async XLA Ops:
  0.6 1.1 %copy-start = (f32[3,128,512]{2,1,0:T(8,128)S(1)}, f32[3,128,512]{2,1,0:T(8,128)}, u32[]{:S(2)}) copy-start(f32[3,128,512]{2,1,0:T(8,128)} %ions.5) | copy-start | bytes 2359300
  7.0 8.5 %collective-permute-start = (f32[80,128]{1,0:T(8,128)S(1)}, f32[80,128]{1,0:T(8,128)S(1)}, u32[]{:S(2)}, u32[]{:S(2)}) collective-permute-start(f32[80,128]{1,0:T(8,128)S(1)} %get-tuple-element.21), channel_id=1, source_target_pairs={{1,0},{2,1},{3,2},{4,3},{5,4},{6,5},{7,6},{0,7},{9,8},{10,9},{11,1... | collective-permute-start | bytes 122888 | tf_op jit(solution)/shard_map/ppermute | solution.py:586
  11.6 5.0 %copy-start.1 = (f32[3,128,512]{2,1,0:T(8,128)S(1)}, f32[3,128,512]{2,1,0:T(8,128)}, u32[]{:S(2)}) copy-start(f32[3,128,512]{2,1,0:T(8,128)} %ions.5) | copy-start | bytes 2359300
  11.6 34.3 %copy-start.2 = (f32[2,16]{1,0:T(2,128)S(1)}, f32[2,16]{1,0:T(2,128)}, u32[]{:S(2)}) copy-start(f32[2,16]{1,0:T(2,128)} %constant.10.clone.factors) | copy-start | bytes 388
  11.6 5.0 %collective-permute-start.1 = (f32[80,128]{1,0:T(8,128)S(1)}, f32[80,128]{1,0:T(8,128)S(1)}, u32[]{:S(2)}, u32[]{:S(2)}) collective-permute-start(f32[80,128]{1,0:T(8,128)S(1)} %get-tuple-element.22), channel_id=1, source_target_pairs={{0,1},{1,2},{2,3},{3,4},{4,5},{5,6},{6,7},{7,0},{8,9},{9,10},{10,1... | collective-permute-start | bytes 122888 | tf_op jit(solution)/shard_map/ppermute | solution.py:587
  17.4 28.4 %collective-permute-start.5 = (f32[2,96,512]{2,1,0:T(8,128)S(1)}, f32[2,96,512]{2,1,0:T(8,128)S(1)}, u32[]{:S(2)}, u32[]{:S(2)}) collective-permute-start(f32[2,96,512]{2,1,0:T(8,128)S(1)} %get-tuple-element.27), channel_id=1, source_target_pairs={{0,120},{8,112},{16,104},{24,96},{32,88},{40,80},{48,72},{56,64},{... | collective-permute-start | bytes 1179656 | tf_op jit(solution)/shard_map/ppermute | solution.py:597
  25.9 13.3 %collective-permute-start.2 = (f32[2,40,768]{2,1,0:T(8,128)S(1)}, f32[2,40,768]{2,1,0:T(8,128)S(1)}, u32[]{:S(2)}, u32[]{:S(2)}) collective-permute-start(f32[2,40,768]{2,1,0:T(8,128)S(1)} %wide_edges.1), channel_id=1, source_target_pairs={{0,120},{8,112},{16,104},{24,96},{32,88},{40,80},{48,72},{56,64},{... | collective-permute-start | bytes 737288 | tf_op jit(solution)/shard_map/ppermute | solution.py:592
  39.8 2.9 %collective-permute-start.3 = (f32[40,640]{1,0:T(8,128)S(1)}, f32[40,640]{1,0:T(8,128)S(1)}, u32[]{:S(2)}, u32[]{:S(2)}) collective-permute-start(f32[40,640]{1,0:T(8,128)S(1)} %get-tuple-element.24), channel_id=1, source_target_pairs={{0,8},{8,0},{16,24},{24,16},{32,40},{40,32},{48,56},{56,48},{64,72... | collective-permute-start | bytes 307208 | tf_op jit(solution)/shard_map/ppermute | solution.py:599
  39.9 6.0 %collective-permute-start.4 = (f32[40,640]{1,0:T(8,128)S(1)}, f32[40,640]{1,0:T(8,128)S(1)}, u32[]{:S(2)}, u32[]{:S(2)}) collective-permute-start(f32[40,640]{1,0:T(8,128)S(1)} %get-tuple-element.25), channel_id=1, source_target_pairs={{8,16},{16,8},{24,32},{32,24},{40,48},{48,40},{56,64},{64,56},{72,... | collective-permute-start | bytes 307208 | tf_op jit(solution)/shard_map/ppermute | solution.py:600

commit v4 on v3

--- a/solution.py
+++ b/solution.py
@@ -107,7 +107,7 @@
     return jnp.where((lane >= first) & (lane < first + count), moved, tile)
 
 
-def write_strips(sums, ions, source, strips):
+def write_strips(sums, source, strips):
     sigma, east, north = (sums.at[0], sums.at[1], sums.at[2])
     for start in range(0, ROWS, 8):
         local_source(east, north, source, start, (0, 1))
@@ -120,9 +120,6 @@
         strip = put_lanes(strip, source[:, span], near, EDGE, EDGE)
         strip = put_lanes(strip, sigma[:, span], LANES - EDGE - 1 if side else EDGE, SIGMA_PLUS, 1)
         strip = put_lanes(strip, east[:, span], side * (LANES - 1), CURRENT, 1)
-        if ions is not None:
-            for s in range(3):
-                strip = put_lanes(strip, ions[s, :, span], side * (LANES - 1), IONS + s, 1)
         turned = strip.T
         out[:SIGMA_PLUS] = turned[:SIGMA_PLUS]
         tile = turned[SIGMA_PLUS:LINES]
@@ -130,7 +127,7 @@
         out[SIGMA_PLUS:] = jnp.where(row == NORTH + 1 - SIGMA_PLUS, north[ROWS - 8 :, span][7:8], tile)
 
 
-def sum_levels(fields, spans, held, arrived, own, far, before=()):
+def sum_levels(fields, spans, held, arrived, own, far):
     steps = ROWS // CHUNK
 
     def copies(step):
@@ -148,8 +145,6 @@
     for step in range(steps):
         for copy in copies(step):
             copy.start()
-    for copy in before:
-        copy.start()
 
     def body(step, _):
         for copy in copies(step):
@@ -173,28 +168,29 @@
         return 0
 
     lax.fori_loop(0, steps, body, 0)
-    for copy in before:
-        copy.wait()
 
 
 def outer_kernel(
-    pedersen, hall, east_wind, north_wind, ions,
-    to_left, to_right, own, far, held, source, held_ions, arrived, ions_arrived,
+    pedersen, hall, east_wind, north_wind, to_left, to_right, own, far, held, arrived, source
 ):
-    last = COLS - LANES
-    spans = ((0, LANES), (last, LANES))
-    copies = [
-        pltpu.make_async_copy(
-            ions.at[:, :, pl.ds(first, LANES)],
-            held_ions.at[:, :, pl.ds(i * LANES, LANES)],
-            ions_arrived.at[i],
-        )
-        for i, (first, _) in enumerate(spans)
-    ]
-    sum_levels((pedersen, hall, east_wind, north_wind), spans, held, arrived, own, far, copies)
-    for v, (sums, lines) in enumerate(((own, held_ions), (far, None))):
+    spans = ((0, LANES), (COLS - LANES, LANES))
+    sum_levels((pedersen, hall, east_wind, north_wind), spans, held, arrived, own, far)
+    for v, sums in enumerate((own, far)):
         rows = pl.ds(v * LINES, LINES)
-        write_strips(sums, lines, source, (to_left.at[rows], to_right.at[rows]))
+        write_strips(sums, source, (to_left.at[rows], to_right.at[rows]))
+
+
+def ion_kernel(left, right, ions, to_left, to_right):
+    row = row_index(8)
+    for side, strip, out in ((0, left, to_left), (1, right, to_right)):
+        at = side * (COLS - LANES)
+        tile = strip[SIGMA_PLUS:LINES]
+        for s in range(3):
+            turned = ions[s, :, at : at + LANES].T
+            line = turned[LANES - 1 :] if side else turned[:1]
+            tile = jnp.where(row == IONS - SIGMA_PLUS + s, line, tile)
+        out[...] = strip[...]
+        out[SIGMA_PLUS:LINES] = tile
 
 
 def inner_kernel(pedersen, hall, east_wind, north_wind, own, far, held, arrived):
@@ -212,9 +208,8 @@
         out_specs=[pl.BlockSpec(memory_space=pltpu.VMEM)] * len(out),
         out_shape=out,
         scratch_shapes=[pltpu.VMEM((4, LEV, ROWS, PART), jnp.float32)]
-        + [pltpu.VMEM(shape, jnp.float32) for shape in scratch]
         + [pltpu.SemaphoreType.DMA((4, steps, parts))]
-        + ([pltpu.SemaphoreType.DMA((2,))] if scratch else []),
+        + [pltpu.VMEM(shape, jnp.float32) for shape in scratch],
         compiler_params=pltpu.CompilerParams(vmem_limit_bytes=COLUMN_BYTES),
         cost_estimate=pl.CostEstimate(flops=1 << 23, bytes_accessed=1 << 23, transcendentals=0),
         name=name,
@@ -295,38 +290,41 @@
 
 def piece_kernel(
     outer_far, inner_far, outer, inner, from_right, from_left, ions,
-    middle, own_edges, own_middle, sigma, east, north, source, spare,
+    far_sigma, far_source, own_edges, own_sigma, own_source, sigma, east, north, source, spare,
 ):
     fields = (sigma, east, north)
-    for v, sums, out in ((1, (outer_far, inner_far), middle), (0, (outer, inner), own_middle)):
+    for v, sums, out in (
+        (1, (outer_far, inner_far), (far_sigma, far_source)),
+        (0, (outer, inner), (own_sigma, own_source)),
+    ):
         gather_columns(*sums, fields)
         rows = pl.ds(v * LINES, LINES)
         write_edges(
             fields, from_right.at[rows], from_left.at[rows], None if v else ions, source,
             spare if v else own_edges, True,
         )
-        out[0] = sigma[EDGE : ROWS - EDGE]
-        out[1] = source[EDGE : ROWS - EDGE]
-
-
-def build(kernel, name, shapes, spare, *fields):
+        out[0][...] = sigma[EDGE : ROWS - EDGE]
+        out[1][...] = source[EDGE : ROWS - EDGE]
+
+
+def build(kernel, name, shapes, scratch, *fields):
     whole = pl.BlockSpec(memory_space=pltpu.VMEM)
     return pl.pallas_call(
         kernel,
         in_specs=[whole] * len(fields),
         out_specs=[whole] * len(shapes),
         out_shape=[jax.ShapeDtypeStruct(shape, jnp.float32) for shape in shapes],
-        scratch_shapes=[pltpu.VMEM((ROWS, COLS), jnp.float32)] * 4
-        + [pltpu.VMEM(shape, jnp.float32) for shape in spare],
+        scratch_shapes=[pltpu.VMEM(shape, jnp.float32) for shape in scratch],
         compiler_params=pltpu.CompilerParams(vmem_limit_bytes=VMEM_BYTES),
         name=name,
     )(*fields)
 
 
 def band_kernel(band, own, far, to_chip, to_next):
-    odd = lax.rem(band[0], 2)
-    to_chip[...] = own[1 - odd, :, :WIDE] + far[1 - odd, :, :WIDE]
-    to_next[...] = own[odd, :, :WIDE] + far[odd, :, :WIDE]
+    odd = lax.rem(band[0], 2) == 1
+    top, bottom = (own[side, :, :WIDE] + far[side, :, :WIDE] for side in range(2))
+    to_chip[...] = jnp.where(odd, top, bottom)
+    to_next[...] = jnp.where(odd, bottom, top)
 
 
 def bands_to_send(band, *fields):
@@ -343,7 +341,8 @@
 
 
 def solve_kernel(
-    factors, band, own_edges, far_edges, from_chip, from_next, own_middle, far_middle,
+    factors, band, own_edges, far_edges, from_chip, from_next,
+    own_sigma, own_source, far_sigma, far_source,
     potential, drift_east, drift_north, fastest,
     sigma, sigma_next, sigma_prev, half_inverse, scaled_source, update, field_a, field_b, carried_a, carried_b,
     ours, theirs,
@@ -351,10 +350,10 @@
     theta = 0.5 * (HIGH_BOUND + LOW_BOUND)
     fields = (field_a, field_b)
     fluxes = (carried_a, carried_b)
-    odd = lax.rem(band[0], 2)
+    odd = lax.rem(band[0], 2) == 1
     ours[...] = own_edges[:, :, :WIDE] + far_edges[:, :, :WIDE]
-    theirs[1 - odd] = from_chip[...]
-    theirs[odd] = from_next[...]
+    theirs[0] = jnp.where(odd, from_chip[...], from_next[...])
+    theirs[1] = jnp.where(odd, from_next[...], from_chip[...])
     top, bottom = (ours.at[0], ours.at[1])
     above, below = (theirs.at[0], theirs.at[1])
     count = TILES + 1
@@ -382,8 +381,8 @@
         sigma[t, EXT - 8 :] = jnp.where(row == 0, outer, 0.0)
         inner = slice(HALO + EDGE, low - EDGE)
         if t < TILES:
-            sigma[t, inner] = own_middle[0, :, span] + far_middle[0, :, span]
-            source = own_middle[1, :, span] + far_middle[1, :, span]
+            sigma[t, inner] = own_sigma[:, span] + far_sigma[:, span]
+            source = own_source[:, span] + far_source[:, span]
         else:
             sigma[t, inner] = sigma_x[middle]
             source = source_x[middle]
@@ -518,12 +517,11 @@
 
 
 def advect_kernel(
-    band, fastest, drift_east, drift_north, ions, from_chip, from_next, from_right, from_left, out, theirs
+    band, fastest, drift_east, drift_north, ions, from_chip, from_next, from_right, from_left, out
 ):
-    odd = lax.rem(band[0], 2)
-    theirs[1 - odd] = from_chip[SIGMA_PLUS:]
-    theirs[odd] = from_next[SIGMA_PLUS:]
-    above, below = (theirs.at[0], theirs.at[1])
+    odd = lax.rem(band[0], 2) == 1
+    above = jnp.where(odd, from_chip[SIGMA_PLUS:, :COLS], from_next[SIGMA_PLUS:, :COLS])
+    below = jnp.where(odd, from_next[SIGMA_PLUS:, :COLS], from_chip[SIGMA_PLUS:, :COLS])
     peak = jnp.max(fastest[...], axis=0)
     peak = jnp.max(peak, axis=1, keepdims=True)
     time_step = COURANT / (peak + 1e-06)
@@ -562,7 +560,6 @@
         in_specs=[pl.BlockSpec(memory_space=pltpu.SMEM)] + [whole] * len(fields),
         out_specs=whole,
         out_shape=jax.ShapeDtypeStruct((3, ROWS, COLS), jnp.float32),
-        scratch_shapes=[pltpu.VMEM((2, 8, WIDE), jnp.float32)],
         compiler_params=pltpu.CompilerParams(vmem_limit_bytes=VMEM_BYTES),
         name="ion_advection",
     )(band, *fields)
@@ -580,21 +577,26 @@
 
     levels = (pedersen, hall_conductivity, east_wind, north_wind)
     strip = (2 * LINES, LANES)
-    to_left, to_right, outer, outer_far = level_sums(
-        outer_kernel, "outer_sums", [strip] * 2, [(ROWS, PART), (3, ROWS, PART)], 2, *levels, ion_density
+    left, right, outer, outer_far = level_sums(
+        outer_kernel, "outer_sums", [strip] * 2, [(ROWS, PART)], 2, *levels
     )
+    to_left, to_right = build(ion_kernel, "lon_strips", [strip] * 2, [], left, right, ion_density)
     from_right = lax.ppermute(to_left, "lon", westward)
     from_left = lax.ppermute(to_right, "lon", eastward)
     inner, inner_far = level_sums(inner_kernel, "inner_sums", [], [], 1, *levels)
+    planes = [(ROWS, COLS)] * 4
     (edges,) = build(
-        far_kernel, "wide_edges", [(2, LINES, SEND)], [], outer_far, inner_far, from_right, from_left
+        far_kernel, "wide_edges", [(2, LINES, SEND)], planes, outer_far, inner_far, from_right, from_left
     )
     far_edges = lax.ppermute(edges, "lat", mirror)
-    middle, own_edges, own_middle = build(
-        piece_kernel, "pieces", [(2, MID, COLS), (2, LINES, SEND), (2, MID, COLS)], [(2, LINES, SEND)],
+    inner, edges = lax.optimization_barrier((inner, edges))
+    inside = (MID, COLS)
+    *middle, own_edges, own_sigma, own_source = build(
+        piece_kernel, "pieces", [inside, inside, (2, LINES, SEND), inside, inside],
+        planes + [(2, LINES, SEND)],
         outer_far, inner_far, outer, inner, from_right, from_left, ion_density,
     )
-    far_middle = lax.ppermute(middle, "lat", mirror)
+    far_middle = [lax.ppermute(part, "lat", mirror) for part in middle]
     to_chip, to_next = bands_to_send(band, own_edges, far_edges)
     from_chip = lax.ppermute(to_chip, "lat", chip)
     from_next = lax.ppermute(to_next, "lat", beyond)
@@ -602,7 +604,8 @@
     theta, first_list, second_list = chebyshev_factors()
     factors = jnp.array([first_list, second_list], jnp.float32)
     potential, drift_east, drift_north, peaks = solve(
-        lats * lons, factors, band, own_edges, far_edges, from_chip, from_next, own_middle, far_middle
+        lats * lons, factors, band, own_edges, far_edges, from_chip, from_next,
+        own_sigma, own_source, *far_middle,
     )
     peaks = lax.all_to_all(peaks, ("lat", "lon"), 0, 0, tiled=True)
     ion_update = advect(

time: 75 us -> 65.5 us (0.87)
  waiting for transfers between devices: 17.4 us -> 5.57 us
  starting transfers between devices: 15.4 us -> 20.2 us
  blocking collectives: 19.4 us -> 18 us
  local copies, waits for them, and re-layouts: 1.14 us -> 0.01 us
    ppermute x1, waiting for transfers between devices: 13.2 us -> 0.01 us  [shards(): far_edges = lax.ppermute(edges, 'lat', mirror)]
    ppermute x1, starting transfers between devices: 0.04 us -> 7.94 us  [shards(): far_edges = lax.ppermute(edges, 'lat', mirror)]
    ppermute x1 -> x2, waiting for transfers between devices: 0.01 us -> 4.52 us  [shards(): far_middle = [lax.ppermute(part, 'lat', mirror) for part in middle]]
    ppermute x1, waiting for transfers between devices: 3.2 us -> 0.01 us  [shards(): from_next = lax.ppermute(to_next, 'lat', beyond)]
    ppermute x1 -> x2, starting transfers between devices: 7.94 us -> 5.39 us  [shards(): far_middle = [lax.ppermute(part, 'lat', mirror) for part in middle]]
    all_to_all x1, blocking collectives: 19.4 us -> 18 us  [shards(): peaks = lax.all_to_all(peaks, ('lat', 'lon'), 0, 0, tiled=True)]
    unnamed x6 -> x4, local copies, waits for them, and re-layouts: 1.14 us -> 0.01 us
    pallas_call x2 -> x3, Pallas kernels: 1.41 us -> 1.57 us  [build(): pl.pallas_call(kernel, in_specs=[whole] * len(fields), out_specs=[whole]...]
  transfers between devices with their start and end apart: 6 -> 7, of which waited for: 3 -> 3; matrix products, arithmetic and copies ran while one was open for 0% -> 0% of each run, Pallas kernels for 7% -> 8%
where the time goes in v4:
time: 65.5 us; the launch traced here: 65.4 us
  Pallas kernels  20.8 us (32%)
  starting transfers between devices  20.2 us (31%)
  blocking collectives  18 us (27%)
  waiting for transfers between devices  5.57 us (9%)
  between operations  0.71 us (1%)
    all_to_all x1, blocking collectives, shards(): peaks = lax.all_to_all(peaks, ('lat', 'lon'), 0, 0, tiled=True)  18 us
    pallas_call x2, Pallas kernels, level_sums(): pl.pallas_call(kernel, in_specs=[pl.BlockSpec(memory_space=pltpu.HBM)] *...  9.08 us
    ppermute x1, starting transfers between devices, shards(): far_edges = lax.ppermute(edges, 'lat', mirror)  7.94 us
    pallas_call x1, Pallas kernels, solve(): pl.pallas_call(solve_kernel, in_specs=[pl.BlockSpec(memory_space=pltpu.SM...  7.3 us
    ppermute x2, starting transfers between devices, shards(): far_middle = [lax.ppermute(part, 'lat', mirror) for part in middle]  5.39 us
    ppermute x1, starting transfers between devices, shards(): from_right = lax.ppermute(to_left, 'lon', westward)  4.56 us
    ppermute x2, waiting for transfers between devices, shards(): far_middle = [lax.ppermute(part, 'lat', mirror) for part in middle]  4.52 us
    pallas_call x1, Pallas kernels, advect(): pl.pallas_call(advect_kernel, in_specs=[pl.BlockSpec(memory_space=pltpu.S...  2.27 us
  transfers between devices with their start and end apart: 7, of which 3 were waited for; matrix products, arithmetic and copies ran while one was open for 0% of the time, Pallas kernels for 8%

profile of v4, /device:TPU:1, one launch (start us, length us, event | category | flops | bytes accessed | tf_op | source)
XLA Modules:
  0.0 65.4 jit_solution(8818783466661011388)
XLA Ops:
  0.6 0.0 copy-start
  0.6 5.2 %outer_sums.1 = (f32[80,128]{1,0:T(8,128)S(1)}, f32[80,128]{1,0:T(8,128)S(1)}, f32[3,128,256]{2,1,0:T(8,128)S(1)}, f32[3,128,256]{2,1,0:T(8,128)S(1)}) custom-call(f32[16,128,512]{2,1,0:T(8,128)} %pedersen.3, f32[16,128,512]{2,1,0:T(8,128)} %hall.3, f32[16,128,512]{2,1,0:T(8,128)} %east_wind.3, f32[16,128,512]{2,1,0:T(8,128)} %north_wind.3), custom_call_target="tpu_custom_call" | custom-call | flops 8388608 | bytes 8388608 | tf_op jit(solution)/shard_map/outer_sums/pallas_call | solution.py:205
  5.8 0.0 copy-done
  5.8 0.2 lon_strips.1
  6.0 4.6 %collective-permute-start = (f32[80,128]{1,0:T(8,128)S(1)}, f32[80,128]{1,0:T(8,128)S(1)}, u32[]{:S(2)}, u32[]{:S(2)}) collective-permute-start(f32[80,128]{1,0:T(8,128)S(1)} %get-tuple-element.28), channel_id=1, source_target_pairs={{1,0},{2,1},{3,2},{4,3},{5,4},{6,5},{7,6},{0,7},{9,8},{10,9},{11,1... | collective-permute-start | bytes 122888 | tf_op jit(solution)/shard_map/ppermute | solution.py:584
  10.6 0.0 copy-start.1
  10.6 0.0 collective-permute-start.1
  10.6 3.9 %inner_sums.1 = (f32[3,128,256]{2,1,0:T(8,128)S(1)}, f32[3,128,256]{2,1,0:T(8,128)S(1)}) custom-call(f32[16,128,512]{2,1,0:T(8,128)} %pedersen.3, f32[16,128,512]{2,1,0:T(8,128)} %hall.3, f32[16,128,512]{2,1,0:T(8,128)} %east_wind.3, f32[16,128,512]{2,1,0:T(8,128)} %north_wind.3), custom_call_target="tpu_custom_call" | custom-call | flops 8388608 | bytes 8388608 | tf_op jit(solution)/shard_map/inner_sums/pallas_call | solution.py:205
  14.5 0.0 collective-permute-done.from_right
  14.5 1.0 %collective-permute-done.1.from_left = f32[80,128]{1,0:T(8,128)S(1)} collective-permute-done((f32[80,128]{1,0:T(8,128)S(1)}, f32[80,128]{1,0:T(8,128)S(1)}, u32[]{:S(2)}, u32[]{:S(2)}) %collective-permute-start.1) | collective-permute-done | bytes 40992 | tf_op jit(solution)/shard_map/ppermute | solution.py:585
  15.5 0.5 wide_edges.1
  16.0 7.9 %collective-permute-start.2 = (f32[2,40,768]{2,1,0:T(8,128)S(1)}, f32[2,40,768]{2,1,0:T(8,128)S(1)}, u32[]{:S(2)}, u32[]{:S(2)}) collective-permute-start(f32[2,40,768]{2,1,0:T(8,128)S(1)} %wide_edges.1), channel_id=1, source_target_pairs={{0,120},{8,112},{16,104},{24,96},{32,88},{40,80},{48,72},{56,64},{... | collective-permute-start | bytes 737288 | tf_op jit(solution)/shard_map/ppermute | solution.py:591
  24.0 0.9 %pieces.1 = (f32[96,512]{1,0:T(8,128)S(1)}, f32[96,512]{1,0:T(8,128)S(1)}, f32[2,40,768]{2,1,0:T(8,128)S(1)}, f32[96,512]{1,0:T(8,128)S(1)}, f32[96,512]{1,0:T(8,128)S(1)}) custom-call(f32[3,128,256]{2,1,0:T(8,128)S(1)} %get-tuple-element.22.outer.outer_far, f32[3,128,256]{2,1,0:T(8,128)S(1)} %get-tuple-element.23.inner.inner_far, ...), custom_call_target="tpu_custom_call" | custom-call | tf_op jit(solution)/shard_map/pieces/pallas_call | solution.py:312
  24.9 0.1 collective-permute-start.5
  24.9 5.3 %collective-permute-start.6 = (f32[96,512]{1,0:T(8,128)S(1)}, f32[96,512]{1,0:T(8,128)S(1)}, u32[]{:S(2)}, u32[]{:S(2)}) collective-permute-start(f32[96,512]{1,0:T(8,128)S(1)} %get-tuple-element.37), channel_id=1, source_target_pairs={{0,120},{8,112},{16,104},{24,96},{32,88},{40,80},{48,72},{56,64},{... | collective-permute-start | bytes 589832 | tf_op jit(solution)/shard_map/ppermute | solution.py:599
  30.3 0.1 pad_add_fusion.band
  30.4 0.0 collective-permute-done.2.far.far_edges
  30.4 0.6 lat_bands.1
  30.9 0.1 collective-permute-start.3
  31.0 2.2 %collective-permute-start.4 = (f32[40,640]{1,0:T(8,128)S(1)}, f32[40,640]{1,0:T(8,128)S(1)}, u32[]{:S(2)}, u32[]{:S(2)}) collective-permute-start(f32[40,640]{1,0:T(8,128)S(1)} %get-tuple-element.33), channel_id=1, source_target_pairs={{8,16},{16,8},{24,32},{32,24},{40,48},{48,40},{56,64},{64,56},{72,... | collective-permute-start | bytes 307208 | tf_op jit(solution)/shard_map/ppermute | solution.py:602
  33.3 2.6 %collective-permute-done.5.far_sigma = f32[96,512]{1,0:T(8,128)S(1)} collective-permute-done((f32[96,512]{1,0:T(8,128)S(1)}, f32[96,512]{1,0:T(8,128)S(1)}, u32[]{:S(2)}, u32[]{:S(2)}) %collective-permute-start.5) | collective-permute-done | bytes 196640 | tf_op jit(solution)/shard_map/ppermute | solution.py:599
  35.8 1.9 %collective-permute-done.6.far_source = f32[96,512]{1,0:T(8,128)S(1)} collective-permute-done((f32[96,512]{1,0:T(8,128)S(1)}, f32[96,512]{1,0:T(8,128)S(1)}, u32[]{:S(2)}, u32[]{:S(2)}) %collective-permute-start.6) | collective-permute-done | bytes 196640 | tf_op jit(solution)/shard_map/ppermute | solution.py:599
  37.8 0.0 collective-permute-done.3.from_chip
  37.8 0.0 collective-permute-done.4.from_next
  37.8 0.0 copy-done.1
  37.8 7.3 %potential_solve.1 = (f32[128,512]{1,0:T(8,128)}, f32[128,512]{1,0:T(8,128)S(1)}, f32[128,512]{1,0:T(8,128)S(1)}, f32[128,1,128]{2,1,0:T(1,128)S(1)}) custom-call(f32[2,16]{1,0:T(2,128)S(1)} %copy-done.1, s32[2]{0:T(128)S(1)} %pad_add_fusion.band, f32[2,40,768]{2,1,0:T(8,128)S(1)} %get-tuple-element.31.own.own_edges, ...), custom_call_target="tpu_custom_call" | custom-call | tf_op jit(solution)/shard_map/potential_solve/pallas_call | solution.py:507
  45.1 18.0 %all_to_all.5.fastest = f32[128,1,128]{2,1,0:T(1,128)S(1)} all-to-all(f32[128,1,128]{2,1,0:T(1,128)S(1)} %get-tuple-element.39), channel_id=1, replica_groups=mesh['lat'=16,'lon'=8] {'lat','lon'}, dimensions={0} | all-to-all | bytes 131072 | tf_op jit(solution)/shard_map/all_to_all | solution.py:610
  63.1 2.3 %ion_advection.1 = f32[3,128,512]{2,1,0:T(8,128)} custom-call(s32[2]{0:T(128)S(1)} %pad_add_fusion.band, f32[128,1,128]{2,1,0:T(1,128)S(1)} %all_to_all.5.fastest, f32[128,512]{1,0:T(8,128)S(1)} %get-tuple-element.40.drift_east, f32[128,512]{1,0:T(8,128)S(1)} %get-tuple-element.41.drift_north, f32[3,128,512]{2,1,0:T(8,128)S(1)} %copy-done, ...), custom_call_target="tpu_custom_call" | custom-call | tf_op jit(solution)/shard_map/ion_advection/pallas_call | solution.py:558
Async XLA Ops:
  0.6 5.2 %copy-start = (f32[3,128,512]{2,1,0:T(8,128)S(1)}, f32[3,128,512]{2,1,0:T(8,128)}, u32[]{:S(2)}) copy-start(f32[3,128,512]{2,1,0:T(8,128)} %ions.5) | copy-start | bytes 2359300
  6.0 8.5 %collective-permute-start = (f32[80,128]{1,0:T(8,128)S(1)}, f32[80,128]{1,0:T(8,128)S(1)}, u32[]{:S(2)}, u32[]{:S(2)}) collective-permute-start(f32[80,128]{1,0:T(8,128)S(1)} %get-tuple-element.28), channel_id=1, source_target_pairs={{1,0},{2,1},{3,2},{4,3},{5,4},{6,5},{7,6},{0,7},{9,8},{10,9},{11,1... | collective-permute-start | bytes 122888 | tf_op jit(solution)/shard_map/ppermute | solution.py:584
  10.6 27.2 %copy-start.1 = (f32[2,16]{1,0:T(2,128)S(1)}, f32[2,16]{1,0:T(2,128)}, u32[]{:S(2)}) copy-start(f32[2,16]{1,0:T(2,128)} %constant.10.clone.factors) | copy-start | bytes 388
  10.6 5.0 %collective-permute-start.1 = (f32[80,128]{1,0:T(8,128)S(1)}, f32[80,128]{1,0:T(8,128)S(1)}, u32[]{:S(2)}, u32[]{:S(2)}) collective-permute-start(f32[80,128]{1,0:T(8,128)S(1)} %get-tuple-element.29), channel_id=1, source_target_pairs={{0,1},{1,2},{2,3},{3,4},{4,5},{5,6},{6,7},{7,0},{8,9},{9,10},{10,1... | collective-permute-start | bytes 122888 | tf_op jit(solution)/shard_map/ppermute | solution.py:585
  16.0 14.3 %collective-permute-start.2 = (f32[2,40,768]{2,1,0:T(8,128)S(1)}, f32[2,40,768]{2,1,0:T(8,128)S(1)}, u32[]{:S(2)}, u32[]{:S(2)}) collective-permute-start(f32[2,40,768]{2,1,0:T(8,128)S(1)} %wide_edges.1), channel_id=1, source_target_pairs={{0,120},{8,112},{16,104},{24,96},{32,88},{40,80},{48,72},{56,64},{... | collective-permute-start | bytes 737288 | tf_op jit(solution)/shard_map/ppermute | solution.py:591
  24.9 10.9 %collective-permute-start.5 = (f32[96,512]{1,0:T(8,128)S(1)}, f32[96,512]{1,0:T(8,128)S(1)}, u32[]{:S(2)}, u32[]{:S(2)}) collective-permute-start(f32[96,512]{1,0:T(8,128)S(1)} %get-tuple-element.36), channel_id=1, source_target_pairs={{0,120},{8,112},{16,104},{24,96},{32,88},{40,80},{48,72},{56,64},{... | collective-permute-start | bytes 589832 | tf_op jit(solution)/shard_map/ppermute | solution.py:599
  24.9 12.8 %collective-permute-start.6 = (f32[96,512]{1,0:T(8,128)S(1)}, f32[96,512]{1,0:T(8,128)S(1)}, u32[]{:S(2)}, u32[]{:S(2)}) collective-permute-start(f32[96,512]{1,0:T(8,128)S(1)} %get-tuple-element.37), channel_id=1, source_target_pairs={{0,120},{8,112},{16,104},{24,96},{32,88},{40,80},{48,72},{56,64},{... | collective-permute-start | bytes 589832 | tf_op jit(solution)/shard_map/ppermute | solution.py:599
  30.9 6.8 %collective-permute-start.3 = (f32[40,640]{1,0:T(8,128)S(1)}, f32[40,640]{1,0:T(8,128)S(1)}, u32[]{:S(2)}, u32[]{:S(2)}) collective-permute-start(f32[40,640]{1,0:T(8,128)S(1)} %get-tuple-element.32), channel_id=1, source_target_pairs={{0,8},{8,0},{16,24},{24,16},{32,40},{40,32},{48,56},{56,48},{64,72... | collective-permute-start | bytes 307208 | tf_op jit(solution)/shard_map/ppermute | solution.py:601
  31.0 6.8 %collective-permute-start.4 = (f32[40,640]{1,0:T(8,128)S(1)}, f32[40,640]{1,0:T(8,128)S(1)}, u32[]{:S(2)}, u32[]{:S(2)}) collective-permute-start(f32[40,640]{1,0:T(8,128)S(1)} %get-tuple-element.33), channel_id=1, source_target_pairs={{8,16},{16,8},{24,32},{32,24},{40,48},{48,40},{56,64},{64,56},{72,... | collective-permute-start | bytes 307208 | tf_op jit(solution)/shard_map/ppermute | solution.py:602

commit v5 on v4

--- a/solution.py
+++ b/solution.py
@@ -31,7 +31,7 @@
 IONS = SIGMA_PLUS + 2
 NORTH = SIGMA_PLUS + 5
 LINES = SIGMA_PLUS + 8
-CHUNK = 16
+CHUNK = 32
 VMEM_BYTES = 32 * 1024 * 1024
 COLUMN_BYTES = 51 * 1024 * 1024
 
@@ -320,28 +320,15 @@
     )(*fields)
 
 
-def band_kernel(band, own, far, to_chip, to_next):
-    odd = lax.rem(band[0], 2) == 1
+def band_kernel(own, far, to_chip, to_next):
+    odd = lax.rem(lax.axis_index("lat"), 2) == 1
     top, bottom = (own[side, :, :WIDE] + far[side, :, :WIDE] for side in range(2))
     to_chip[...] = jnp.where(odd, top, bottom)
     to_next[...] = jnp.where(odd, bottom, top)
 
 
-def bands_to_send(band, *fields):
-    shape = jax.ShapeDtypeStruct((LINES, WIDE), jnp.float32)
-    whole = pl.BlockSpec(memory_space=pltpu.VMEM)
-    return pl.pallas_call(
-        band_kernel,
-        in_specs=[pl.BlockSpec(memory_space=pltpu.SMEM)] + [whole] * len(fields),
-        out_specs=[whole] * 2,
-        out_shape=[shape, shape],
-        compiler_params=pltpu.CompilerParams(vmem_limit_bytes=VMEM_BYTES),
-        name="lat_bands",
-    )(band, *fields)
-
-
 def solve_kernel(
-    factors, band, own_edges, far_edges, from_chip, from_next,
+    factors, own_edges, far_edges, from_chip, from_next,
     own_sigma, own_source, far_sigma, far_source,
     potential, drift_east, drift_north, fastest,
     sigma, sigma_next, sigma_prev, half_inverse, scaled_source, update, field_a, field_b, carried_a, carried_b,
@@ -350,7 +337,8 @@
     theta = 0.5 * (HIGH_BOUND + LOW_BOUND)
     fields = (field_a, field_b)
     fluxes = (carried_a, carried_b)
-    odd = lax.rem(band[0], 2) == 1
+    band = lax.axis_index("lat")
+    odd = lax.rem(band, 2) == 1
     ours[...] = own_edges[:, :, :WIDE] + far_edges[:, :, :WIDE]
     theirs[0] = jnp.where(odd, from_chip[...], from_next[...])
     theirs[1] = jnp.where(odd, from_next[...], from_chip[...])
@@ -397,8 +385,8 @@
             tile = scaled_source[t, at : at + 8]
             scaled_source[t, at : at + 8] = tile + jnp.where(row == spot, line, 0.0)
 
-    first_band = band[0] == 0
-    last_band = band[0] == band[1] - 1
+    first_band = band == 0
+    last_band = band == lax.axis_size("lat") - 1
     blank = jnp.zeros((8, LANES), jnp.float32)
     for t in range(count):
         for slot in range(2):
@@ -437,8 +425,8 @@
     def sweep(k, now, later, low, high):
         field_now, carried_now = (fields[now], fluxes[now])
         field_later, carried_later = (fields[later], fluxes[later])
-        keep = factors[0, k - 1]
-        gain = factors[1, k - 1]
+        keep = factors[k - 1]
+        gain = factors[SWEEPS + k - 1]
         for start in range(low, high, 8):
             rows = slice(start, start + 8)
             upper = slice(start - 1, start + 7)
@@ -500,26 +488,25 @@
     fastest[...] = jnp.broadcast_to(peak[None], fastest.shape)
 
 
-def solve(peers, factors, band, *fields):
+def solve(peers, *fields):
     shapes = [(ROWS, COLS)] * 3 + [(peers, 1, LANES)]
     plane = (TILES + 1, EXT, LANES)
     memory = pltpu.VMEM(plane, jnp.float32)
     return pl.pallas_call(
         solve_kernel,
-        in_specs=[pl.BlockSpec(memory_space=pltpu.SMEM)] * 2
-        + [pl.BlockSpec(memory_space=pltpu.VMEM)] * len(fields),
+        in_specs=[pl.BlockSpec(memory_space=pltpu.VMEM)] * len(fields),
         out_specs=[pl.BlockSpec(memory_space=pltpu.VMEM)] * 4,
         out_shape=[jax.ShapeDtypeStruct(shape, jnp.float32) for shape in shapes],
         scratch_shapes=[memory] * 10 + [pltpu.VMEM((2, LINES, WIDE), jnp.float32)] * 2,
         compiler_params=pltpu.CompilerParams(vmem_limit_bytes=VMEM_BYTES),
         name="potential_solve",
-    )(factors, band, *fields)
+    )(*fields)
 
 
 def advect_kernel(
-    band, fastest, drift_east, drift_north, ions, from_chip, from_next, from_right, from_left, out
+    fastest, drift_east, drift_north, ions, from_chip, from_next, from_right, from_left, out
 ):
-    odd = lax.rem(band[0], 2) == 1
+    odd = lax.rem(lax.axis_index("lat"), 2) == 1
     above = jnp.where(odd, from_chip[SIGMA_PLUS:, :COLS], from_next[SIGMA_PLUS:, :COLS])
     below = jnp.where(odd, from_next[SIGMA_PLUS:, :COLS], from_chip[SIGMA_PLUS:, :COLS])
     peak = jnp.max(fastest[...], axis=0)
@@ -553,18 +540,6 @@
             out[s, :, span] = result
 
 
-def advect(band, *fields):
-    whole = pl.BlockSpec(memory_space=pltpu.VMEM)
-    return pl.pallas_call(
-        advect_kernel,
-        in_specs=[pl.BlockSpec(memory_space=pltpu.SMEM)] + [whole] * len(fields),
-        out_specs=whole,
-        out_shape=jax.ShapeDtypeStruct((3, ROWS, COLS), jnp.float32),
-        compiler_params=pltpu.CompilerParams(vmem_limit_bytes=VMEM_BYTES),
-        name="ion_advection",
-    )(band, *fields)
-
-
 def shards(pedersen, hall_conductivity, east_wind, north_wind, ion_density):
     lats = lax.axis_size("lat")
     lons = lax.axis_size("lon")
@@ -573,7 +548,6 @@
     westward = [(j, i) for i, j in eastward]
     chip = [(i, i ^ 1) for i in range(lats)]
     beyond = [(i, i + 1 if i % 2 else i - 1) for i in range(1, lats - 1)]
-    band = jnp.stack([lax.axis_index("lat").astype(jnp.int32), jnp.int32(lats)])
 
     levels = (pedersen, hall_conductivity, east_wind, north_wind)
     strip = (2 * LINES, LANES)
@@ -597,19 +571,21 @@
         outer_far, inner_far, outer, inner, from_right, from_left, ion_density,
     )
     far_middle = [lax.ppermute(part, "lat", mirror) for part in middle]
-    to_chip, to_next = bands_to_send(band, own_edges, far_edges)
+    to_chip, to_next = build(band_kernel, "lat_bands", [(LINES, WIDE)] * 2, [], own_edges, far_edges)
     from_chip = lax.ppermute(to_chip, "lat", chip)
     from_next = lax.ppermute(to_next, "lat", beyond)
 
     theta, first_list, second_list = chebyshev_factors()
-    factors = jnp.array([first_list, second_list], jnp.float32)
+    factors = jnp.array(first_list + second_list, jnp.float32)
+    factors = jnp.broadcast_to(factors[:, None, None], (2 * SWEEPS, 8, LANES))
     potential, drift_east, drift_north, peaks = solve(
-        lats * lons, factors, band, own_edges, far_edges, from_chip, from_next,
+        lats * lons, factors, own_edges, far_edges, from_chip, from_next,
         own_sigma, own_source, *far_middle,
     )
     peaks = lax.all_to_all(peaks, ("lat", "lon"), 0, 0, tiled=True)
-    ion_update = advect(
-        band, peaks, drift_east, drift_north, ion_density, from_chip, from_next, from_right, from_left
+    (ion_update,) = build(
+        advect_kernel, "ion_advection", [(3, ROWS, COLS)], [],
+        peaks, drift_east, drift_north, ion_density, from_chip, from_next, from_right, from_left,
     )
     return (potential, ion_update)
 

time: 65.5 us -> 63.8 us (0.974)
  Pallas kernels: 20.8 us -> 19 us
    pallas_call x3 -> x1, Pallas kernels: 10.1 us -> 6.76 us  [solve(): pl.pallas_call(solve_kernel, in_specs=[pl.BlockSpec(memory_space=pltpu.VM...]
    pallas_call x3 -> x5, Pallas kernels: 1.57 us -> 3.36 us  [build(): pl.pallas_call(kernel, in_specs=[whole] * len(fields), out_specs=[whole]...]
where the time goes in v5:
time: 63.8 us; the launch traced here: 63.7 us
  starting transfers between devices  20.3 us (32%)
  Pallas kernels  19 us (30%)
  blocking collectives  17.5 us (27%)
  waiting for transfers between devices  6.1 us (10%)
  between operations  0.72 us (1%)
    all_to_all x1, blocking collectives, shards(): peaks = lax.all_to_all(peaks, ('lat', 'lon'), 0, 0, tiled=True)  17.5 us
    pallas_call x2, Pallas kernels, level_sums(): pl.pallas_call(kernel, in_specs=[pl.BlockSpec(memory_space=pltpu.HBM)] *...  8.84 us
    ppermute x1, starting transfers between devices, shards(): far_edges = lax.ppermute(edges, 'lat', mirror)  7.94 us
    pallas_call x1, Pallas kernels, solve(): pl.pallas_call(solve_kernel, in_specs=[pl.BlockSpec(memory_space=pltpu.VM...  6.76 us
    ppermute x2, starting transfers between devices, shards(): far_middle = [lax.ppermute(part, 'lat', mirror) for part in middle]  5.39 us
    ppermute x2, waiting for transfers between devices, shards(): far_middle = [lax.ppermute(part, 'lat', mirror) for part in middle]  5.06 us
    ppermute x1, starting transfers between devices, shards(): from_right = lax.ppermute(to_left, 'lon', westward)  4.56 us
    pallas_call x5, Pallas kernels, build(): pl.pallas_call(kernel, in_specs=[whole] * len(fields), out_specs=[whole]...  3.36 us
  transfers between devices with their start and end apart: 7, of which 3 were waited for; matrix products, arithmetic and copies ran while one was open for 0% of the time, Pallas kernels for 8%

profile of v5, /device:TPU:1, one launch (start us, length us, event | category | flops | bytes accessed | tf_op | source)
XLA Modules:
  0.0 63.7 jit_solution(14181249870412946777)
XLA Ops:
  0.6 0.0 copy-start
  0.6 4.9 %outer_sums.1 = (f32[80,128]{1,0:T(8,128)S(1)}, f32[80,128]{1,0:T(8,128)S(1)}, f32[3,128,256]{2,1,0:T(8,128)S(1)}, f32[3,128,256]{2,1,0:T(8,128)S(1)}) custom-call(f32[16,128,512]{2,1,0:T(8,128)} %pedersen.3, f32[16,128,512]{2,1,0:T(8,128)} %hall.3, f32[16,128,512]{2,1,0:T(8,128)} %east_wind.3, f32[16,128,512]{2,1,0:T(8,128)} %north_wind.3), custom_call_target="tpu_custom_call" | custom-call | flops 8388608 | bytes 8388608 | tf_op jit(solution)/shard_map/outer_sums/pallas_call | solution.py:205
  5.6 0.0 copy-done
  5.6 0.2 lon_strips.1
  5.8 4.6 %collective-permute-start = (f32[80,128]{1,0:T(8,128)S(1)}, f32[80,128]{1,0:T(8,128)S(1)}, u32[]{:S(2)}, u32[]{:S(2)}) collective-permute-start(f32[80,128]{1,0:T(8,128)S(1)} %get-tuple-element.28), channel_id=1, source_target_pairs={{1,0},{2,1},{3,2},{4,3},{5,4},{6,5},{7,6},{0,7},{9,8},{10,9},{11,1... | collective-permute-start | bytes 122888 | tf_op jit(solution)/shard_map/ppermute | solution.py:558
  10.3 0.0 copy-start.1
  10.3 0.0 collective-permute-start.1
  10.3 3.9 %inner_sums.1 = (f32[3,128,256]{2,1,0:T(8,128)S(1)}, f32[3,128,256]{2,1,0:T(8,128)S(1)}) custom-call(f32[16,128,512]{2,1,0:T(8,128)} %pedersen.3, f32[16,128,512]{2,1,0:T(8,128)} %hall.3, f32[16,128,512]{2,1,0:T(8,128)} %east_wind.3, f32[16,128,512]{2,1,0:T(8,128)} %north_wind.3), custom_call_target="tpu_custom_call" | custom-call | flops 8388608 | bytes 8388608 | tf_op jit(solution)/shard_map/inner_sums/pallas_call | solution.py:205
  14.2 0.0 collective-permute-done.from_right
  14.3 1.0 %collective-permute-done.1.from_left = f32[80,128]{1,0:T(8,128)S(1)} collective-permute-done((f32[80,128]{1,0:T(8,128)S(1)}, f32[80,128]{1,0:T(8,128)S(1)}, u32[]{:S(2)}, u32[]{:S(2)}) %collective-permute-start.1) | collective-permute-done | bytes 40992 | tf_op jit(solution)/shard_map/ppermute | solution.py:559
  15.3 0.5 wide_edges.1
  15.8 7.9 %collective-permute-start.2 = (f32[2,40,768]{2,1,0:T(8,128)S(1)}, f32[2,40,768]{2,1,0:T(8,128)S(1)}, u32[]{:S(2)}, u32[]{:S(2)}) collective-permute-start(f32[2,40,768]{2,1,0:T(8,128)S(1)} %wide_edges.1), channel_id=1, source_target_pairs={{0,120},{8,112},{16,104},{24,96},{32,88},{40,80},{48,72},{56,64},{... | collective-permute-start | bytes 737288 | tf_op jit(solution)/shard_map/ppermute | solution.py:565
  23.7 0.9 %pieces.1 = (f32[96,512]{1,0:T(8,128)S(1)}, f32[96,512]{1,0:T(8,128)S(1)}, f32[2,40,768]{2,1,0:T(8,128)S(1)}, f32[96,512]{1,0:T(8,128)S(1)}, f32[96,512]{1,0:T(8,128)S(1)}) custom-call(f32[3,128,256]{2,1,0:T(8,128)S(1)} %get-tuple-element.22.outer.outer_far, f32[3,128,256]{2,1,0:T(8,128)S(1)} %get-tuple-element.23.inner.inner_far, ...), custom_call_target="tpu_custom_call" | custom-call | tf_op jit(solution)/shard_map/pieces/pallas_call | solution.py:312
  24.6 0.0 collective-permute-start.5
  24.7 5.3 %collective-permute-start.6 = (f32[96,512]{1,0:T(8,128)S(1)}, f32[96,512]{1,0:T(8,128)S(1)}, u32[]{:S(2)}, u32[]{:S(2)}) collective-permute-start(f32[96,512]{1,0:T(8,128)S(1)} %get-tuple-element.37), channel_id=1, source_target_pairs={{0,120},{8,112},{16,104},{24,96},{32,88},{40,80},{48,72},{56,64},{... | collective-permute-start | bytes 589832 | tf_op jit(solution)/shard_map/ppermute | solution.py:573
  30.0 0.0 collective-permute-done.2.far.far_edges
  30.1 0.1 collective-permute-start.3
  30.2 2.3 %collective-permute-start.4 = (f32[40,640]{1,0:T(8,128)S(1)}, f32[40,640]{1,0:T(8,128)S(1)}, u32[]{:S(2)}, u32[]{:S(2)}) collective-permute-start(f32[40,640]{1,0:T(8,128)S(1)} %get-tuple-element.33), channel_id=1, source_target_pairs={{8,16},{16,8},{24,32},{32,24},{40,48},{48,40},{56,64},{64,56},{72,... | collective-permute-start | bytes 307208 | tf_op jit(solution)/shard_map/ppermute | solution.py:576
  32.5 3.1 %collective-permute-done.5.far_sigma = f32[96,512]{1,0:T(8,128)S(1)} collective-permute-done((f32[96,512]{1,0:T(8,128)S(1)}, f32[96,512]{1,0:T(8,128)S(1)}, u32[]{:S(2)}, u32[]{:S(2)}) %collective-permute-start.5) | collective-permute-done | bytes 196640 | tf_op jit(solution)/shard_map/ppermute | solution.py:573
  35.6 1.9 %collective-permute-done.6.far_source = f32[96,512]{1,0:T(8,128)S(1)} collective-permute-done((f32[96,512]{1,0:T(8,128)S(1)}, f32[96,512]{1,0:T(8,128)S(1)}, u32[]{:S(2)}, u32[]{:S(2)}) %collective-permute-start.6) | collective-permute-done | bytes 196640 | tf_op jit(solution)/shard_map/ppermute | solution.py:573
  37.5 0.0 collective-permute-done.3.from_chip
  37.5 0.0 collective-permute-done.4.from_next
  37.5 0.0 copy-done.1
  37.5 0.1 broadcast_in_dim.2.factors
  37.6 6.8 %potential_solve.1 = (f32[128,512]{1,0:T(8,128)}, f32[128,512]{1,0:T(8,128)S(1)}, f32[128,512]{1,0:T(8,128)S(1)}, f32[128,1,128]{2,1,0:T(1,128)S(1)}) custom-call(f32[32,8,128]{2,1,0:T(8,128)S(1)} %broadcast_in_dim.2.factors, f32[2,40,768]{2,1,0:T(8,128)S(1)} %get-tuple-element.31.own.own_edges, f32[2,40,768]{2,1,0:T(8,128)S(1)} %collective-permute-done.2.far.far_edges, ...), custom_call_target="tpu_custom_call" | custom-call | tf_op jit(solution)/shard_map/potential_solve/pallas_call | solution.py:495
  44.4 17.5 %all_to_all.5.fastest = f32[128,1,128]{2,1,0:T(1,128)S(1)} all-to-all(f32[128,1,128]{2,1,0:T(1,128)S(1)} %get-tuple-element.39), channel_id=1, replica_groups=mesh['lat'=16,'lon'=8] {'lat','lon'}, dimensions={0} | all-to-all | bytes 131072 | tf_op jit(solution)/shard_map/all_to_all | solution.py:585
  61.9 1.8 %ion_advection.1 = f32[3,128,512]{2,1,0:T(8,128)} custom-call(f32[128,1,128]{2,1,0:T(1,128)S(1)} %all_to_all.5.fastest, f32[128,512]{1,0:T(8,128)S(1)} %get-tuple-element.40.drift_east, f32[128,512]{1,0:T(8,128)S(1)} %get-tuple-element.41.drift_north, f32[3,128,512]{2,1,0:T(8,128)S(1)} %copy-done, f32[40,640]{1,0:T(8,128)S(1)} %collective-permute-done.3.from_chip, ...), custom_call_target="tpu_custom_call" | custom-call | tf_op jit(solution)/shard_map/ion_advection/pallas_call | solution.py:312
  (1 shorter events, 0.0 us)
Async XLA Ops:
  0.6 5.0 %copy-start = (f32[3,128,512]{2,1,0:T(8,128)S(1)}, f32[3,128,512]{2,1,0:T(8,128)}, u32[]{:S(2)}) copy-start(f32[3,128,512]{2,1,0:T(8,128)} %ions.5) | copy-start | bytes 2359300
  5.8 8.5 %collective-permute-start = (f32[80,128]{1,0:T(8,128)S(1)}, f32[80,128]{1,0:T(8,128)S(1)}, u32[]{:S(2)}, u32[]{:S(2)}) collective-permute-start(f32[80,128]{1,0:T(8,128)S(1)} %get-tuple-element.28), channel_id=1, source_target_pairs={{1,0},{2,1},{3,2},{4,3},{5,4},{6,5},{7,6},{0,7},{9,8},{10,9},{11,1... | collective-permute-start | bytes 122888 | tf_op jit(solution)/shard_map/ppermute | solution.py:558
  10.3 27.2 %copy-start.1 = (f32[32]{0:T(128)S(1)}, f32[32]{0:T(128)}, u32[]{:S(2)}) copy-start(f32[32]{0:T(128)} %constant.2.clone) | copy-start | bytes 388
  10.3 5.0 %collective-permute-start.1 = (f32[80,128]{1,0:T(8,128)S(1)}, f32[80,128]{1,0:T(8,128)S(1)}, u32[]{:S(2)}, u32[]{:S(2)}) collective-permute-start(f32[80,128]{1,0:T(8,128)S(1)} %get-tuple-element.29), channel_id=1, source_target_pairs={{0,1},{1,2},{2,3},{3,4},{4,5},{5,6},{6,7},{7,0},{8,9},{9,10},{10,1... | collective-permute-start | bytes 122888 | tf_op jit(solution)/shard_map/ppermute | solution.py:559
  15.8 14.2 %collective-permute-start.2 = (f32[2,40,768]{2,1,0:T(8,128)S(1)}, f32[2,40,768]{2,1,0:T(8,128)S(1)}, u32[]{:S(2)}, u32[]{:S(2)}) collective-permute-start(f32[2,40,768]{2,1,0:T(8,128)S(1)} %wide_edges.1), channel_id=1, source_target_pairs={{0,120},{8,112},{16,104},{24,96},{32,88},{40,80},{48,72},{56,64},{... | collective-permute-start | bytes 737288 | tf_op jit(solution)/shard_map/ppermute | solution.py:565
  24.6 10.9 %collective-permute-start.5 = (f32[96,512]{1,0:T(8,128)S(1)}, f32[96,512]{1,0:T(8,128)S(1)}, u32[]{:S(2)}, u32[]{:S(2)}) collective-permute-start(f32[96,512]{1,0:T(8,128)S(1)} %get-tuple-element.36), channel_id=1, source_target_pairs={{0,120},{8,112},{16,104},{24,96},{32,88},{40,80},{48,72},{56,64},{... | collective-permute-start | bytes 589832 | tf_op jit(solution)/shard_map/ppermute | solution.py:573
  24.7 12.8 %collective-permute-start.6 = (f32[96,512]{1,0:T(8,128)S(1)}, f32[96,512]{1,0:T(8,128)S(1)}, u32[]{:S(2)}, u32[]{:S(2)}) collective-permute-start(f32[96,512]{1,0:T(8,128)S(1)} %get-tuple-element.37), channel_id=1, source_target_pairs={{0,120},{8,112},{16,104},{24,96},{32,88},{40,80},{48,72},{56,64},{... | collective-permute-start | bytes 589832 | tf_op jit(solution)/shard_map/ppermute | solution.py:573
  30.1 7.5 %collective-permute-start.3 = (f32[40,640]{1,0:T(8,128)S(1)}, f32[40,640]{1,0:T(8,128)S(1)}, u32[]{:S(2)}, u32[]{:S(2)}) collective-permute-start(f32[40,640]{1,0:T(8,128)S(1)} %get-tuple-element.32), channel_id=1, source_target_pairs={{0,8},{8,0},{16,24},{24,16},{32,40},{40,32},{48,56},{56,48},{64,72... | collective-permute-start | bytes 307208 | tf_op jit(solution)/shard_map/ppermute | solution.py:575
  30.2 7.4 %collective-permute-start.4 = (f32[40,640]{1,0:T(8,128)S(1)}, f32[40,640]{1,0:T(8,128)S(1)}, u32[]{:S(2)}, u32[]{:S(2)}) collective-permute-start(f32[40,640]{1,0:T(8,128)S(1)} %get-tuple-element.33), channel_id=1, source_target_pairs={{8,16},{16,8},{24,32},{32,24},{40,48},{48,40},{56,64},{64,56},{72,... | collective-permute-start | bytes 307208 | tf_op jit(solution)/shard_map/ppermute | solution.py:576

commit v6 on v5

--- a/solution.py
+++ b/solution.py
@@ -504,7 +504,7 @@
 
 
 def advect_kernel(
-    fastest, drift_east, drift_north, ions, from_chip, from_next, from_right, from_left, out
+    fastest, drift_east, drift_north, ions, from_chip, from_next, from_right, from_left, out, made, sent
 ):
     odd = lax.rem(lax.axis_index("lat"), 2) == 1
     above = jnp.where(odd, from_chip[SIGMA_PLUS:, :COLS], from_next[SIGMA_PLUS:, :COLS])
@@ -512,32 +512,54 @@
     peak = jnp.max(fastest[...], axis=0)
     peak = jnp.max(peak, axis=1, keepdims=True)
     time_step = COURANT / (peak + 1e-06)
-    lane = lane_index(ROWS)
-    wide = row_index(ROWS, LANES)
+    lane = lane_index(8)
+    row = row_index(8)
     beyond_right, beyond_left = (turned_back(from_right[:LINES]), turned_back(from_left[:LINES]))
+    copies = []
     for s in range(3):
-        pace = MOBILITY[s] * time_step
-        tiles = [ions[s, :, t * LANES : (t + 1) * LANES] for t in range(TILES)]
-        left = [pltpu.roll(tile, 1, 1) for tile in tiles]
-        right = [pltpu.roll(tile, LANES - 1, 1) for tile in tiles]
+        pace = jnp.broadcast_to(MOBILITY[s] * time_step, (8, LANES))
         edge_right = pltpu.roll(beyond_right, LANES - 1 - IONS - s, 1)
         edge_left = pltpu.roll(beyond_left, LANES - IONS - s, 1)
-        for t in range(TILES):
-            span = slice(t * LANES, (t + 1) * LANES)
-            density = tiles[t]
-            west = jnp.where(lane == 0, left[t - 1] if t else edge_left, left[t])
-            east = jnp.where(lane == LANES - 1, right[t + 1] if t < TILES - 1 else edge_right, right[t])
-            behind = above[:, span][IONS - SIGMA_PLUS + s :][:1]
-            ahead = below[:, span][IONS - SIGMA_PLUS + s :][:1]
-            south = jnp.where(wide == 0, behind, pltpu.roll(density, 1, 0))
-            north = jnp.where(wide == ROWS - 1, ahead, pltpu.roll(density, ROWS - 1, 0))
-            cross_east = pace * drift_east[:, span]
-            cross_north = pace * drift_north[:, span]
-            result = density - jnp.maximum(cross_east, 0.0) * (density - west)
-            result = result - jnp.minimum(cross_east, 0.0) * (east - density)
-            result = result - jnp.maximum(cross_north, 0.0) * (density - south)
-            result = result - jnp.minimum(cross_north, 0.0) * (north - density)
-            out[s, :, span] = result
+        line = slice(IONS - SIGMA_PLUS + s, IONS - SIGMA_PLUS + s + 1)
+        for start in range(0, ROWS, 8):
+            rows = slice(start, start + 8)
+            tiles = [ions[s, rows, t * LANES : (t + 1) * LANES] for t in range(TILES)]
+            left = [edge_left[rows]] + [pltpu.roll(tile, 1, 1) for tile in tiles]
+            right = [pltpu.roll(tile, LANES - 1, 1) for tile in tiles] + [edge_right[rows]]
+            for t in range(TILES):
+                span = slice(t * LANES, (t + 1) * LANES)
+                density = tiles[t]
+                west = jnp.where(lane == 0, left[t], left[t + 1])
+                east = jnp.where(lane == LANES - 1, right[t + 1], right[t])
+                behind = ions[s, start - 8 : start, span][7:8] if start else above[line, span]
+                ahead = below[line, span]
+                if start + 8 < ROWS:
+                    ahead = ions[s, start + 8 : start + 16, span][:1]
+                south = jnp.where(row == 0, behind, pltpu.roll(density, 1, 0))
+                north = jnp.where(row == 7, ahead, pltpu.roll(density, 7, 0))
+                cross_east = pace * drift_east[rows, span]
+                cross_north = pace * drift_north[rows, span]
+                result = density - jnp.maximum(cross_east, 0.0) * (density - west)
+                result = result - jnp.minimum(cross_east, 0.0) * (east - density)
+                result = result - jnp.maximum(cross_north, 0.0) * (density - south)
+                result = result - jnp.minimum(cross_north, 0.0) * (north - density)
+                made[s, rows, span] = result
+        copies.append(pltpu.make_async_copy(made.at[s], out.at[s], sent.at[s]))
+        copies[s].start()
+    for copy in copies:
+        copy.wait()
+
+
+def advect(*fields):
+    return pl.pallas_call(
+        advect_kernel,
+        in_specs=[pl.BlockSpec(memory_space=pltpu.VMEM)] * len(fields),
+        out_specs=pl.BlockSpec(memory_space=pltpu.HBM),
+        out_shape=jax.ShapeDtypeStruct((3, ROWS, COLS), jnp.float32),
+        scratch_shapes=[pltpu.VMEM((3, ROWS, COLS), jnp.float32), pltpu.SemaphoreType.DMA((3,))],
+        compiler_params=pltpu.CompilerParams(vmem_limit_bytes=VMEM_BYTES),
+        name="ion_advection",
+    )(*fields)
 
 
 def shards(pedersen, hall_conductivity, east_wind, north_wind, ion_density):
@@ -583,9 +605,8 @@
         own_sigma, own_source, *far_middle,
     )
     peaks = lax.all_to_all(peaks, ("lat", "lon"), 0, 0, tiled=True)
-    (ion_update,) = build(
-        advect_kernel, "ion_advection", [(3, ROWS, COLS)], [],
-        peaks, drift_east, drift_north, ion_density, from_chip, from_next, from_right, from_left,
+    ion_update = advect(
+        peaks, drift_east, drift_north, ion_density, from_chip, from_next, from_right, from_left
     )
     return (potential, ion_update)
 

time: 63.8 us -> 63.6 us (level)
    pallas_call x5 -> x4, Pallas kernels: 3.36 us -> 1.6 us  [build(): pl.pallas_call(kernel, in_specs=[whole] * len(fields), out_specs=[whole]...]
    pallas_call x0 -> x1, Pallas kernels: none -> 1.51 us  [advect(): pl.pallas_call(advect_kernel, in_specs=[pl.BlockSpec(memory_space=pltpu.V...]
where the time goes in v6:
time: 63.6 us; the launch traced here: 63.4 us
  starting transfers between devices  20.3 us (32%)
  Pallas kernels  18.7 us (29%)
  blocking collectives  17.5 us (28%)
  waiting for transfers between devices  6.1 us (10%)
  between operations  0.72 us (1%)
    all_to_all x1, blocking collectives, shards(): peaks = lax.all_to_all(peaks, ('lat', 'lon'), 0, 0, tiled=True)  17.5 us
    pallas_call x2, Pallas kernels, level_sums(): pl.pallas_call(kernel, in_specs=[pl.BlockSpec(memory_space=pltpu.HBM)] *...  8.84 us
    ppermute x1, starting transfers between devices, shards(): far_edges = lax.ppermute(edges, 'lat', mirror)  7.94 us
    pallas_call x1, Pallas kernels, solve(): pl.pallas_call(solve_kernel, in_specs=[pl.BlockSpec(memory_space=pltpu.VM...  6.76 us
    ppermute x2, starting transfers between devices, shards(): far_middle = [lax.ppermute(part, 'lat', mirror) for part in middle]  5.39 us
    ppermute x2, waiting for transfers between devices, shards(): far_middle = [lax.ppermute(part, 'lat', mirror) for part in middle]  5.06 us
    ppermute x1, starting transfers between devices, shards(): from_right = lax.ppermute(to_left, 'lon', westward)  4.56 us
    ppermute x1, starting transfers between devices, shards(): from_next = lax.ppermute(to_next, 'lat', beyond)  2.3 us
  transfers between devices with their start and end apart: 7, of which 3 were waited for; matrix products, arithmetic and copies ran while one was open for 0% of the time, Pallas kernels for 8%

profile of v6, /device:TPU:1, one launch (start us, length us, event | category | flops | bytes accessed | tf_op | source)
XLA Modules:
  0.0 63.4 jit_solution(5402773583080802000)
XLA Ops:
  0.6 0.0 copy-start
  0.6 4.9 %outer_sums.1 = (f32[80,128]{1,0:T(8,128)S(1)}, f32[80,128]{1,0:T(8,128)S(1)}, f32[3,128,256]{2,1,0:T(8,128)S(1)}, f32[3,128,256]{2,1,0:T(8,128)S(1)}) custom-call(f32[16,128,512]{2,1,0:T(8,128)} %pedersen.3, f32[16,128,512]{2,1,0:T(8,128)} %hall.3, f32[16,128,512]{2,1,0:T(8,128)} %east_wind.3, f32[16,128,512]{2,1,0:T(8,128)} %north_wind.3), custom_call_target="tpu_custom_call" | custom-call | flops 8388608 | bytes 8388608 | tf_op jit(solution)/shard_map/outer_sums/pallas_call | solution.py:205
  5.6 0.0 copy-done
  5.6 0.2 lon_strips.1
  5.8 4.6 %collective-permute-start = (f32[80,128]{1,0:T(8,128)S(1)}, f32[80,128]{1,0:T(8,128)S(1)}, u32[]{:S(2)}, u32[]{:S(2)}) collective-permute-start(f32[80,128]{1,0:T(8,128)S(1)} %get-tuple-element.28), channel_id=1, source_target_pairs={{1,0},{2,1},{3,2},{4,3},{5,4},{6,5},{7,6},{0,7},{9,8},{10,9},{11,1... | collective-permute-start | bytes 122888 | tf_op jit(solution)/shard_map/ppermute | solution.py:580
  10.3 0.0 copy-start.1
  10.3 0.0 collective-permute-start.1
  10.3 3.9 %inner_sums.1 = (f32[3,128,256]{2,1,0:T(8,128)S(1)}, f32[3,128,256]{2,1,0:T(8,128)S(1)}) custom-call(f32[16,128,512]{2,1,0:T(8,128)} %pedersen.3, f32[16,128,512]{2,1,0:T(8,128)} %hall.3, f32[16,128,512]{2,1,0:T(8,128)} %east_wind.3, f32[16,128,512]{2,1,0:T(8,128)} %north_wind.3), custom_call_target="tpu_custom_call" | custom-call | flops 8388608 | bytes 8388608 | tf_op jit(solution)/shard_map/inner_sums/pallas_call | solution.py:205
  14.2 0.0 collective-permute-done.from_right
  14.3 1.0 %collective-permute-done.1.from_left = f32[80,128]{1,0:T(8,128)S(1)} collective-permute-done((f32[80,128]{1,0:T(8,128)S(1)}, f32[80,128]{1,0:T(8,128)S(1)}, u32[]{:S(2)}, u32[]{:S(2)}) %collective-permute-start.1) | collective-permute-done | bytes 40992 | tf_op jit(solution)/shard_map/ppermute | solution.py:581
  15.3 0.5 wide_edges.1
  15.8 7.9 %collective-permute-start.2 = (f32[2,40,768]{2,1,0:T(8,128)S(1)}, f32[2,40,768]{2,1,0:T(8,128)S(1)}, u32[]{:S(2)}, u32[]{:S(2)}) collective-permute-start(f32[2,40,768]{2,1,0:T(8,128)S(1)} %wide_edges.1), channel_id=1, source_target_pairs={{0,120},{8,112},{16,104},{24,96},{32,88},{40,80},{48,72},{56,64},{... | collective-permute-start | bytes 737288 | tf_op jit(solution)/shard_map/ppermute | solution.py:587
  23.7 0.9 %pieces.1 = (f32[96,512]{1,0:T(8,128)S(1)}, f32[96,512]{1,0:T(8,128)S(1)}, f32[2,40,768]{2,1,0:T(8,128)S(1)}, f32[96,512]{1,0:T(8,128)S(1)}, f32[96,512]{1,0:T(8,128)S(1)}) custom-call(f32[3,128,256]{2,1,0:T(8,128)S(1)} %get-tuple-element.22.outer.outer_far, f32[3,128,256]{2,1,0:T(8,128)S(1)} %get-tuple-element.23.inner.inner_far, ...), custom_call_target="tpu_custom_call" | custom-call | tf_op jit(solution)/shard_map/pieces/pallas_call | solution.py:312
  24.6 0.0 collective-permute-start.5
  24.7 5.3 %collective-permute-start.6 = (f32[96,512]{1,0:T(8,128)S(1)}, f32[96,512]{1,0:T(8,128)S(1)}, u32[]{:S(2)}, u32[]{:S(2)}) collective-permute-start(f32[96,512]{1,0:T(8,128)S(1)} %get-tuple-element.37), channel_id=1, source_target_pairs={{0,120},{8,112},{16,104},{24,96},{32,88},{40,80},{48,72},{56,64},{... | collective-permute-start | bytes 589832 | tf_op jit(solution)/shard_map/ppermute | solution.py:595
  30.0 0.0 collective-permute-done.2.far.far_edges
  30.1 0.1 collective-permute-start.3
  30.2 2.3 %collective-permute-start.4 = (f32[40,640]{1,0:T(8,128)S(1)}, f32[40,640]{1,0:T(8,128)S(1)}, u32[]{:S(2)}, u32[]{:S(2)}) collective-permute-start(f32[40,640]{1,0:T(8,128)S(1)} %get-tuple-element.33), channel_id=1, source_target_pairs={{8,16},{16,8},{24,32},{32,24},{40,48},{48,40},{56,64},{64,56},{72,... | collective-permute-start | bytes 307208 | tf_op jit(solution)/shard_map/ppermute | solution.py:598
  32.5 3.1 %collective-permute-done.5.far_sigma = f32[96,512]{1,0:T(8,128)S(1)} collective-permute-done((f32[96,512]{1,0:T(8,128)S(1)}, f32[96,512]{1,0:T(8,128)S(1)}, u32[]{:S(2)}, u32[]{:S(2)}) %collective-permute-start.5) | collective-permute-done | bytes 196640 | tf_op jit(solution)/shard_map/ppermute | solution.py:595
  35.6 1.9 %collective-permute-done.6.far_source = f32[96,512]{1,0:T(8,128)S(1)} collective-permute-done((f32[96,512]{1,0:T(8,128)S(1)}, f32[96,512]{1,0:T(8,128)S(1)}, u32[]{:S(2)}, u32[]{:S(2)}) %collective-permute-start.6) | collective-permute-done | bytes 196640 | tf_op jit(solution)/shard_map/ppermute | solution.py:595
  37.5 0.0 collective-permute-done.3.from_chip
  37.5 0.0 collective-permute-done.4.from_next
  37.5 0.0 copy-done.1
  37.5 0.1 broadcast_in_dim.2.factors
  37.6 6.8 %potential_solve.1 = (f32[128,512]{1,0:T(8,128)}, f32[128,512]{1,0:T(8,128)S(1)}, f32[128,512]{1,0:T(8,128)S(1)}, f32[128,1,128]{2,1,0:T(1,128)S(1)}) custom-call(f32[32,8,128]{2,1,0:T(8,128)S(1)} %broadcast_in_dim.2.factors, f32[2,40,768]{2,1,0:T(8,128)S(1)} %get-tuple-element.31.own.own_edges, f32[2,40,768]{2,1,0:T(8,128)S(1)} %collective-permute-done.2.far.far_edges, ...), custom_call_target="tpu_custom_call" | custom-call | tf_op jit(solution)/shard_map/potential_solve/pallas_call | solution.py:495
  44.4 17.5 %all_to_all.5.fastest = f32[128,1,128]{2,1,0:T(1,128)S(1)} all-to-all(f32[128,1,128]{2,1,0:T(1,128)S(1)} %get-tuple-element.39), channel_id=1, replica_groups=mesh['lat'=16,'lon'=8] {'lat','lon'}, dimensions={0} | all-to-all | bytes 131072 | tf_op jit(solution)/shard_map/all_to_all | solution.py:607
  61.9 1.5 %ion_advection.1 = f32[3,128,512]{2,1,0:T(8,128)} custom-call(f32[128,1,128]{2,1,0:T(1,128)S(1)} %all_to_all.5.fastest, f32[128,512]{1,0:T(8,128)S(1)} %get-tuple-element.40.drift_east, f32[128,512]{1,0:T(8,128)S(1)} %get-tuple-element.41.drift_north, f32[3,128,512]{2,1,0:T(8,128)S(1)} %copy-done, f32[40,640]{1,0:T(8,128)S(1)} %collective-permute-done.3.from_chip, ...), custom_call_target="tpu_custom_call" | custom-call | tf_op jit(solution)/shard_map/ion_advection/pallas_call | solution.py:554
  (1 shorter events, 0.0 us)
Async XLA Ops:
  0.6 5.0 %copy-start = (f32[3,128,512]{2,1,0:T(8,128)S(1)}, f32[3,128,512]{2,1,0:T(8,128)}, u32[]{:S(2)}) copy-start(f32[3,128,512]{2,1,0:T(8,128)} %ions.5) | copy-start | bytes 2359300
  5.8 8.5 %collective-permute-start = (f32[80,128]{1,0:T(8,128)S(1)}, f32[80,128]{1,0:T(8,128)S(1)}, u32[]{:S(2)}, u32[]{:S(2)}) collective-permute-start(f32[80,128]{1,0:T(8,128)S(1)} %get-tuple-element.28), channel_id=1, source_target_pairs={{1,0},{2,1},{3,2},{4,3},{5,4},{6,5},{7,6},{0,7},{9,8},{10,9},{11,1... | collective-permute-start | bytes 122888 | tf_op jit(solution)/shard_map/ppermute | solution.py:580
  10.3 27.2 %copy-start.1 = (f32[32]{0:T(128)S(1)}, f32[32]{0:T(128)}, u32[]{:S(2)}) copy-start(f32[32]{0:T(128)} %constant.2.clone) | copy-start | bytes 388
  10.3 5.0 %collective-permute-start.1 = (f32[80,128]{1,0:T(8,128)S(1)}, f32[80,128]{1,0:T(8,128)S(1)}, u32[]{:S(2)}, u32[]{:S(2)}) collective-permute-start(f32[80,128]{1,0:T(8,128)S(1)} %get-tuple-element.29), channel_id=1, source_target_pairs={{0,1},{1,2},{2,3},{3,4},{4,5},{5,6},{6,7},{7,0},{8,9},{9,10},{10,1... | collective-permute-start | bytes 122888 | tf_op jit(solution)/shard_map/ppermute | solution.py:581
  15.8 14.2 %collective-permute-start.2 = (f32[2,40,768]{2,1,0:T(8,128)S(1)}, f32[2,40,768]{2,1,0:T(8,128)S(1)}, u32[]{:S(2)}, u32[]{:S(2)}) collective-permute-start(f32[2,40,768]{2,1,0:T(8,128)S(1)} %wide_edges.1), channel_id=1, source_target_pairs={{0,120},{8,112},{16,104},{24,96},{32,88},{40,80},{48,72},{56,64},{... | collective-permute-start | bytes 737288 | tf_op jit(solution)/shard_map/ppermute | solution.py:587
  24.6 10.9 %collective-permute-start.5 = (f32[96,512]{1,0:T(8,128)S(1)}, f32[96,512]{1,0:T(8,128)S(1)}, u32[]{:S(2)}, u32[]{:S(2)}) collective-permute-start(f32[96,512]{1,0:T(8,128)S(1)} %get-tuple-element.36), channel_id=1, source_target_pairs={{0,120},{8,112},{16,104},{24,96},{32,88},{40,80},{48,72},{56,64},{... | collective-permute-start | bytes 589832 | tf_op jit(solution)/shard_map/ppermute | solution.py:595
  24.7 12.8 %collective-permute-start.6 = (f32[96,512]{1,0:T(8,128)S(1)}, f32[96,512]{1,0:T(8,128)S(1)}, u32[]{:S(2)}, u32[]{:S(2)}) collective-permute-start(f32[96,512]{1,0:T(8,128)S(1)} %get-tuple-element.37), channel_id=1, source_target_pairs={{0,120},{8,112},{16,104},{24,96},{32,88},{40,80},{48,72},{56,64},{... | collective-permute-start | bytes 589832 | tf_op jit(solution)/shard_map/ppermute | solution.py:595
  30.1 7.5 %collective-permute-start.3 = (f32[40,640]{1,0:T(8,128)S(1)}, f32[40,640]{1,0:T(8,128)S(1)}, u32[]{:S(2)}, u32[]{:S(2)}) collective-permute-start(f32[40,640]{1,0:T(8,128)S(1)} %get-tuple-element.32), channel_id=1, source_target_pairs={{0,8},{8,0},{16,24},{24,16},{32,40},{40,32},{48,56},{56,48},{64,72... | collective-permute-start | bytes 307208 | tf_op jit(solution)/shard_map/ppermute | solution.py:597
  30.2 7.4 %collective-permute-start.4 = (f32[40,640]{1,0:T(8,128)S(1)}, f32[40,640]{1,0:T(8,128)S(1)}, u32[]{:S(2)}, u32[]{:S(2)}) collective-permute-start(f32[40,640]{1,0:T(8,128)S(1)} %get-tuple-element.33), channel_id=1, source_target_pairs={{8,16},{16,8},{24,32},{32,24},{40,48},{48,40},{56,64},{64,56},{72,... | collective-permute-start | bytes 307208 | tf_op jit(solution)/shard_map/ppermute | solution.py:598
